TPU v7x, 32 devices: a whole 2x2x4 slice. The times are simulated.
32 devices in a mesh: seq: 2 (over y), fsdp: 16 (over z, x, core).
Axes of the slice: x: 2, y: 2, z: 4, core: 2. Of those that a mesh axis runs over, the one named last changes fastest.
Arguments:
- latents: bfloat16 [32, 512, 1024], P('fsdp', 'seq'), may hold values from -6 to 6
- timesteps: int32 [32], replicated, may hold values from 0 to 999
- class_ids: int32 [32], replicated, may hold values from 0 to 1000
- class_table: bfloat16 [1001, 1024], P(None, 'fsdp'), may hold values from -6 to 6
- w_mod: bfloat16 [1024, 6144], P('fsdp'), may hold values from -0.1875 to 0.1875
- b_mod: bfloat16 [6144], P('fsdp'), may hold values from -3 to 3
- w_qkv: bfloat16 [1024, 3072], P('fsdp'), may hold values from -0.1875 to 0.1875
- b_q: bfloat16 [1024], P('fsdp'), may hold values from -3 to 3
- b_v: bfloat16 [1024], P('fsdp'), may hold values from -0.29882812 to 0.29882812
- w_out: bfloat16 [1024, 1024], P('fsdp'), may hold values from -1.5 to 1.5
- b_out: bfloat16 [1024], P('fsdp'), may hold values from -2 to 2
- w_fc1: bfloat16 [1024, 4096], P('fsdp'), may hold values from -0.1875 to 0.1875
- b_fc1: bfloat16 [4096], P('fsdp'), may hold values from -3 to 3
- w_fc2: bfloat16 [4096, 1024], P('fsdp'), may hold values from -0.09375 to 0.09375
- b_fc2: bfloat16 [1024], P('fsdp'), may hold values from -2 to 2
- out_cotangent: bfloat16 [32, 512, 1024], P('fsdp', 'seq'), may hold values from -6 to 6
Outputs:
- result: bfloat16 [32, 512, 1024], P('fsdp', 'seq')
- grad_latents: float32 [32, 512, 1024], P('fsdp', 'seq')
- grad_table: float32 [1001, 1024], P(None, 'fsdp')
- grad_w_mod: float32 [1024, 6144], P('fsdp')
- grad_b_mod: float32 [6144], P('fsdp')
- grad_w_qkv: float32 [1024, 3072], P('fsdp')
- grad_b_q: float32 [1024], P('fsdp')
- grad_b_v: float32 [1024], P('fsdp')
- grad_w_out: float32 [1024, 1024], P('fsdp')
- grad_b_out: float32 [1024], P('fsdp')
- grad_w_fc1: float32 [1024, 4096], P('fsdp')
- grad_b_fc1: float32 [4096], P('fsdp')
- grad_w_fc2: float32 [4096, 1024], P('fsdp')
- grad_b_fc2: float32 [1024], P('fsdp')
All inputs are finite; a program needn't handle non-finite values.
Results may differ from a plain program's by a relative error of at most 0.014.
The roundings to bfloat16 on the way count: a program that leaves them out, or rounds other values in their place, can miss the bound.
Values may be sent and summed in bfloat16 or wider, within the bound.
No kernel may reach another device: no remote copies, remote signals or barrier semaphores. Data moves between devices by JAX's collectives and lax.ppermute only.
A program may use at most 256 MiB of HBM per device.

v0:
```python
import math

import jax
import jax.numpy as jnp
from jax import lax
from jax.sharding import PartitionSpec as P

HEAD_DIM = 64


def time_features(step_ids, columns):
    half_width = columns // 2
    freqs = jnp.exp(-math.log(10000.0) * jnp.arange(half_width, dtype=jnp.float32) / half_width)
    angles = step_ids.astype(jnp.float32)[:, None] * freqs[None, :]
    return jnp.concatenate([jnp.cos(angles), jnp.sin(angles)], axis=1)


def normalize_keep(tensor):
    centered = tensor - jnp.mean(tensor, axis=-1, keepdims=True)
    variance = jnp.mean(centered * centered, axis=-1, keepdims=True)
    inverse = lax.rsqrt(variance + 1e-06)
    return (centered * inverse, inverse)


def normalize_back(grad_hat, normed, inverse):
    mean_grad = jnp.mean(grad_hat, axis=-1, keepdims=True)
    mean_cross = jnp.mean(grad_hat * normed, axis=-1, keepdims=True)
    return inverse * (grad_hat - mean_grad - normed * mean_cross)


def gelu_tanh(tensor):
    return (
        0.5
        * tensor
        * (1.0 + jnp.tanh(0.7978845608028654 * (tensor + 0.044715 * tensor * tensor * tensor)))
    )


def lift_silu(tensor):
    return tensor * jax.nn.sigmoid(tensor)


def outer_sum(earlier_value, latter):
    return lax.dot_general(
        earlier_value, latter, (((0,), (0,)), ((), ())), preferred_element_type=jnp.float32
    )


def compared_with(earlier_value, latter):
    return lax.dot_general(
        earlier_value, latter, (((1,), (1,)), ((), ())), preferred_element_type=jnp.float32
    )


def regroup(tensor, axis_pos, outer_count, inner_count):
    extents = tensor.shape
    splitted = (
        extents[:axis_pos]
        + (outer_count, inner_count, extents[axis_pos] // (outer_count * inner_count))
        + extents[axis_pos + 1 :]
    )
    swapped = jnp.swapaxes(tensor.reshape(splitted), axis_pos, axis_pos + 1)
    return swapped.reshape(extents)


def make_term(lefts, rights, ratio):
    first_left, second_left, third_left, fourth_left = lefts
    first_right, second_right, third_right, fourth_right = rights

    def term(start, count):
        qkv_part = outer_sum(first_left, first_right)
        out_part = outer_sum(second_left, second_right)
        fc1_part = outer_sum(third_left, third_right)
        fc2_part = outer_sum(fourth_left, fourth_right).reshape(
            count, ratio * fourth_right.shape[1]
        )
        return jnp.concatenate([qkv_part, out_part, fc1_part, fc2_part], axis=1)

    return term


def attend_heads(queries, keys_all, values_all, block_rows):
    length_all = queries.shape[0]
    head_count = queries.shape[1] // HEAD_DIM
    scaling = HEAD_DIM ** (-0.5)
    query_blocks = queries.reshape(length_all // block_rows, block_rows, head_count, HEAD_DIM)
    key_heads = keys_all.reshape(length_all, head_count, HEAD_DIM)
    value_heads = values_all.reshape(length_all, head_count, HEAD_DIM)

    def one_block(query_block):
        scores = (
            jnp.einsum("qhd,khd->hqk", query_block, key_heads, preferred_element_type=jnp.float32)
            * scaling
        )
        highest = jnp.max(scores, axis=-1, keepdims=True)
        powers = jnp.exp(scores - highest)
        totals = jnp.sum(powers, axis=-1, keepdims=True)
        weight_tensors = (powers / totals).astype(jnp.bfloat16)
        mixed = jnp.einsum(
            "hqk,khd->qhd", weight_tensors, value_heads, preferred_element_type=jnp.float32
        )
        return (mixed.astype(jnp.bfloat16), (highest + jnp.log(totals))[:, :, 0])

    mixed, log_totals = lax.map(one_block, query_blocks)
    return (mixed.reshape(length_all, head_count * HEAD_DIM), log_totals)


def attend_back(queries, keys_all, values_all, grad_mixed, log_totals, block_rows):
    length_all = queries.shape[0]
    head_count = queries.shape[1] // HEAD_DIM
    scaling = HEAD_DIM ** (-0.5)
    block_count = length_all // block_rows
    query_blocks = queries.reshape(block_count, block_rows, head_count, HEAD_DIM)
    grad_blocks = grad_mixed.reshape(block_count, block_rows, head_count, HEAD_DIM)
    key_heads = keys_all.reshape(length_all, head_count, HEAD_DIM)
    value_heads = values_all.reshape(length_all, head_count, HEAD_DIM)

    def one_block(carried, blocked):
        grad_keys, grad_values = carried
        query_block, grad_block, log_block = blocked
        scores = (
            jnp.einsum("qhd,khd->hqk", query_block, key_heads, preferred_element_type=jnp.float32)
            * scaling
        )
        probs = jnp.exp(scores - log_block[:, :, None])
        grad_values = grad_values + jnp.einsum(
            "hqk,qhd->khd",
            probs.astype(jnp.bfloat16),
            grad_block,
            preferred_element_type=jnp.float32,
        )
        grad_probs = jnp.einsum(
            "qhd,khd->hqk", grad_block, value_heads, preferred_element_type=jnp.float32
        )
        grad_scores = (
            probs * (grad_probs - jnp.sum(grad_probs * probs, axis=-1, keepdims=True))
        ).astype(jnp.bfloat16)
        grad_query = (
            jnp.einsum("hqk,khd->qhd", grad_scores, key_heads, preferred_element_type=jnp.float32)
            * scaling
        )
        grad_keys = (
            grad_keys
            + jnp.einsum(
                "hqk,qhd->khd", grad_scores, query_block, preferred_element_type=jnp.float32
            )
            * scaling
        )
        return ((grad_keys, grad_values), grad_query.astype(jnp.bfloat16))

    zeroed = jnp.zeros((length_all, head_count, HEAD_DIM), jnp.float32)
    (grad_keys, grad_values), grad_queries = lax.scan(
        one_block, (zeroed, zeroed), (query_blocks, grad_blocks, log_totals)
    )
    flat_width = head_count * HEAD_DIM
    return (
        grad_queries.reshape(length_all, flat_width),
        grad_keys.reshape(length_all, flat_width).astype(jnp.bfloat16),
        grad_values.reshape(length_all, flat_width).astype(jnp.bfloat16),
    )


def local(
    latents,
    timesteps,
    class_ids,
    class_table,
    w_mod,
    b_mod,
    w_qkv,
    b_q,
    b_v,
    w_out,
    b_out,
    w_fc1,
    b_fc1,
    w_fc2,
    b_fc2,
    out_cotangent,
):
    micro_count, row_count, width_all = latents.shape
    tokens_here = micro_count * row_count
    columns = class_table.shape[1]
    owner = lax.axis_index("fsdp")
    seq_count = lax.axis_size("seq")
    fsdp_count = lax.axis_size("fsdp")
    class_range = jnp.arange(class_table.shape[0], dtype=jnp.int32)
    one_hot = (class_ids[:, None] == class_range[None, :]).astype(jnp.bfloat16)
    looked_up = jnp.dot(one_hot, class_table, preferred_element_type=jnp.float32)
    timing = lax.dynamic_slice_in_dim(
        time_features(timesteps, width_all), owner * columns, columns, 1
    )
    condition = looked_up + timing
    lifted_full, lift_pull = jax.vjp(lift_silu, condition)
    lifted = lifted_full.astype(jnp.bfloat16)
    mod_width = w_mod.shape[1]
    mod_cols = b_mod.shape[0]
    bias_line = lax.dynamic_update_slice_in_dim(
        jnp.zeros((mod_width,), jnp.float32), b_mod.astype(jnp.float32), owner * mod_cols, 0
    )
    modulation = lax.psum_scatter(
        jnp.dot(lifted, w_mod, preferred_element_type=jnp.float32) + bias_line[None, :],
        "fsdp",
        scatter_dimension=0,
        tiled=True,
    )
    mod_parts = [
        modulation[:, None, position * width_all : (position + 1) * width_all]
        for position in range(6)
    ]
    shift_one, scale_one, gate_one, shift_two, scale_two, gate_two = mod_parts
    gathered = (
        lax.all_gather(w_qkv, "fsdp", axis=0, tiled=True),
        lax.all_gather(b_q, "fsdp", axis=0, tiled=True),
        lax.all_gather(b_v, "fsdp", axis=0, tiled=True),
        lax.all_gather(w_out, "fsdp", axis=0, tiled=True),
        lax.all_gather(b_out, "fsdp", axis=0, tiled=True),
        lax.all_gather(w_fc1, "fsdp", axis=0, tiled=True),
        lax.all_gather(b_fc1, "fsdp", axis=0, tiled=True),
        lax.all_gather(w_fc2, "fsdp", axis=0, tiled=True),
        lax.all_gather(b_fc2, "fsdp", axis=0, tiled=True),
    )
    (
        full_qkv,
        query_bias,
        value_bias,
        full_out,
        out_bias,
        full_fc1,
        up_bias,
        gathered_down_weight,
        down_bias,
    ) = gathered
    ratio = gathered_down_weight.shape[0] // width_all
    inputs_full = latents.astype(jnp.float32)
    normed_one, inverse_one = normalize_keep(inputs_full)
    entry_one = (
        (normed_one * (1.0 + scale_one) + shift_one)
        .astype(jnp.bfloat16)
        .reshape(tokens_here, width_all)
    )
    projected = jnp.dot(entry_one, full_qkv, preferred_element_type=jnp.float32)
    token_shape = (micro_count, row_count, width_all)
    queries = (
        (projected[:, :width_all] + query_bias.astype(jnp.float32))
        .astype(jnp.bfloat16)
        .reshape(token_shape)
    )
    keys_here = projected[:, width_all : 2 * width_all].astype(jnp.bfloat16).reshape(token_shape)
    values_here = (
        (projected[:, 2 * width_all :] + value_bias.astype(jnp.float32))
        .astype(jnp.bfloat16)
        .reshape(token_shape)
    )
    head_queries, head_keys, head_values = (
        lax.all_to_all(queries, "seq", split_axis=2, concat_axis=1, tiled=True),
        lax.all_to_all(keys_here, "seq", split_axis=2, concat_axis=1, tiled=True),
        lax.all_to_all(values_here, "seq", split_axis=2, concat_axis=1, tiled=True),
    )
    block_rows = min(1024, head_queries.shape[1])

    def attend_one(trio):
        return attend_heads(trio[0], trio[1], trio[2], block_rows)

    head_mixed, log_totals = lax.map(attend_one, (head_queries, head_keys, head_values))
    token_mixed = lax.all_to_all(
        head_mixed, "seq", split_axis=1, concat_axis=2, tiled=True
    ).reshape(tokens_here, width_all)
    branch_one = (
        jnp.dot(token_mixed, full_out, preferred_element_type=jnp.float32)
        + out_bias.astype(jnp.float32)
    ).reshape(token_shape)
    middle = inputs_full + gate_one * branch_one
    normed_two, inverse_two = normalize_keep(middle)
    entry_two = (
        (normed_two * (1.0 + scale_two) + shift_two)
        .astype(jnp.bfloat16)
        .reshape(tokens_here, width_all)
    )
    hidden = jnp.dot(entry_two, full_fc1, preferred_element_type=jnp.float32) + up_bias.astype(
        jnp.float32
    )
    active_full, gelu_pull = jax.vjp(gelu_tanh, hidden)
    active = active_full.astype(jnp.bfloat16)
    branch_two = (
        jnp.dot(active, gathered_down_weight, preferred_element_type=jnp.float32)
        + down_bias.astype(jnp.float32)
    ).reshape(token_shape)
    result = (middle + gate_two * branch_two).astype(jnp.bfloat16)
    grad_output = out_cotangent.astype(jnp.float32)
    grad_gate_two = jnp.sum(grad_output * branch_two, axis=1)
    grad_branch_two = (gate_two * grad_output).astype(jnp.bfloat16).reshape(tokens_here, width_all)
    grad_active = compared_with(grad_branch_two, gathered_down_weight)
    grad_hidden = gelu_pull(grad_active)[0].astype(jnp.bfloat16)
    grad_entry_two = compared_with(grad_hidden, full_fc1).reshape(token_shape)
    grad_shift_two = jnp.sum(grad_entry_two, axis=1)
    grad_scale_two = jnp.sum(grad_entry_two * normed_two, axis=1)
    grad_middle = grad_output + normalize_back(
        grad_entry_two * (1.0 + scale_two), normed_two, inverse_two
    )
    grad_gate_one = jnp.sum(grad_middle * branch_one, axis=1)
    grad_branch_one = (gate_one * grad_middle).astype(jnp.bfloat16).reshape(tokens_here, width_all)
    grad_mixed = compared_with(grad_branch_one, full_out).astype(jnp.bfloat16).reshape(token_shape)
    head_grads = lax.all_to_all(grad_mixed, "seq", split_axis=2, concat_axis=1, tiled=True)

    def back_one(grouped):
        return attend_back(grouped[0], grouped[1], grouped[2], grouped[3], grouped[4], block_rows)

    grad_heads_q, grad_heads_k, grad_heads_v = lax.map(
        back_one, (head_queries, head_keys, head_values, head_grads, log_totals)
    )
    grad_queries, grad_keys, grad_values = (
        lax.all_to_all(grad_heads_q, "seq", split_axis=1, concat_axis=2, tiled=True),
        lax.all_to_all(grad_heads_k, "seq", split_axis=1, concat_axis=2, tiled=True),
        lax.all_to_all(grad_heads_v, "seq", split_axis=1, concat_axis=2, tiled=True),
    )
    grad_project = jnp.concatenate([grad_queries, grad_keys, grad_values], axis=2).reshape(
        tokens_here, 3 * width_all
    )
    grad_entry_one = compared_with(grad_project, full_qkv).reshape(token_shape)
    grad_shift_one = jnp.sum(grad_entry_one, axis=1)
    grad_scale_one = jnp.sum(grad_entry_one * normed_one, axis=1)
    grad_latents = grad_middle + normalize_back(
        grad_entry_one * (1.0 + scale_one), normed_one, inverse_one
    )
    grad_mod_part = jnp.concatenate(
        [
            grad_shift_one,
            grad_scale_one,
            grad_gate_one,
            grad_shift_two,
            grad_scale_two,
            grad_gate_two,
        ],
        axis=1,
    )
    grad_mod_seq = lax.psum(grad_mod_part, "seq").astype(jnp.bfloat16)
    grad_mod_all = lax.all_gather(grad_mod_seq, "fsdp", axis=0, tiled=True)
    grad_w_mod = outer_sum(lifted, grad_mod_all)
    grad_b_mod = jnp.sum(
        lax.dynamic_slice_in_dim(grad_mod_all, owner * mod_cols, mod_cols, 1).astype(jnp.float32),
        axis=0,
    )
    grad_lifted = compared_with(grad_mod_all, w_mod)
    grad_condition = lift_pull(grad_lifted)[0]
    grad_table = jnp.dot(
        one_hot.astype(jnp.float32).T,
        grad_condition,
        precision=lax.Precision.HIGHEST,
        preferred_element_type=jnp.float32,
    )
    grad_q_bias = jnp.sum(grad_project[:, :width_all].astype(jnp.float32), axis=0)
    grad_v_bias = jnp.sum(grad_project[:, 2 * width_all :].astype(jnp.float32), axis=0)
    grad_out_bias = jnp.sum(grad_branch_one.astype(jnp.float32), axis=0)
    grad_up_bias = jnp.sum(grad_hidden.astype(jnp.float32), axis=0)
    grad_down_bias = jnp.sum(grad_branch_two.astype(jnp.float32), axis=0)
    rights = (grad_project, grad_branch_one, grad_hidden, grad_branch_two)
    lefts = (
        regroup(entry_one, 1, fsdp_count, seq_count),
        regroup(token_mixed, 1, fsdp_count, seq_count),
        regroup(entry_two, 1, fsdp_count, seq_count),
        regroup(active, 1, fsdp_count, seq_count),
    )
    wide_term = make_term(lefts, rights, ratio)
    wide = lax.psum_scatter(
        wide_term(
            jnp.int32(0), width_all // (fsdp_count * seq_count) * lax.axis_size(("seq", "fsdp"))
        ),
        ("seq", "fsdp"),
        scatter_dimension=0,
        tiled=True,
    )
    biases = (
        lax.psum_scatter(
            regroup(grad_q_bias, 0, fsdp_count, seq_count),
            ("seq", "fsdp"),
            scatter_dimension=0,
            tiled=True,
        ),
        lax.psum_scatter(
            regroup(grad_v_bias, 0, fsdp_count, seq_count),
            ("seq", "fsdp"),
            scatter_dimension=0,
            tiled=True,
        ),
        lax.psum_scatter(
            regroup(grad_out_bias, 0, fsdp_count, seq_count),
            ("seq", "fsdp"),
            scatter_dimension=0,
            tiled=True,
        ),
        lax.psum_scatter(
            regroup(grad_up_bias, 0, fsdp_count, seq_count),
            ("seq", "fsdp"),
            scatter_dimension=0,
            tiled=True,
        ),
        lax.psum_scatter(
            regroup(grad_down_bias, 0, fsdp_count, seq_count),
            ("seq", "fsdp"),
            scatter_dimension=0,
            tiled=True,
        ),
    )
    owned = (
        lax.all_gather(wide, "seq", axis=0, tiled=True),
        lax.all_gather(biases[0], "seq", axis=0, tiled=True),
        lax.all_gather(biases[1], "seq", axis=0, tiled=True),
        lax.all_gather(biases[2], "seq", axis=0, tiled=True),
        lax.all_gather(biases[3], "seq", axis=0, tiled=True),
        lax.all_gather(biases[4], "seq", axis=0, tiled=True),
    )
    wide_owned = owned[0]
    ff_width = full_fc1.shape[1]
    grad_w_qkv = wide_owned[:, : 3 * width_all]
    grad_w_out = wide_owned[:, 3 * width_all : 4 * width_all]
    grad_w_fc1 = wide_owned[:, 4 * width_all : 4 * width_all + ff_width]
    grad_w_fc2 = wide_owned[:, 4 * width_all + ff_width :].reshape(-1, width_all)
    return (
        result,
        grad_latents,
        grad_table,
        grad_w_mod,
        grad_b_mod,
        grad_w_qkv,
        owned[1],
        owned[2],
        grad_w_out,
        owned[3],
        grad_w_fc1,
        owned[4],
        grad_w_fc2,
        owned[5],
    )


def solution(mesh):
    placed = (
        P("fsdp", "seq", None),
        P(),
        P(),
        P(None, "fsdp"),
        P("fsdp", None),
        P("fsdp"),
        P("fsdp", None),
        P("fsdp"),
        P("fsdp"),
        P("fsdp", None),
        P("fsdp"),
        P("fsdp", None),
        P("fsdp"),
        P("fsdp", None),
        P("fsdp"),
        P("fsdp", "seq", None),
    )
    return jax.shard_map(
        local,
        mesh=mesh,
        in_specs=placed,
        out_specs=(
            P("fsdp", "seq", None),
            P("fsdp", "seq", None),
            P(None, "fsdp"),
            P("fsdp", None),
            P("fsdp"),
            P("fsdp", None),
            P("fsdp"),
            P("fsdp"),
            P("fsdp", None),
            P("fsdp"),
            P("fsdp", None),
            P("fsdp"),
            P("fsdp", None),
            P("fsdp"),
        ),
        check_vma=False,
    )
```

profile of v0, /device:TPU:0, one launch (start us, length us, event | category | flops | bytes accessed | tf_op | source)
XLA Modules:
  0.0 1115.4 jit_solution(14875869446813498801)
XLA Ops:
  16.7 90.3 %all-reduce.19.cloned.1.call-done = f32[32,6144]{1,0:T(8,128)} async-done(((f32[32,6144]{1,0:T(8,128)}), f32[32,6144]{1,0:T(8,128)}) %all-reduce.19.cloned.1.call-update) | async-done | bytes 786448
  108.5 61.9 %all-gather.9.cloned.1.call-done = bf16[1024,3072]{1,0:T(8,128)(2,1)} async-done(((bf16[64,3072]{1,0:T(8,128)(2,1)}), bf16[1024,3072]{1,0:T(8,128)(2,1)}) %all-gather.9.cloned.1.call-update) | async-done | bytes 6291472 | tf_op jit(solution)/shard_map/all_gather | solution.py:213
  170.4 5.5 fusion.78
  186.0 32.2 %all-reduce.16 = (bf16[1024]{0:T(1024)(128)(2,1)S(1)}, bf16[1024]{0:T(1024)(128)(2,1)S(1)}, bf16[1024]{0:T(1024)(128)(2,1)S(1)}, bf16[1024]{0:T(1024)(128)(2,1)S(1)}) all-reduce(bf16[1024]{0:T(1024)(128)(2,1)S(1)} %dynamic-update-slice, bf16[1024]{0:T(1024)(128)(2,1)S(1)} %dynamic-update-slice.1, ...), channel_id=1, replica_groups=mesh['seq'=2,'fsdp'=16] {'fsdp'}, use_global_device_ids=true, to_apply=%add | all-reduce | flops 4096 | bytes 16384
  231.3 8.7 all-to-all-done
  240.0 4.9 all-to-all-start.1
  262.6 13.8 %while.10 = (s32[]{:T(128)}, bf16[2,512,512]{1,2,0:T(8,128)(2,1)}, f32[2,1,8,512]{3,2,1,0:T(8,128)S(1)}, bf16[2,512,512]{1,2,0:T(8,128)(2,1)}, bf16[2,512,512]{1...) while((s32[]{:T(128)}, bf16[2,512,512]{1,2,0:T(8,128)(2,1)}, ...), condition=%wide.region_6.0_spmd, body=%wide.region_3.6_spmd.sunk | while | flops 556003328 | bytes 39977116 | solution.py:265
  280.4 4.4 all-to-all-start.3
  284.9 18.6 %all-gather = bf16[16,1,256]{2,1,0:T(2,128)(2,1)S(1)} all-gather(bf16[1,1,256]{2,1,0:T(2,128)(2,1)S(1)} %reshape.344), channel_id=1, replica_groups=mesh['seq'=2,'fsdp'=16] {'fsdp'}, dimensions={0}, use_global_device_ids=true | all-gather | bytes 8704 | tf_op jit(solution)/shard_map/all_gather | solution.py:219
  315.3 11.5 %fusion.79 = f32[512,4096]{1,0:T(8,128)} fusion(bf16[512,1024]{1,0:T(8,128)(2,1)} %bitcast.248, bf16[1024,4096]{1,0:T(8,128)(2,1)} %all-gather.13.cloned.1.call-done), kind=kOutput, calls=%fused_computation.167 | convolution fusion | flops 4294967296 | bytes 17825792 | tf_op jit(solution)/shard_map/dot_general | solution.py:280
  326.8 37.8 %all-gather.15.cloned.1.call-done = bf16[4096,1024]{1,0:T(8,128)(2,1)} async-done(((bf16[256,1024]{1,0:T(8,128)(2,1)}), bf16[4096,1024]{1,0:T(8,128)(2,1)}) %all-gather.15.cloned.1.call-update) | async-done | bytes 8388624 | tf_op jit(solution)/shard_map/all_gather | solution.py:220
  364.5 17.5 %convert_reduce_fusion = (f32[4096]{0:T(1024)}, bf16[512,4096]{1,0:T(8,128)(2,1)S(1)}, bf16[512,4096]{1,0:T(8,128)(2,1)}) fusion(f32[512,4096]{1,0:T(8,128)} %fusion.79, f32[4096]{0:T(1024)S(1)} %bitcast.279, bf16[512,1024]{1,0:T(8,128)(2,1)} %bitcast.262, bf16[4096,1024]{1,0:T(8,128)(2,1)} %all-gather.15.cloned.1.call-done), kind=kOutput, calls=%fused_computation.44 | convolution fusion | flops 4355780608 | bytes 26247168 | tf_op jit(solution)/shard_map/dot_general | solution.py:50
  382.0 5.9 fusion.52
  391.6 7.0 convolution_add_fusion.2
  404.5 16.8 %all_to_all.132 = bf16[2,256,1024]{1,0,2:T(2,128)(2,1)S(1)} all-to-all(bf16[2,256,1024]{1,0,2:T(2,128)(2,1)S(1)} %copy.100), channel_id=1, replica_groups=mesh['seq'=2,'fsdp'=16] {'seq'}, dimensions={2} | all-to-all | bytes 2097152 | tf_op jit(solution)/shard_map/all_to_all | solution.py:304
  429.0 29.5 %while.27 = (s32[]{:T(128)}, bf16[2,512,512]{1,2,0:T(8,128)(2,1)}, bf16[2,512,512]{1,2,0:T(8,128)(2,1)}, bf16[2,512,512]{1,2,0:T(8,128)(2,1)}, bf16[2,512,512]{1...) while((s32[]{:T(128)}, bf16[2,512,512]{1,2,0:T(8,128)(2,1)}, ...), condition=%wide.region_13.14_spmd, body=%wide.region_11.13_spmd.sunk | while | flops 1368649728 | bytes 100778288 | solution.py:309
  475.0 5.8 copy.98
  489.4 7.8 reshape.306
  497.2 11.2 %copy.113 = bf16[512,16,2,128]{0,3,1,2:T(8,128)(2,1)} copy(bf16[512,16,2,128]{3,2,1,0:T(2,128)(2,1)} %reshape.306) | data formatting | bytes 8388608 | tf_op jit(solution)/shard_map/reshape | solution.py:62
  514.1 12.8 %fusion.83 = f32[4096,1024]{1,0:T(8,128)} fusion(bf16[512,4096]{0,1:T(8,128)(2,1)} %bitcast.246, bf16[512,1024]{1,0:T(8,128)(2,1)} %bitcast.263), kind=kOutput, calls=%fused_computation.171 | convolution fusion | flops 4294967296 | bytes 22020096 | tf_op jit(solution)/shard_map/dot_general | solution.py:44
  530.5 4.4 all-to-all-start.6
  535.0 12.8 %fusion.82 = f32[1024,4096]{1,0:T(8,128)} fusion(bf16[512,1024]{0,1:T(8,128)(2,1)} %bitcast.266, bf16[512,4096]{1,0:T(8,128)(2,1)} %copy-done.60), kind=kOutput, calls=%fused_computation.170 | convolution fusion | flops 4294967296 | bytes 22020096 | tf_op jit(solution)/shard_map/dot_general | solution.py:44
  547.8 20.6 %reshape.308 = f32[1024,4096]{1,0:T(8,128)} reshape(f32[4096,1024]{1,0:T(8,128)} %fusion.83) | data formatting | bytes 33554432 | tf_op jit(solution)/shard_map/reshape | solution.py:74
  568.3 4.7 fusion.81
  582.6 6.6 fusion.28
  589.1 33.2 %pad_maximum_fusion = f32[1024,12288]{1,0:T(8,128)} fusion(f32[1024,4096]{1,0:T(8,128)} %reshape.308, f32[1024,4096]{1,0:T(8,128)} %fusion.82, f32[1024,1024]{1,0:T(8,128)} %fusion.81, f32[1024,3072]{1,0:T(8,128)} %fusion.28), kind=kLoop, calls=%fused_computation.33 | loop fusion | flops 37748736 | bytes 100663296 | tf_op jit(solution)/shard_map/concatenate | solution.py:77
  629.9 39.3 %all-reduce.14 = (f32[1024]{0:T(1024)S(1)}, f32[1024]{0:T(1024)S(1)}, f32[1024]{0:T(1024)S(1)}, f32[4096]{0:T(1024)S(1)}, f32[1024]{0:T(1024)S(1)}) all-reduce(f32[1024]{0:T(1024)S(1)} %reshape.310, f32[1024]{0:T(1024)S(1)} %reshape.312, f32[1024]{0:T(1024)S(1)} %reshape.314, ...), channel_id=4, replica_groups=mesh['seq'=2,'fsdp'=16] {'seq','fsdp'}, use_global_device_ids=true, to_apply=%region_26.27.clone | all-reduce | flops 8192 | bytes 65536
  669.3 4.4 all-gather.2
  679.9 373.1 %reduce-scatter.2.cloned.1.call-done = f32[32,12288]{1,0:T(8,128)} async-done(((f32[1024,12288]{1,0:T(8,128)}), f32[32,12288]{1,0:T(8,128)}) %reduce-scatter.2.cloned.1.call-update) | async-done | bytes 1572880 | tf_op jit(solution)/shard_map/reduce_scatter | solution.py:365
  1053.1 7.5 fusion.46
  1063.1 10.4 all-reduce.15
  1073.5 20.5 %all-gather.1 = bf16[16,2,6144]{2,1,0:T(2,128)(2,1)S(1)} all-gather(bf16[1,2,6144]{2,1,0:T(2,128)(2,1)S(1)} %bitcast.277), channel_id=1, replica_groups=mesh['seq'=2,'fsdp'=16] {'fsdp'}, dimensions={0}, use_global_device_ids=true | all-gather | bytes 417792 | tf_op jit(solution)/shard_map/all_gather | solution.py:338
  (331 shorter events, 199.5 us)
Async XLA Ops:
  7.2 8.8 copy-start.5
  7.2 99.8 %all-reduce.19.cloned.1.call-start = ((), (), s32[]{:S(2)}) async-start(), calls=%async_computation.15 | async-start | bytes 1572864
  12.1 158.3 %all-gather.9.cloned.1.call-start = ((), (), s32[]{:S(2)}) async-start(), calls=%async_computation.9 | async-start | bytes 6684672 | tf_op jit(solution)/shard_map/all_gather | solution.py:213
  12.9 296.3 %all-gather.11.cloned.1.call-start = ((), (), s32[]{:S(2)}) async-start(), calls=%async_computation.10 | async-start | bytes 2228224 | tf_op jit(solution)/shard_map/all_gather | solution.py:216
  13.6 301.7 %all-gather.13.cloned.1.call-start = ((), (), s32[]{:S(2)}) async-start(), calls=%async_computation.11 | async-start | bytes 8912896 | tf_op jit(solution)/shard_map/all_gather | solution.py:218
  14.2 350.3 %all-gather.15.cloned.1.call-start = ((), (), s32[]{:S(2)}) async-start(), calls=%async_computation.12 | async-start | bytes 8912896 | tf_op jit(solution)/shard_map/all_gather | solution.py:220
  16.3 159.7 %copy-start.43 = (f32[2,256]{1,0:T(2,128)}, f32[2,256]{1,0:T(2,128)S(1)}, u32[]{:S(2)}) copy-start(f32[2,256]{1,0:T(2,128)S(1)} %broadcast_multiply_fusion.5) | copy-start | bytes 6148
  16.7 159.2 %copy-start.45 = (f32[2,256]{1,0:T(2,128)}, f32[2,256]{1,0:T(2,128)S(1)}, u32[]{:S(2)}) copy-start(f32[2,256]{1,0:T(2,128)S(1)} %add_rsqrt_fusion.1) | copy-start | bytes 6148
  108.0 68.0 %copy-start.38 = (f32[2,1024]{1,0:T(2,128)}, f32[2,1024]{1,0:T(2,128)S(1)}, u32[]{:S(2)}) copy-start(f32[2,1024]{1,0:T(2,128)S(1)} %get-tuple-element.232) | copy-start | bytes 24580
  108.5 67.5 %copy-start.18 = (bf16[2,256,1024]{2,1,0:T(8,128)(2,1)}, bf16[2,256,1024]{2,1,0:T(8,128)(2,1)S(1)}, u32[]{:S(2)}) copy-start(bf16[2,256,1024]{2,1,0:T(8,128)(2,1)S(1)} %fusion.41) | copy-start | bytes 3145732
  180.8 43.3 %all-to-all-start.2 = ((bf16[2,256,1024]{1,0,2:T(2,128)(2,1)}), bf16[2,256,1024]{1,0,2:T(2,128)(2,1)S(1)}, u32[]{:S(2)}, u32[]{:S(2)}) async-start(bf16[2,256,1024]{1,0,2:T(2,128)(2,1)} %copy.95), calls=%async_computation.2 | async-start | bytes 2097152 | tf_op jit(solution)/shard_map/all_to_all | solution.py:257
  224.1 15.9 %all-to-all-start = ((bf16[2,256,1024]{1,0,2:T(2,128)(2,1)}), bf16[2,256,1024]{1,0,2:T(2,128)(2,1)S(1)}, u32[]{:S(2)}, u32[]{:S(2)}) async-start(bf16[2,256,1024]{1,0,2:T(2,128)(2,1)} %copy.91), calls=%async_computation | async-start | bytes 2097152 | tf_op jit(solution)/shard_map/all_to_all | solution.py:258
  240.0 16.6 %all-to-all-start.1 = ((bf16[2,256,1024]{1,0,2:T(2,128)(2,1)}), bf16[2,256,1024]{1,0,2:T(2,128)(2,1)}, u32[]{:S(2)}, u32[]{:S(2)}) async-start(bf16[2,256,1024]{1,0,2:T(2,128)(2,1)} %copy.93), calls=%async_computation.1 | async-start | bytes 2097152 | tf_op jit(solution)/shard_map/all_to_all | solution.py:256
  276.5 32.4 %copy-start.1 = (bf16[2,512,512]{1,2,0:T(8,128)(2,1)}, bf16[2,512,512]{1,2,0:T(8,128)(2,1)S(1)}, u32[]{:S(2)}) copy-start(bf16[2,512,512]{1,2,0:T(8,128)(2,1)S(1)} %get-tuple-element.440) | copy-start | bytes 3145732
  276.5 32.4 %copy-start.3 = (bf16[2,512,512]{1,2,0:T(8,128)(2,1)}, bf16[2,512,512]{1,2,0:T(8,128)(2,1)S(1)}, u32[]{:S(2)}) copy-start(bf16[2,512,512]{1,2,0:T(8,128)(2,1)S(1)} %get-tuple-element.441) | copy-start | bytes 3145732
  276.5 8.3 copy-start.58
  280.4 26.2 %all-to-all-start.3 = ((bf16[2,512,512]{2,0,1:T(2,128)(2,1)}), bf16[2,512,512]{2,0,1:T(2,128)(2,1)}, u32[]{:S(2)}, u32[]{:S(2)}) async-start(bf16[2,512,512]{2,0,1:T(2,128)(2,1)} %copy.97), calls=%async_computation.3 | async-start | bytes 2097152 | tf_op jit(solution)/shard_map/all_to_all | solution.py:266
  364.5 17.5 %copy-start.52 = (bf16[1024,4096]{1,0:T(8,128)(2,1)S(1)}, bf16[1024,4096]{1,0:T(8,128)(2,1)}, u32[]{:S(2)}) copy-start(bf16[1024,4096]{1,0:T(8,128)(2,1)} %all-gather.13.cloned.1.call-done) | copy-start | bytes 25165828
  462.2 48.3 %all-to-all-start.7 = ((bf16[2,512,512]{2,0,1:T(2,128)(2,1)}), bf16[2,512,512]{2,0,1:T(2,128)(2,1)S(1)}, u32[]{:S(2)}, u32[]{:S(2)}) async-start(bf16[2,512,512]{2,0,1:T(2,128)(2,1)} %copy.106), calls=%async_computation.7 | async-start | bytes 2097152 | tf_op jit(solution)/shard_map/all_to_all | solution.py:315
  475.0 10.6 copy-start.30
  497.2 11.2 %copy-start.27 = (bf16[2,512,512]{1,2,0:T(8,128)(2,1)S(1)}, bf16[2,512,512]{1,2,0:T(8,128)(2,1)}, u32[]{:S(2)}) copy-start(bf16[2,512,512]{1,2,0:T(8,128)(2,1)} %get-tuple-element.143) | copy-start | bytes 3145732
  510.5 20.0 %all-to-all-start.5 = ((bf16[2,512,512]{2,0,1:T(2,128)(2,1)}), bf16[2,512,512]{2,0,1:T(2,128)(2,1)S(1)}, u32[]{:S(2)}, u32[]{:S(2)}) async-start(bf16[2,512,512]{2,0,1:T(2,128)(2,1)} %copy.102), calls=%async_computation.5 | async-start | bytes 2097152 | tf_op jit(solution)/shard_map/all_to_all | solution.py:313
  530.5 48.3 %all-to-all-start.6 = ((bf16[2,512,512]{2,0,1:T(2,128)(2,1)}), bf16[2,512,512]{2,0,1:T(2,128)(2,1)}, u32[]{:S(2)}, u32[]{:S(2)}) async-start(bf16[2,512,512]{2,0,1:T(2,128)(2,1)} %copy.104), calls=%async_computation.6 | async-start | bytes 2097152 | tf_op jit(solution)/shard_map/all_to_all | solution.py:314
  535.0 518.1 %reduce-scatter.2.cloned.1.call-start = ((), (), s32[]{:S(2)}) async-start(), calls=%async_computation.13 | async-start | bytes 51904512 | tf_op jit(solution)/shard_map/reduce_scatter | solution.py:365
  622.4 477.4 %all-gather.17.cloned.1.call-start = ((), (), s32[]{:S(2)}) async-start(), calls=%async_computation.14 | async-start | bytes 4718592 | tf_op jit(solution)/shard_map/all_gather | solution.py:406
  625.9 427.2 %copy-start.7 = (bf16[2,256,1024]{2,1,0:T(8,128)(2,1)S(1)}, bf16[2,256,1024]{2,1,0:T(8,128)(2,1)}, u32[]{:S(2)}) copy-start(bf16[2,256,1024]{2,1,0:T(8,128)(2,1)} %param.20) | copy-start | bytes 3145732
  625.9 427.2 %copy-start.39 = (f32[2,1024]{1,0:T(2,128)S(1)}, f32[2,1024]{1,0:T(2,128)}, u32[]{:S(2)}) copy-start(f32[2,1024]{1,0:T(2,128)} %copy-done.38) | copy-start | bytes 24580
  625.9 427.2 %copy-start.44 = (f32[2,256]{1,0:T(2,128)S(1)}, f32[2,256]{1,0:T(2,128)}, u32[]{:S(2)}) copy-start(f32[2,256]{1,0:T(2,128)} %copy-done.43) | copy-start | bytes 6148
  625.9 427.2 %copy-start.46 = (f32[2,256]{1,0:T(2,128)S(1)}, f32[2,256]{1,0:T(2,128)}, u32[]{:S(2)}) copy-start(f32[2,256]{1,0:T(2,128)} %copy-done.45) | copy-start | bytes 6148
  629.8 423.3 %copy-start.33 = (bf16[2,256,1024]{2,1,0:T(8,128)(2,1)S(1)}, bf16[2,256,1024]{2,1,0:T(8,128)(2,1)}, u32[]{:S(2)}) copy-start(bf16[2,256,1024]{2,1,0:T(8,128)(2,1)} %concatenate.31) | copy-start | bytes 3145732
  1060.7 34.3 %copy-start.37 = (f32[32,64]{1,0:T(8,128)S(1)}, f32[32,64]{1,0:T(8,128)}, u32[]{:S(2)}) copy-start(f32[32,64]{1,0:T(8,128)} %copy-done.36) | copy-start | bytes 24580
  1060.8 34.3 %copy-start.50 = (s32[32]{0:T(128)S(1)}, s32[32]{0:T(128)}, u32[]{:S(2)}) copy-start(s32[32]{0:T(128)} %param.22) | copy-start | bytes 388
  (51 other events, 169.4 us)
Sparse Core Ops, SparseCore 0:
  12.2 94.7 all-reduce.18
  109.5 60.8 all-gather.8
  172.8 40.1 all-gather.10
  215.2 73.8 all-gather.12
  291.4 73.0 all-gather.14
  622.5 430.4 reduce-scatter.1
  1054.6 45.1 all-gather.16
where the time goes:
time: 1120 us
  waiting for transfers between devices  580 us (52%)
  local copies, waits for them, and re-layouts  158 us (14%)
  blocking collectives  142 us (13%)
  matrix products  123 us (11%)
  other arithmetic  66.5 us (6%)
  starting transfers between devices  28.4 us (3%)
  between operations  17.4 us (2%)
    reduce_scatter x1, waiting for transfers between devices, local(): lax.psum_scatter(wide_term(jnp.int32(0), width_all // (fsdp_count * seq_c...  373 us
    unnamed x8, waiting for transfers between devices  92.8 us
    unnamed x2, blocking collectives  71.6 us
    all_gather x1, waiting for transfers between devices, local(): lax.all_gather(w_qkv, 'fsdp', axis=0, tiled=True)  61.9 us
    dot_general x5, matrix products, outer_sum(): lax.dot_general(earlier_value, latter, (((0,), (0,)), ((), ())), preferre...  38.4 us
    all_gather x1, waiting for transfers between devices, local(): lax.all_gather(w_fc2, 'fsdp', axis=0, tiled=True)  37.8 us
    concatenate x1, other arithmetic, term(): return jnp.concatenate([qkv_part, out_part, fc1_part, fc2_part], axis=1)  33.2 us
    dot_general x5, matrix products, compared_with(): lax.dot_general(earlier_value, latter, (((1,), (1,)), ((), ())), preferre...  32.5 us
  transfers between devices with their start and end apart: 14, of which 7 were waited for; matrix products, arithmetic and copies ran while one was open for 18% of the time, Pallas kernels for 0%

commit v1 on v0

--- a/solution.py
+++ b/solution.py
@@ -3,6 +3,8 @@
 import jax
 import jax.numpy as jnp
 from jax import lax
+from jax.experimental import pallas as pl
+from jax.experimental.pallas import tpu as pltpu
 from jax.sharding import PartitionSpec as P
 
 HEAD_DIM = 64
@@ -434,6 +436,371 @@
     )
 
 
+def attend_kernel(q_ref, k_ref, v_ref, o_ref, lse_ref):
+    for head in range(2):
+        at = slice(head * HEAD_DIM, (head + 1) * HEAD_DIM)
+        queries = q_ref[:, at] * jnp.bfloat16(HEAD_DIM ** (-0.5))
+        scores = compared_with(k_ref[:, at], queries)
+        highest = jnp.max(scores, axis=0, keepdims=True)
+        powers = jnp.exp(scores - highest)
+        totals = jnp.sum(powers, axis=0, keepdims=True)
+        probs = (powers * (1.0 / totals)).astype(jnp.bfloat16)
+        mixed = jnp.dot(v_ref[:, at].T, probs, preferred_element_type=jnp.float32)
+        o_ref[:, at] = mixed.T.astype(jnp.bfloat16)
+        lse_ref[0, head : head + 1, :] = highest + jnp.log(totals)
+
+
+def attend_back_kernel(q_ref, k_ref, v_ref, do_ref, lse_ref, dq_ref, dk_ref, dv_ref):
+    for head in range(2):
+        at = slice(head * HEAD_DIM, (head + 1) * HEAD_DIM)
+        queries = q_ref[:, at] * jnp.bfloat16(HEAD_DIM ** (-0.5))
+        keys = k_ref[:, at]
+        grad_mixed = do_ref[:, at]
+        probs = jnp.exp(compared_with(keys, queries) - lse_ref[0, head : head + 1, :])
+        dv_ref[:, at] = jnp.dot(
+            probs.astype(jnp.bfloat16), grad_mixed, preferred_element_type=jnp.float32
+        ).astype(jnp.bfloat16)
+        grad_probs = compared_with(v_ref[:, at], grad_mixed)
+        inner = jnp.sum(grad_probs * probs, axis=0, keepdims=True)
+        grad_scores = (probs * (grad_probs - inner)).astype(jnp.bfloat16)
+        dk_ref[:, at] = jnp.dot(
+            grad_scores, queries, preferred_element_type=jnp.float32
+        ).astype(jnp.bfloat16)
+        scaled_keys = keys * jnp.bfloat16(HEAD_DIM ** (-0.5))
+        grad_queries = jnp.dot(scaled_keys.T, grad_scores, preferred_element_type=jnp.float32)
+        dq_ref[:, at] = grad_queries.T.astype(jnp.bfloat16)
+
+
+VMEM_LIMIT = 48 * 1024 * 1024
+
+
+def attend_local(projected):
+    length, wide = projected.shape
+    pairs = wide // 3 // 128
+
+    def part(which):
+        return pl.BlockSpec((length, 128), lambda i: (0, which * pairs + i))
+
+    cost = pl.CostEstimate(
+        flops=16 * pairs * length * length * 128,
+        bytes_accessed=length * wide * 3,
+        transcendentals=2 * pairs * length * length,
+    )
+    return pl.pallas_call(
+        attend_kernel,
+        grid=(pairs,),
+        in_specs=[part(0), part(1), part(2)],
+        out_specs=[part(0), pl.BlockSpec((1, 2, length), lambda i: (i, 0, 0))],
+        out_shape=[
+            jax.ShapeDtypeStruct((length, wide // 3), jnp.bfloat16),
+            jax.ShapeDtypeStruct((pairs, 2, length), jnp.float32),
+        ],
+        compiler_params=pltpu.CompilerParams(vmem_limit_bytes=VMEM_LIMIT),
+        cost_estimate=cost,
+        name="attend",
+    )(projected, projected, projected)
+
+
+def attend_local_back(projected, grad_mixed, log_totals):
+    length, wide = projected.shape
+    pairs = wide // 3 // 128
+
+    def part(which):
+        return pl.BlockSpec((length, 128), lambda i: (0, which * pairs + i))
+
+    cost = pl.CostEstimate(
+        flops=40 * pairs * length * length * 128,
+        bytes_accessed=length * wide * 6,
+        transcendentals=2 * pairs * length * length,
+    )
+    grads = jax.ShapeDtypeStruct((length, wide // 3), jnp.bfloat16)
+    return pl.pallas_call(
+        attend_back_kernel,
+        grid=(pairs,),
+        in_specs=[
+            part(0),
+            part(1),
+            part(2),
+            part(0),
+            pl.BlockSpec((1, 2, length), lambda i: (i, 0, 0)),
+        ],
+        out_specs=[part(0), part(0), part(0)],
+        out_shape=[grads, grads, grads],
+        compiler_params=pltpu.CompilerParams(vmem_limit_bytes=VMEM_LIMIT),
+        cost_estimate=cost,
+        name="attend_back",
+    )(projected, projected, projected, grad_mixed, log_totals)
+
+
+def swapped_pairs(count, bit):
+    return [(place, place ^ bit) for place in range(count)]
+
+
+def assemble_kernel(p00, p01, p10, p11, out_ref, sems):
+    owner = lax.axis_index("fsdp")
+    core_at = lax.rem(owner, 2)
+    x_at = lax.rem(lax.div(owner, 2), 2)
+    copies = []
+    for place, (piece, flip_x, flip_core) in enumerate(
+        ((p00, 0, 0), (p01, 0, 1), (p10, 1, 0), (p11, 1, 1))
+    ):
+        to_x = 1 - x_at if flip_x else x_at
+        to_core = 1 - core_at if flip_core else core_at
+        copies.append(
+            pltpu.make_async_copy(piece, out_ref.at[:, to_x * 2 + to_core], sems.at[place])
+        )
+    for copy in copies:
+        copy.start()
+    for copy in copies:
+        copy.wait()
+
+
+def gather_rows(weight):
+    rows, columns = weight.shape
+    count = lax.axis_size("fsdp")
+    depth = count // 4
+    z_groups = [[base + 4 * step for step in range(depth)] for base in range(4)]
+    own = lax.all_gather(weight, "fsdp", axis=0, tiled=False, axis_index_groups=z_groups)
+    across = lax.ppermute(own, "fsdp", swapped_pairs(count, 2))
+    own_core = lax.ppermute(own, "fsdp", swapped_pairs(count, 1))
+    across_core = lax.ppermute(across, "fsdp", swapped_pairs(count, 1))
+    anywhere = pl.BlockSpec(memory_space=pl.ANY)
+    whole = pl.pallas_call(
+        assemble_kernel,
+        in_specs=[anywhere] * 4,
+        out_specs=anywhere,
+        out_shape=jax.ShapeDtypeStruct((depth, 4, rows, columns), weight.dtype),
+        scratch_shapes=[pltpu.SemaphoreType.DMA((4,))],
+        cost_estimate=pl.CostEstimate(
+            flops=0, bytes_accessed=16 * depth * rows * columns, transcendentals=0
+        ),
+        name="assemble",
+    )(own, own_core, across, across_core)
+    return whole.reshape(count * rows, columns)
+
+
+def low(tensor):
+    return tensor.astype(jnp.bfloat16)
+
+
+def wide(tensor):
+    return tensor.astype(jnp.float32)
+
+
+def reduce_rows(partial):
+    count = lax.axis_size("fsdp")
+    depth = count // 4
+    owner = lax.axis_index("fsdp")
+    core_at = lax.rem(owner, 2)
+    x_at = lax.rem(lax.div(owner, 2), 2)
+    z_at = lax.div(owner, 4)
+    columns = partial.shape[1]
+    blocks = low(partial).reshape(depth, 2, 2, partial.shape[0] // count, columns)
+
+    def pick(tensor, axis, place):
+        return lax.dynamic_index_in_dim(tensor, place, axis, keepdims=False)
+
+    arrived = lax.ppermute(pick(blocks, 2, 1 - core_at), "fsdp", swapped_pairs(count, 1))
+    kept = pick(blocks, 2, core_at)
+    away = low(wide(pick(kept, 1, 1 - x_at)) + wide(pick(arrived, 1, 1 - x_at)))
+    crossed = lax.ppermute(away, "fsdp", swapped_pairs(count, 2))
+    here = wide(pick(kept, 1, x_at)) + wide(pick(arrived, 1, x_at))
+    total = pick(here, 0, z_at) + wide(pick(crossed, 0, z_at))
+    for shift in range(1, depth):
+        target = lax.rem(z_at + shift, depth)
+        leaving = low(pick(here, 0, target) + wide(pick(crossed, 0, target)))
+        pairs = [(place, (place + 4 * shift) % count) for place in range(count)]
+        total = total + wide(lax.ppermute(leaving, "fsdp", pairs))
+    mine = low(total)
+    return wide(mine) + wide(lax.ppermute(mine, "seq", swapped_pairs(2, 1)))
+
+
+def local_whole_latent(
+    latents,
+    timesteps,
+    class_ids,
+    class_table,
+    w_mod,
+    b_mod,
+    w_qkv,
+    b_q,
+    b_v,
+    w_out,
+    b_out,
+    w_fc1,
+    b_fc1,
+    w_fc2,
+    b_fc2,
+    out_cotangent,
+):
+    rows_here, width_all = latents.shape[1:]
+    columns = class_table.shape[1]
+    owner = lax.axis_index("fsdp")
+    mine = lax.axis_index("seq")
+    fsdp_count = lax.axis_size("fsdp")
+    seq_swap = swapped_pairs(2, 1)
+
+    def whole_latent(pair):
+        kept = lax.dynamic_index_in_dim(pair, mine, 0, keepdims=False)
+        given = lax.dynamic_index_in_dim(pair, 1 - mine, 0, keepdims=False)
+        return jnp.concatenate([kept, lax.ppermute(given, "seq", seq_swap)], axis=0)
+
+    def both_halves(tokens):
+        given = lax.ppermute(tokens[rows_here:], "seq", seq_swap)
+        kept = tokens[:rows_here]
+        first = jnp.where(mine == 0, kept, given)
+        second = jnp.where(mine == 0, given, kept)
+        return jnp.stack([first, second], axis=0)
+
+    class_range = jnp.arange(class_table.shape[0], dtype=jnp.int32)
+    one_hot = (class_ids[:, None] == class_range[None, :]).astype(jnp.bfloat16)
+    looked_up = jnp.dot(one_hot, class_table, preferred_element_type=jnp.float32)
+    timing = lax.dynamic_slice_in_dim(
+        time_features(timesteps, width_all), owner * columns, columns, 1
+    )
+    condition = looked_up + timing
+    lifted_full, lift_pull = jax.vjp(lift_silu, condition)
+    lifted = lifted_full.astype(jnp.bfloat16)
+    mod_width = w_mod.shape[1]
+    mod_cols = b_mod.shape[0]
+    bias_line = lax.dynamic_update_slice_in_dim(
+        jnp.zeros((mod_width,), jnp.float32), b_mod.astype(jnp.float32), owner * mod_cols, 0
+    )
+    lifted_mine = lax.dynamic_index_in_dim(
+        lifted.reshape(fsdp_count, 2, columns), mine, 1, keepdims=False
+    )
+    small = [b_q, b_v, b_out, b_fc1, b_fc2]
+    small_line = wide(jnp.concatenate(small))
+    to_owners = jnp.concatenate(
+        [
+            jnp.dot(lifted_mine, w_mod, preferred_element_type=jnp.float32) + bias_line[None, :],
+            jnp.broadcast_to(small_line[None, :], (fsdp_count, small_line.shape[0])),
+        ],
+        axis=1,
+    )
+    from_owners = lax.all_to_all(to_owners, "fsdp", 0, 0, tiled=True)
+    modulation = jnp.sum(from_owners[:, :mod_width], axis=0, keepdims=True)
+    shift_one, scale_one, gate_one, shift_two, scale_two, gate_two = [
+        modulation[:, position * width_all : (position + 1) * width_all] for position in range(6)
+    ]
+    biases = []
+    begin = mod_width
+    for part in small:
+        end = begin + part.shape[0]
+        biases.append(from_owners[:, begin:end].reshape(1, -1))
+        begin = end
+    query_bias, value_bias, out_bias, up_bias, down_bias = biases
+
+    full_qkv = gather_rows(w_qkv)
+    full_out = gather_rows(w_out)
+    full_fc1 = gather_rows(w_fc1)
+    full_fc2 = gather_rows(w_fc2)
+
+    inputs_full = whole_latent(latents).astype(jnp.float32)
+    grad_output = whole_latent(out_cotangent).astype(jnp.float32)
+    normed_one, inverse_one = normalize_keep(inputs_full)
+    entry_one = low(normed_one * (1.0 + scale_one) + shift_one)
+    qkv_bias = jnp.concatenate([query_bias, jnp.zeros_like(query_bias), value_bias], axis=1)
+    projected = low(jnp.dot(entry_one, full_qkv, preferred_element_type=jnp.float32) + qkv_bias)
+    mixed, log_totals = attend_local(projected)
+    branch_one = jnp.dot(mixed, full_out, preferred_element_type=jnp.float32) + out_bias
+    middle = inputs_full + gate_one * branch_one
+    normed_two, inverse_two = normalize_keep(middle)
+    entry_two = low(normed_two * (1.0 + scale_two) + shift_two)
+    hidden = jnp.dot(entry_two, full_fc1, preferred_element_type=jnp.float32) + up_bias
+    active_full, gelu_pull = jax.vjp(gelu_tanh, hidden)
+    active = low(active_full)
+    grad_branch_two = low(gate_two * grad_output)
+    sum_fc2 = reduce_rows(outer_sum(active, grad_branch_two))
+    branch_two = jnp.dot(active, full_fc2, preferred_element_type=jnp.float32) + down_bias
+    result = both_halves(low(middle + gate_two * branch_two))
+    grad_gate_two = jnp.sum(grad_output * branch_two, axis=0, keepdims=True)
+    grad_active = compared_with(grad_branch_two, full_fc2)
+    grad_hidden = low(gelu_pull(grad_active)[0])
+    sum_fc1 = reduce_rows(outer_sum(entry_two, grad_hidden))
+    grad_entry_two = compared_with(grad_hidden, full_fc1)
+    grad_shift_two = jnp.sum(grad_entry_two, axis=0, keepdims=True)
+    grad_scale_two = jnp.sum(grad_entry_two * normed_two, axis=0, keepdims=True)
+    grad_middle = grad_output + normalize_back(
+        grad_entry_two * (1.0 + scale_two), normed_two, inverse_two
+    )
+    grad_gate_one = jnp.sum(grad_middle * branch_one, axis=0, keepdims=True)
+    grad_branch_one = low(gate_one * grad_middle)
+    sum_out = reduce_rows(outer_sum(mixed, grad_branch_one))
+    grad_mixed = low(compared_with(grad_branch_one, full_out))
+    grad_project = jnp.concatenate(attend_local_back(projected, grad_mixed, log_totals), axis=1)
+    sum_qkv = reduce_rows(outer_sum(entry_one, grad_project))
+    grad_entry_one = compared_with(grad_project, full_qkv)
+    grad_shift_one = jnp.sum(grad_entry_one, axis=0, keepdims=True)
+    grad_scale_one = jnp.sum(grad_entry_one * normed_one, axis=0, keepdims=True)
+    grad_latents = both_halves(
+        grad_middle
+        + normalize_back(grad_entry_one * (1.0 + scale_one), normed_one, inverse_one)
+    )
+    grad_mod_mine = low(
+        jnp.concatenate(
+            [
+                grad_shift_one,
+                grad_scale_one,
+                grad_gate_one,
+                grad_shift_two,
+                grad_scale_two,
+                grad_gate_two,
+            ],
+            axis=1,
+        )
+    )
+    grad_mod_all = lax.all_gather(grad_mod_mine, ("fsdp", "seq"), axis=0, tiled=True)
+    grad_w_mod = outer_sum(lifted, grad_mod_all)
+    grad_b_mod = jnp.sum(
+        lax.dynamic_slice_in_dim(grad_mod_all, owner * mod_cols, mod_cols, 1).astype(jnp.float32),
+        axis=0,
+    )
+    grad_lifted = compared_with(grad_mod_all, w_mod)
+    grad_condition = lift_pull(grad_lifted)[0]
+    grad_table = jnp.dot(
+        one_hot.astype(jnp.float32).T,
+        grad_condition,
+        precision=lax.Precision.HIGHEST,
+        preferred_element_type=jnp.float32,
+    )
+    grad_small = [
+        wide(grad_project[:, :width_all]),
+        wide(grad_project[:, 2 * width_all :]),
+        wide(grad_branch_one),
+        wide(grad_hidden),
+        wide(grad_branch_two),
+    ]
+    small_sums = jnp.concatenate(
+        [jnp.sum(part, axis=0).reshape(fsdp_count, -1) for part in grad_small], axis=1
+    )
+    small_here = jnp.sum(
+        lax.all_to_all(small_sums, "fsdp", 0, 0, tiled=True), axis=0, keepdims=True
+    )
+    small_total = (small_here + lax.ppermute(small_here, "seq", seq_swap))[0]
+    small_grads = []
+    begin = 0
+    for part in small:
+        small_grads.append(small_total[begin : begin + part.shape[0]])
+        begin += part.shape[0]
+    return (
+        result,
+        grad_latents,
+        grad_table,
+        grad_w_mod,
+        grad_b_mod,
+        sum_qkv,
+        small_grads[0],
+        small_grads[1],
+        sum_out,
+        small_grads[2],
+        sum_fc1,
+        small_grads[3],
+        sum_fc2,
+        small_grads[4],
+    )
+
+
 def solution(mesh):
     placed = (
         P("fsdp", "seq", None),
@@ -453,8 +820,14 @@
         P("fsdp"),
         P("fsdp", "seq", None),
     )
+    spans = mesh.shape["fsdp"]
+
+    def body(*arrays):
+        whole_fits = arrays[0].shape[0] == mesh.shape["seq"] == 2 and spans % 4 == 0
+        return (local_whole_latent if whole_fits else local)(*arrays)
+
     return jax.shard_map(
-        local,
+        body,
         mesh=mesh,
         in_specs=placed,
         out_specs=(

time: 1120 us -> 1430 us (1.28)
  Pallas kernels: 0 us -> 798 us
  waiting for transfers between devices: 580 us -> 296 us
  local copies, waits for them, and re-layouts: 158 us -> 24.3 us
  matrix products: 123 us -> 93.3 us
  blocking collectives: 142 us -> 113 us
  other arithmetic: 66.5 us -> 38.2 us
  starting transfers between devices: 28.4 us -> 47.8 us
    pallas_call x0 -> x6, Pallas kernels: none -> 798 us  [the longest x4 767 us: gather_rows(): pl.pallas_call(assemble_kernel, in_specs=[anywhere] * 4, out_specs=anywhe...]
    reduce_scatter x1 -> x0, waiting for transfers between devices: 373 us -> none  [local(): lax.psum_scatter(wide_term(jnp.int32(0), width_all // (fsdp_count * seq_c...]
    ppermute x0 -> x41, waiting for transfers between devices: none -> 199 us  [the longest x4 71.1 us: reduce_rows(): crossed = lax.ppermute(away, 'fsdp', swapped_pairs(count, 2))]
    unnamed x8 -> x3, waiting for transfers between devices: 92.8 us -> 2.06 us
    unnamed x2 -> x0, blocking collectives: 71.6 us -> none
    all_gather x3 -> x2, blocking collectives: 43.4 us -> 113 us  [the longest x1 74.6 us: local_whole_latent(): lax.all_gather(grad_mod_mine, ('fsdp', 'seq'), axis=0, tiled=True)]
    reshape x16 -> x7, local copies, waits for them, and re-layouts: 50.1 us -> 0.44 us  [the longest x5 0.28 us: local_whole_latent(): jnp.sum(part, axis=0).reshape(fsdp_count, -1)]
    ppermute x0 -> x41, starting transfers between devices: none -> 40.4 us  [the longest x12 15.3 us: reduce_rows(): total = total + wide(lax.ppermute(leaving, 'fsdp', pairs))]
  transfers between devices with their start and end apart: 14 -> 46, of which waited for: 7 -> 16; matrix products, arithmetic and copies ran while one was open for 18% -> 7% of each run, Pallas kernels for 0% -> 55%
where the time goes in v1:
time: 1430 us; the launch traced here: 1420 us
  Pallas kernels  798 us (56%)
  waiting for transfers between devices  296 us (21%)
  blocking collectives  113 us (8%)
  matrix products  93.3 us (7%)
  starting transfers between devices  47.8 us (3%)
  other arithmetic  38.2 us (3%)
  local copies, waits for them, and re-layouts  24.3 us (2%)
  between operations  15.2 us (1%)
    pallas_call x4, Pallas kernels, gather_rows(): pl.pallas_call(assemble_kernel, in_specs=[anywhere] * 4, out_specs=anywhe...  767 us
    all_gather x3, waiting for transfers between devices, gather_rows(): lax.all_gather(weight, 'fsdp', axis=0, tiled=False, axis_index_groups=z_g...  93.9 us
    all_gather x1, blocking collectives, local_whole_latent(): lax.all_gather(grad_mod_mine, ('fsdp', 'seq'), axis=0, tiled=True)  74.6 us
    ppermute x4, waiting for transfers between devices, reduce_rows(): crossed = lax.ppermute(away, 'fsdp', swapped_pairs(count, 2))  71.1 us
    ppermute x4, waiting for transfers between devices, gather_rows(): across = lax.ppermute(own, 'fsdp', swapped_pairs(count, 2))  55.1 us
    ppermute x12, waiting for transfers between devices, reduce_rows(): total = total + wide(lax.ppermute(leaving, 'fsdp', pairs))  43.7 us
    all_gather x1, blocking collectives, gather_rows(): lax.all_gather(weight, 'fsdp', axis=0, tiled=False, axis_index_groups=z_g...  38.1 us
    dot_general x5, matrix products, compared_with(): lax.dot_general(earlier_value, latter, (((1,), (1,)), ((), ())), preferre...  33.4 us
  transfers between devices with their start and end apart: 46, of which 16 were waited for; matrix products, arithmetic and copies ran while one was open for 7% of the time, Pallas kernels for 55%

profile of v1, /device:TPU:0, one launch (start us, length us, event | category | flops | bytes accessed | tf_op | source)
XLA Modules:
  0.0 1424.9 jit_solution(12395799259418835047)
XLA Ops:
  15.7 33.9 %all-gather.9.cloned.1.call-done = bf16[256,3072]{1,0:T(8,128)(2,1)} async-done(((bf16[64,3072]{1,0:T(8,128)(2,1)}), bf16[256,3072]{1,0:T(8,128)(2,1)}) %all-gather.9.cloned.1.call-update) | async-done | bytes 1572880 | tf_op jit(solution)/shard_map/all_gather | solution.py:563
  55.9 38.1 %all-gather.1 = bf16[256,1024]{1,0:T(8,128)(2,1)S(1)} all-gather(bf16[64,1024]{1,0:T(8,128)(2,1)S(1)} %copy-done.25), channel_id=3, replica_groups={{0,4,8,12},{1,5,9,13},{2,6,10,14},{3,7,11,15},{16,20,24,28},{17,21,25,2..., dimensions={0}, use_global_device_ids=true | all-gather | bytes 655360 | tf_op jit(solution)/shard_map/all_gather | solution.py:563
  96.6 14.9 %all-gather.13.cloned.1.call-done = bf16[1024,1024]{1,0:T(8,128)(2,1)} async-done(((bf16[256,1024]{1,0:T(8,128)(2,1)}), bf16[1024,1024]{1,0:T(8,128)(2,1)}) %all-gather.13.cloned.1.call-update) | async-done | bytes 2097168 | tf_op jit(solution)/shard_map/all_gather | solution.py:563
  113.0 45.1 %all-gather.11.cloned.1.call-done = bf16[256,4096]{1,0:T(8,128)(2,1)} async-done(((bf16[64,4096]{1,0:T(8,128)(2,1)}), bf16[256,4096]{1,0:T(8,128)(2,1)}) %all-gather.11.cloned.1.call-update) | async-done | bytes 2097168 | tf_op jit(solution)/shard_map/all_gather | solution.py:563
  161.8 55.1 %collective-permute-done.5.p10 = bf16[4,64,1024]{2,1,0:T(8,128)(2,1)S(1)} collective-permute-done((bf16[4,64,1024]{2,1,0:T(8,128)(2,1)S(1)}, bf16[4,64,1024]{2,1,0:T(8,128)(2,1)S(1)}, u32[]{:S(2)}, u32[]{:S(2)}) %collective-permute-start.5) | collective-permute-done | bytes 524320 | tf_op jit(solution)/shard_map/ppermute | solution.py:564
  220.3 64.7 %assemble.5 = bf16[4,4,64,1024]{3,2,1,0:T(8,128)(2,1)} custom-call(bf16[4,64,1024]{2,1,0:T(8,128)(2,1)} %bitcast.233, bf16[4,64,1024]{2,1,0:T(8,128)(2,1)} %collective-permute-done.4.p01, bf16[4,64,1024]{2,1,0:T(8,128)(2,1)} %copy-done.21, bf16[4,64,1024]{2,1,0:T(8,128)(2,1)} %copy-done.22), custom_call_target="tpu_custom_call" | custom-call | bytes 4194304 | tf_op jit(solution)/shard_map/assemble/pallas_call | solution.py:568
  286.1 191.7 %assemble.4 = bf16[4,4,64,3072]{3,2,1,0:T(8,128)(2,1)} custom-call(bf16[4,64,3072]{2,1,0:T(8,128)(2,1)} %bitcast.245, bf16[4,64,3072]{2,1,0:T(8,128)(2,1)} %collective-permute-done.1.p01, bf16[4,64,3072]{2,1,0:T(8,128)(2,1)} %collective-permute-done.2.p10, bf16[4,64,3072]{2,1,0:T(8,128)(2,1)} %collective-permute-done.3.p11), custom_call_target="tpu_custom_call" | custom-call | bytes 12582912 | tf_op jit(solution)/shard_map/assemble/pallas_call | solution.py:568
  477.8 7.2 add_convert_fusion.q_ref.k_ref.v_ref
  485.0 13.0 attend.1
  502.4 255.3 %assemble.6 = bf16[4,4,64,4096]{3,2,1,0:T(8,128)(2,1)} custom-call(bf16[4,64,4096]{2,1,0:T(8,128)(2,1)} %bitcast.239, bf16[4,64,4096]{2,1,0:T(8,128)(2,1)} %collective-permute-done.7.p01, bf16[4,64,4096]{2,1,0:T(8,128)(2,1)} %collective-permute-done.8.p10, bf16[4,64,4096]{2,1,0:T(8,128)(2,1)} %collective-permute-done.9.p11), custom_call_target="tpu_custom_call" | custom-call | bytes 16777216 | tf_op jit(solution)/shard_map/assemble/pallas_call | solution.py:568
  757.7 11.9 fusion.74
  769.6 255.3 %assemble.7 = bf16[4,4,256,1024]{3,2,1,0:T(8,128)(2,1)} custom-call(bf16[4,256,1024]{2,1,0:T(8,128)(2,1)} %bitcast.236, bf16[4,256,1024]{2,1,0:T(8,128)(2,1)} %collective-permute-done.10.p01, bf16[4,256,1024]{2,1,0:T(8,128)(2,1)} %collective-permute-done.11.p10, bf16[4,256,1024]{2,1,0:T(8,128)(2,1)} %collective-permute-done.12.p11), custom_call_target="tpu_custom_call" | custom-call | bytes 16777216 | tf_op jit(solution)/shard_map/assemble/pallas_call | solution.py:568
  1024.9 15.1 %convert_reduce_fusion = (f32[4096]{0:T(1024)S(1)}, bf16[512,4096]{1,0:T(8,128)(2,1)S(1)}) fusion(bf16[4096,1024]{1,0:T(8,128)(2,1)} %bitcast.219, f32[1024]{0:T(1024)S(1)} %bitcast.260, bf16[256,1024]{1,0:T(8,128)(2,1)} %collective-permute-done.14, bf16[256,1024]{1,0:T(8,128)(2,1)S(1)} %copy-done.20, f32[512,4096]{1,0:T(8,128)} %fusion.74, ...), kind=kOutput, calls=%fused_computation.10 | convolution fusion | flops 4354732032 | bytes 22056960 | tf_op jit(solution)/shard_map/dot_general | solution.py:52
  1040.0 9.1 multiply_reduce_fusion
  1049.2 10.9 convert_reduce_fusion.2
  1064.9 5.3 convolution_convert_fusion.1
  1070.3 17.8 %attend_back.1 = (bf16[512,1024]{1,0:T(8,128)(2,1)S(1)}, bf16[512,1024]{1,0:T(8,128)(2,1)S(1)}, bf16[512,1024]{1,0:T(8,128)(2,1)S(1)}) custom-call(bf16[512,3072]{1,0:T(8,128)(2,1)} %copy-done.1, bf16[512,3072]{1,0:T(8,128)(2,1)} %copy-done.1, bf16[512,3072]{1,0:T(8,128)(2,1)} %copy-done.1, bf16[512,1024]{1,0:T(8,128)(2,1)S(1)} %convolution_convert_fusion.4.do_ref, ...), custom_call_target="tpu_custom_call" | custom-call | flops 10737418240 | bytes 9437184 | tf_op jit(solution)/shard_map/attend_back/pallas_call | solution.py:517
  1088.3 4.3 convolution_convert_fusion.2
  1100.6 10.2 convolution_convert_fusion
  1116.4 6.4 fusion.21
  1125.0 74.6 %all-gather.4 = bf16[32,1,6144]{2,1,0:T(2,128)(2,1)} all-gather(bf16[1,1,6144]{2,1,0:T(2,128)(2,1)S(1)} %bitcast.249), channel_id=1, replica_groups=mesh['seq'=2,'fsdp'=16] {'fsdp','seq'}, dimensions={0}, use_global_device_ids=true | all-gather | bytes 405504 | tf_op jit(solution)/shard_map/all_gather | solution.py:753
  1200.8 3.7 all-to-all-start.1
  1220.4 5.2 fusion.8
  1227.1 7.1 fusion.7
  1235.5 14.5 %collective-permute-done.15 = f32[256,1024]{1,0:T(8,128)S(1)} collective-permute-done((f32[256,1024]{1,0:T(8,128)S(1)}, f32[256,1024]{1,0:T(8,128)S(1)}, u32[]{:S(2)}, u32[]{:S(2)}) %collective-permute-start.15) | collective-permute-done | bytes 1048608 | tf_op jit(solution)/shard_map/ppermute | solution.py:649
  1254.6 4.3 fusion.6
  1260.4 4.0 collective-permute-done.26
  1276.7 36.7 %collective-permute-done.30 = bf16[4,64,4096]{2,1,0:T(8,128)(2,1)} collective-permute-done((bf16[4,64,4096]{2,1,0:T(8,128)(2,1)}, bf16[4,64,4096]{2,1,0:T(8,128)(2,1)}, u32[]{:S(2)}, u32[]{:S(2)}) %collective-permute-start.30) | collective-permute-done | bytes 2097184 | tf_op jit(solution)/shard_map/ppermute | solution.py:606
  1321.2 34.4 %collective-permute-done.36 = bf16[4,256,1024]{2,1,0:T(8,128)(2,1)S(1)} collective-permute-done((bf16[4,256,1024]{2,1,0:T(8,128)(2,1)S(1)}, bf16[4,256,1024]{2,1,0:T(8,128)(2,1)S(1)}, u32[]{:S(2)}, u32[]{:S(2)}) %collective-permute-start.36) | collective-permute-done | bytes 2097184 | tf_op jit(solution)/shard_map/ppermute | solution.py:606
  1364.2 7.3 collective-permute-done.39
  1371.5 31.9 %collective-permute-done.38 = bf16[256,1024]{1,0:T(8,128)(2,1)S(1)} collective-permute-done((bf16[256,1024]{1,0:T(8,128)(2,1)S(1)}, bf16[256,1024]{1,0:T(8,128)(2,1)S(1)}, u32[]{:S(2)}, u32[]{:S(2)}) %collective-permute-start.38) | collective-permute-done | bytes 524320 | tf_op jit(solution)/shard_map/ppermute | solution.py:613
  1407.1 9.7 collective-permute-done.40
  (260 shorter events, 111.2 us)
Async XLA Ops:
  8.0 103.5 %all-gather.13.cloned.1.call-start = ((), (), s32[]{:S(2)}) async-start(), calls=%async_computation.4 | async-start | bytes 2621440 | tf_op jit(solution)/shard_map/all_gather | solution.py:563
  8.8 149.3 %all-gather.11.cloned.1.call-start = ((), (), s32[]{:S(2)}) async-start(), calls=%async_computation.3 | async-start | bytes 2621440 | tf_op jit(solution)/shard_map/all_gather | solution.py:563
  10.4 86.0 %collective-permute-start = (bf16[256,1024]{1,0:T(8,128)(2,1)}, bf16[256,1024]{1,0:T(8,128)(2,1)S(1)}, u32[]{:S(2)}, u32[]{:S(2)}) collective-permute-start(bf16[256,1024]{1,0:T(8,128)(2,1)} %get-tuple-element.72), channel_id=1, source_target_pairs={{0,16},{16,0},{1,17},{17,1},{2,18},{18,2},{3,19},{19,3},{4,20},{20... | collective-permute-start | bytes 1572872 | tf_op jit(solution)/shard_map/ppermute | solution.py:646
  49.6 110.5 %collective-permute-start.2 = (bf16[4,64,3072]{2,1,0:T(8,128)(2,1)}, bf16[4,64,3072]{2,1,0:T(8,128)(2,1)}, u32[]{:S(2)}, u32[]{:S(2)}) collective-permute-start(bf16[4,64,3072]{2,1,0:T(8,128)(2,1)} %bitcast.243), channel_id=1, source_target_pairs={{0,2},{1,3},{2,0},{3,1},{4,6},{5,7},{6,4},{7,5},{8,10},{9,11},{10,... | collective-permute-start | bytes 4718600 | tf_op jit(solution)/shard_map/ppermute | solution.py:564
  52.3 108.3 %all-to-all-start = ((f32[16,1,6656]{2,1,0:T(1,128)}), f32[16,1,6656]{2,1,0:T(1,128)S(1)}, u32[]{:S(2)}, u32[]{:S(2)}) async-start(f32[16,1,6656]{2,1,0:T(1,128)} %copy.56), calls=%async_computation | async-start | bytes 851968 | tf_op jit(solution)/shard_map/all_to_all | solution.py:681
  94.0 67.0 %collective-permute-start.4 = (bf16[4,64,1024]{2,1,0:T(8,128)(2,1)S(1)}, bf16[4,64,1024]{2,1,0:T(8,128)(2,1)}, u32[]{:S(2)}, u32[]{:S(2)}) collective-permute-start(bf16[4,64,1024]{2,1,0:T(8,128)(2,1)S(1)} %bitcast.231), channel_id=1, source_target_pairs={{0,1},{1,0},{2,3},{3,2},{4,5},{5,4},{6,7},{7,6},{8,9},{9,8},{10,11... | collective-permute-start | bytes 1572872 | tf_op jit(solution)/shard_map/ppermute | solution.py:565
  111.5 173.6 %collective-permute-start.11 = (bf16[4,256,1024]{2,1,0:T(8,128)(2,1)}, bf16[4,256,1024]{2,1,0:T(8,128)(2,1)}, u32[]{:S(2)}, u32[]{:S(2)}) collective-permute-start(bf16[4,256,1024]{2,1,0:T(8,128)(2,1)} %bitcast.234), channel_id=1, source_target_pairs={{0,2},{1,3},{2,0},{3,1},{4,6},{5,7},{6,4},{7,5},{8,10},{9,11},{10,... | collective-permute-start | bytes 6291464 | tf_op jit(solution)/shard_map/ppermute | solution.py:564
  158.1 127.5 %collective-permute-start.8 = (bf16[4,64,4096]{2,1,0:T(8,128)(2,1)}, bf16[4,64,4096]{2,1,0:T(8,128)(2,1)}, u32[]{:S(2)}, u32[]{:S(2)}) collective-permute-start(bf16[4,64,4096]{2,1,0:T(8,128)(2,1)} %bitcast.237), channel_id=1, source_target_pairs={{0,2},{1,3},{2,0},{3,1},{4,6},{5,7},{6,4},{7,5},{8,10},{9,11},{10,... | collective-permute-start | bytes 6291464 | tf_op jit(solution)/shard_map/ppermute | solution.py:564
  160.0 125.0 %collective-permute-start.1 = (bf16[4,64,3072]{2,1,0:T(8,128)(2,1)}, bf16[4,64,3072]{2,1,0:T(8,128)(2,1)}, u32[]{:S(2)}, u32[]{:S(2)}) collective-permute-start(bf16[4,64,3072]{2,1,0:T(8,128)(2,1)} %bitcast.244), channel_id=1, source_target_pairs={{0,1},{1,0},{2,3},{3,2},{4,5},{5,4},{6,7},{7,6},{8,9},{9,8},{10,11... | collective-permute-start | bytes 4718600 | tf_op jit(solution)/shard_map/ppermute | solution.py:565
  160.1 125.6 %collective-permute-start.3 = (bf16[4,64,3072]{2,1,0:T(8,128)(2,1)}, bf16[4,64,3072]{2,1,0:T(8,128)(2,1)}, u32[]{:S(2)}, u32[]{:S(2)}) collective-permute-start(bf16[4,64,3072]{2,1,0:T(8,128)(2,1)} %collective-permute-done.2.p10), channel_id=1, source_target_pairs={{0,1},{1,0},{2,3},{3,2},{4,5},{5,4},{6,7},{7,6},{8,9},{9,8},{10,11... | collective-permute-start | bytes 4718600 | tf_op jit(solution)/shard_map/ppermute | solution.py:566
  161.0 55.9 %collective-permute-start.5 = (bf16[4,64,1024]{2,1,0:T(8,128)(2,1)S(1)}, bf16[4,64,1024]{2,1,0:T(8,128)(2,1)S(1)}, u32[]{:S(2)}, u32[]{:S(2)}) collective-permute-start(bf16[4,64,1024]{2,1,0:T(8,128)(2,1)S(1)} %bitcast.232), channel_id=1, source_target_pairs={{0,2},{1,3},{2,0},{3,1},{4,6},{5,7},{6,4},{7,5},{8,10},{9,11},{10,... | collective-permute-start | bytes 1572872 | tf_op jit(solution)/shard_map/ppermute | solution.py:564
  218.8 806.0 %collective-permute-start.14 = (bf16[256,1024]{1,0:T(8,128)(2,1)}, bf16[256,1024]{1,0:T(8,128)(2,1)}, u32[]{:S(2)}, u32[]{:S(2)}) collective-permute-start(bf16[256,1024]{1,0:T(8,128)(2,1)} %get-tuple-element.70), channel_id=1, source_target_pairs={{0,16},{16,0},{1,17},{17,1},{2,18},{18,2},{3,19},{19,3},{4,20},{20... | collective-permute-start | bytes 1572872 | tf_op jit(solution)/shard_map/ppermute | solution.py:646
  285.0 484.6 %collective-permute-start.10 = (bf16[4,256,1024]{2,1,0:T(8,128)(2,1)}, bf16[4,256,1024]{2,1,0:T(8,128)(2,1)}, u32[]{:S(2)}, u32[]{:S(2)}) collective-permute-start(bf16[4,256,1024]{2,1,0:T(8,128)(2,1)} %bitcast.235), channel_id=1, source_target_pairs={{0,1},{1,0},{2,3},{3,2},{4,5},{5,4},{6,7},{7,6},{8,9},{9,8},{10,11... | collective-permute-start | bytes 6291464 | tf_op jit(solution)/shard_map/ppermute | solution.py:565
  285.1 217.3 %collective-permute-start.7 = (bf16[4,64,4096]{2,1,0:T(8,128)(2,1)}, bf16[4,64,4096]{2,1,0:T(8,128)(2,1)}, u32[]{:S(2)}, u32[]{:S(2)}) collective-permute-start(bf16[4,64,4096]{2,1,0:T(8,128)(2,1)} %bitcast.238), channel_id=1, source_target_pairs={{0,1},{1,0},{2,3},{3,2},{4,5},{5,4},{6,7},{7,6},{8,9},{9,8},{10,11... | collective-permute-start | bytes 6291464 | tf_op jit(solution)/shard_map/ppermute | solution.py:565
  285.6 484.0 %collective-permute-start.12 = (bf16[4,256,1024]{2,1,0:T(8,128)(2,1)}, bf16[4,256,1024]{2,1,0:T(8,128)(2,1)}, u32[]{:S(2)}, u32[]{:S(2)}) collective-permute-start(bf16[4,256,1024]{2,1,0:T(8,128)(2,1)} %collective-permute-done.11.p10), channel_id=1, source_target_pairs={{0,1},{1,0},{2,3},{3,2},{4,5},{5,4},{6,7},{7,6},{8,9},{9,8},{10,11... | collective-permute-start | bytes 6291464 | tf_op jit(solution)/shard_map/ppermute | solution.py:566
  285.7 216.7 %collective-permute-start.9 = (bf16[4,64,4096]{2,1,0:T(8,128)(2,1)}, bf16[4,64,4096]{2,1,0:T(8,128)(2,1)}, u32[]{:S(2)}, u32[]{:S(2)}) collective-permute-start(bf16[4,64,4096]{2,1,0:T(8,128)(2,1)} %collective-permute-done.8.p10), channel_id=1, source_target_pairs={{0,1},{1,0},{2,3},{3,2},{4,5},{5,4},{6,7},{7,6},{8,9},{9,8},{10,11... | collective-permute-start | bytes 6291464 | tf_op jit(solution)/shard_map/ppermute | solution.py:566
  1096.4 123.3 %collective-permute-start.16 = (bf16[4,2,64,3072]{3,2,0,1:T(8,128)(2,1)}, bf16[4,2,64,3072]{3,2,0,1:T(8,128)(2,1)}, u32[]{:S(2)}, u32[]{:S(2)}) collective-permute-start(bf16[4,2,64,3072]{3,2,0,1:T(8,128)(2,1)} %copy_bitcast_fusion.2), channel_id=1, source_target_pairs={{0,1},{1,0},{2,3},{3,2},{4,5},{5,4},{6,7},{7,6},{8,9},{9,8},{10,11... | collective-permute-start | bytes 9437192 | tf_op jit(solution)/shard_map/ppermute | solution.py:603
  1097.5 119.7 %collective-permute-start.23 = (bf16[4,2,64,1024]{3,2,0,1:T(8,128)(2,1)}, bf16[4,2,64,1024]{3,2,0,1:T(8,128)(2,1)}, u32[]{:S(2)}, u32[]{:S(2)}) collective-permute-start(bf16[4,2,64,1024]{3,2,0,1:T(8,128)(2,1)} %copy_bitcast_fusion.3), channel_id=1, source_target_pairs={{0,1},{1,0},{2,3},{3,2},{4,5},{5,4},{6,7},{7,6},{8,9},{9,8},{10,11... | collective-permute-start | bytes 3145736 | tf_op jit(solution)/shard_map/ppermute | solution.py:603
  1100.5 125.1 %collective-permute-start.29 = (bf16[4,2,64,4096]{3,2,0,1:T(8,128)(2,1)}, bf16[4,2,64,4096]{3,2,0,1:T(8,128)(2,1)}, u32[]{:S(2)}, u32[]{:S(2)}) collective-permute-start(bf16[4,2,64,4096]{3,2,0,1:T(8,128)(2,1)} %copy_bitcast_fusion.1), channel_id=1, source_target_pairs={{0,1},{1,0},{2,3},{3,2},{4,5},{5,4},{6,7},{7,6},{8,9},{9,8},{10,11... | collective-permute-start | bytes 12582920 | tf_op jit(solution)/shard_map/ppermute | solution.py:603
  1116.0 137.4 %collective-permute-start.35 = (bf16[4,2,256,1024]{3,2,0,1:T(8,128)(2,1)}, bf16[4,2,256,1024]{3,2,0,1:T(8,128)(2,1)}, u32[]{:S(2)}, u32[]{:S(2)}) collective-permute-start(bf16[4,2,256,1024]{3,2,0,1:T(8,128)(2,1)} %copy_bitcast_fusion), channel_id=1, source_target_pairs={{0,1},{1,0},{2,3},{3,2},{4,5},{5,4},{6,7},{7,6},{8,9},{9,8},{10,11... | collective-permute-start | bytes 12582920 | tf_op jit(solution)/shard_map/ppermute | solution.py:603
  1225.6 45.6 %collective-permute-start.17 = (bf16[4,64,3072]{2,1,0:T(8,128)(2,1)}, bf16[4,64,3072]{2,1,0:T(8,128)(2,1)}, u32[]{:S(2)}, u32[]{:S(2)}) collective-permute-start(bf16[4,64,3072]{2,1,0:T(8,128)(2,1)} %get-tuple-element.43), channel_id=1, source_target_pairs={{0,2},{1,3},{2,0},{3,1},{4,6},{5,7},{6,4},{7,5},{8,10},{9,11},{10,... | collective-permute-start | bytes 4718600 | tf_op jit(solution)/shard_map/ppermute | solution.py:606
  1234.1 79.2 %collective-permute-start.30 = (bf16[4,64,4096]{2,1,0:T(8,128)(2,1)}, bf16[4,64,4096]{2,1,0:T(8,128)(2,1)}, u32[]{:S(2)}, u32[]{:S(2)}) collective-permute-start(bf16[4,64,4096]{2,1,0:T(8,128)(2,1)} %get-tuple-element.41), channel_id=1, source_target_pairs={{0,2},{1,3},{2,0},{3,1},{4,6},{5,7},{6,4},{7,5},{8,10},{9,11},{10,... | collective-permute-start | bytes 6291464 | tf_op jit(solution)/shard_map/ppermute | solution.py:606
  1258.9 96.7 %collective-permute-start.36 = (bf16[4,256,1024]{2,1,0:T(8,128)(2,1)S(1)}, bf16[4,256,1024]{2,1,0:T(8,128)(2,1)S(1)}, u32[]{:S(2)}, u32[]{:S(2)}) collective-permute-start(bf16[4,256,1024]{2,1,0:T(8,128)(2,1)S(1)} %get-tuple-element.39), channel_id=1, source_target_pairs={{0,2},{1,3},{2,0},{3,1},{4,6},{5,7},{6,4},{7,5},{8,10},{9,11},{10,... | collective-permute-start | bytes 6291464 | tf_op jit(solution)/shard_map/ppermute | solution.py:606
  1272.6 45.0 %collective-permute-start.20 = (bf16[64,3072]{1,0:T(8,128)(2,1)S(1)}, bf16[64,3072]{1,0:T(8,128)(2,1)S(1)}, u32[]{:S(2)}, u32[]{:S(2)}) collective-permute-start(bf16[64,3072]{1,0:T(8,128)(2,1)S(1)} %get-tuple-element.52), channel_id=1, source_target_pairs={{0,12},{1,13},{2,14},{3,15},{4,0},{5,1},{6,2},{7,3},{8,4},{9,5},{1... | collective-permute-start | bytes 1179656 | tf_op jit(solution)/shard_map/ppermute | solution.py:613
  1273.4 44.2 %collective-permute-start.19 = (bf16[64,3072]{1,0:T(8,128)(2,1)S(1)}, bf16[64,3072]{1,0:T(8,128)(2,1)S(1)}, u32[]{:S(2)}, u32[]{:S(2)}) collective-permute-start(bf16[64,3072]{1,0:T(8,128)(2,1)S(1)} %get-tuple-element.53), channel_id=1, source_target_pairs={{0,8},{1,9},{2,10},{3,11},{4,12},{5,13},{6,14},{7,15},{8,0},{9,1},... | collective-permute-start | bytes 1179656 | tf_op jit(solution)/shard_map/ppermute | solution.py:613
  1274.7 44.0 %collective-permute-start.18 = (bf16[64,3072]{1,0:T(8,128)(2,1)S(1)}, bf16[64,3072]{1,0:T(8,128)(2,1)S(1)}, u32[]{:S(2)}, u32[]{:S(2)}) collective-permute-start(bf16[64,3072]{1,0:T(8,128)(2,1)S(1)} %get-tuple-element.51), channel_id=1, source_target_pairs={{0,4},{1,5},{2,6},{3,7},{4,8},{5,9},{6,10},{7,11},{8,12},{9,13},{1... | collective-permute-start | bytes 1179656 | tf_op jit(solution)/shard_map/ppermute | solution.py:613
  1315.1 44.0 %collective-permute-start.33 = (bf16[64,4096]{1,0:T(8,128)(2,1)S(1)}, bf16[64,4096]{1,0:T(8,128)(2,1)S(1)}, u32[]{:S(2)}, u32[]{:S(2)}) collective-permute-start(bf16[64,4096]{1,0:T(8,128)(2,1)S(1)} %get-tuple-element.49), channel_id=1, source_target_pairs={{0,12},{1,13},{2,14},{3,15},{4,0},{5,1},{6,2},{7,3},{8,4},{9,5},{1... | collective-permute-start | bytes 1572872 | tf_op jit(solution)/shard_map/ppermute | solution.py:613
  1317.6 42.6 %collective-permute-start.31 = (bf16[64,4096]{1,0:T(8,128)(2,1)S(1)}, bf16[64,4096]{1,0:T(8,128)(2,1)S(1)}, u32[]{:S(2)}, u32[]{:S(2)}) collective-permute-start(bf16[64,4096]{1,0:T(8,128)(2,1)S(1)} %get-tuple-element.48), channel_id=1, source_target_pairs={{0,4},{1,5},{2,6},{3,7},{4,8},{5,9},{6,10},{7,11},{8,12},{9,13},{1... | collective-permute-start | bytes 1572872 | tf_op jit(solution)/shard_map/ppermute | solution.py:613
  1320.0 43.3 %collective-permute-start.21 = (bf16[64,3072]{1,0:T(8,128)(2,1)S(1)}, bf16[64,3072]{1,0:T(8,128)(2,1)S(1)}, u32[]{:S(2)}, u32[]{:S(2)}) collective-permute-start(bf16[64,3072]{1,0:T(8,128)(2,1)S(1)} %fusion.39), channel_id=1, source_target_pairs={{0,16},{16,0},{1,17},{17,1},{2,18},{18,2},{3,19},{19,3},{4,20},{20... | collective-permute-start | bytes 1179656 | tf_op jit(solution)/shard_map/ppermute | solution.py:615
  1359.1 44.3 %collective-permute-start.38 = (bf16[256,1024]{1,0:T(8,128)(2,1)S(1)}, bf16[256,1024]{1,0:T(8,128)(2,1)S(1)}, u32[]{:S(2)}, u32[]{:S(2)}) collective-permute-start(bf16[256,1024]{1,0:T(8,128)(2,1)S(1)} %get-tuple-element.47), channel_id=1, source_target_pairs={{0,8},{1,9},{2,10},{3,11},{4,12},{5,13},{6,14},{7,15},{8,0},{9,1},... | collective-permute-start | bytes 1572872 | tf_op jit(solution)/shard_map/ppermute | solution.py:613
  1359.7 43.7 %collective-permute-start.37 = (bf16[256,1024]{1,0:T(8,128)(2,1)S(1)}, bf16[256,1024]{1,0:T(8,128)(2,1)S(1)}, u32[]{:S(2)}, u32[]{:S(2)}) collective-permute-start(bf16[256,1024]{1,0:T(8,128)(2,1)S(1)} %get-tuple-element.45), channel_id=1, source_target_pairs={{0,4},{1,5},{2,6},{3,7},{4,8},{5,9},{6,10},{7,11},{8,12},{9,13},{1... | collective-permute-start | bytes 1572872 | tf_op jit(solution)/shard_map/ppermute | solution.py:613
  1361.6 44.4 %collective-permute-start.34 = (bf16[64,4096]{1,0:T(8,128)(2,1)S(1)}, bf16[64,4096]{1,0:T(8,128)(2,1)S(1)}, u32[]{:S(2)}, u32[]{:S(2)}) collective-permute-start(bf16[64,4096]{1,0:T(8,128)(2,1)S(1)} %fusion.31), channel_id=1, source_target_pairs={{0,16},{16,0},{1,17},{17,1},{2,18},{18,2},{3,19},{19,3},{4,20},{20... | collective-permute-start | bytes 1572872 | tf_op jit(solution)/shard_map/ppermute | solution.py:615
  (57 other events, 2024.2 us)
Sparse Core Ops, SparseCore 0:
  9.7 39.8 all-gather.8
  51.1 60.3 all-gather.12
  113.1 44.9 all-gather.10

commit v2 on v1

--- a/solution.py
+++ b/solution.py
@@ -536,72 +536,126 @@
     return [(place, place ^ bit) for place in range(count)]
 
 
-def assemble_kernel(p00, p01, p10, p11, out_ref, sems):
-    owner = lax.axis_index("fsdp")
-    core_at = lax.rem(owner, 2)
-    x_at = lax.rem(lax.div(owner, 2), 2)
-    copies = []
-    for place, (piece, flip_x, flip_core) in enumerate(
-        ((p00, 0, 0), (p01, 0, 1), (p10, 1, 0), (p11, 1, 1))
-    ):
-        to_x = 1 - x_at if flip_x else x_at
-        to_core = 1 - core_at if flip_core else core_at
-        copies.append(
-            pltpu.make_async_copy(piece, out_ref.at[:, to_x * 2 + to_core], sems.at[place])
-        )
-    for copy in copies:
-        copy.start()
-    for copy in copies:
-        copy.wait()
-
-
-def gather_rows(weight):
+def assemble_kernel(place_ref, p00, p01, p10, p11, *out_refs):
+    del place_ref
+    for which, piece in enumerate((p00, p01, p10, p11)):
+
+        @pl.when(pl.program_id(0) == which)
+        def _():
+            begin = 0
+            for out_ref in out_refs:
+                end = begin + out_ref.shape[-1]
+                out_ref[0, 0] = piece[0, :, begin:end]
+                begin = end
+
+
+def gather_rows(weight, *widths):
     rows, columns = weight.shape
     count = lax.axis_size("fsdp")
     depth = count // 4
+    owner = lax.axis_index("fsdp")
     z_groups = [[base + 4 * step for step in range(depth)] for base in range(4)]
     own = lax.all_gather(weight, "fsdp", axis=0, tiled=False, axis_index_groups=z_groups)
     across = lax.ppermute(own, "fsdp", swapped_pairs(count, 2))
     own_core = lax.ppermute(own, "fsdp", swapped_pairs(count, 1))
     across_core = lax.ppermute(across, "fsdp", swapped_pairs(count, 1))
-    anywhere = pl.BlockSpec(memory_space=pl.ANY)
+    places = jnp.bitwise_xor(lax.rem(owner, 4), jnp.arange(4, dtype=jnp.int32))
+
+    def piece_spec(which):
+        def block(p, z, place_ref):
+            del place_ref
+            return (jnp.where(p == which, z, jnp.where(p < which, 0, depth - 1)), 0, 0)
+
+        return pl.BlockSpec((1, rows, columns), block)
+
+    def out_block(p, z, place_ref):
+        return (z, place_ref[p], 0, 0)
+
     whole = pl.pallas_call(
         assemble_kernel,
-        in_specs=[anywhere] * 4,
-        out_specs=anywhere,
-        out_shape=jax.ShapeDtypeStruct((depth, 4, rows, columns), weight.dtype),
-        scratch_shapes=[pltpu.SemaphoreType.DMA((4,))],
+        grid_spec=pltpu.PrefetchScalarGridSpec(
+            num_scalar_prefetch=1,
+            grid=(4, depth),
+            in_specs=[piece_spec(which) for which in range(4)],
+            out_specs=[pl.BlockSpec((1, 1, rows, width), out_block) for width in widths],
+        ),
+        out_shape=[
+            jax.ShapeDtypeStruct((depth, 4, rows, width), weight.dtype) for width in widths
+        ],
+        compiler_params=pltpu.CompilerParams(vmem_limit_bytes=VMEM_LIMIT),
         cost_estimate=pl.CostEstimate(
             flops=0, bytes_accessed=16 * depth * rows * columns, transcendentals=0
         ),
         name="assemble",
-    )(own, own_core, across, across_core)
-    return whole.reshape(count * rows, columns)
-
-
-def low(tensor):
-    return tensor.astype(jnp.bfloat16)
-
-
-def wide(tensor):
-    return tensor.astype(jnp.float32)
-
-
-def reduce_rows(partial):
+    )(places, own, own_core, across, across_core)
+    return [part.reshape(count * rows, -1) for part in whole]
+
+
+def gather_latents(line):
     count = lax.axis_size("fsdp")
     depth = count // 4
     owner = lax.axis_index("fsdp")
-    core_at = lax.rem(owner, 2)
+    z_at = lax.div(owner, 4)
+
+    def doubled(tensor, place, axis, other):
+        first = jnp.where(place == 0, tensor, other)
+        second = jnp.where(place == 0, other, tensor)
+        return jnp.stack([first, second], axis=axis)
+
+    tensor = doubled(
+        line, lax.axis_index("seq"), 0, lax.ppermute(line, "seq", swapped_pairs(2, 1))
+    )
+    tensor = doubled(
+        tensor, lax.rem(owner, 2), 0, lax.ppermute(tensor, "fsdp", swapped_pairs(count, 1))
+    )
+    tensor = doubled(
+        tensor,
+        lax.rem(lax.div(owner, 2), 2),
+        0,
+        lax.ppermute(tensor, "fsdp", swapped_pairs(count, 2)),
+    )
+    tensor = tensor.reshape(8, -1)
+    slots = [tensor]
+    for shift in range(1, depth):
+        pairs = [(place, (place + 4 * shift) % count) for place in range(count)]
+        slots.append(lax.ppermute(tensor, "fsdp", pairs))
+    ordered = []
+    for z in range(depth):
+        shift = lax.rem(z_at - z + depth, depth)
+        chosen = slots[0]
+        for step in range(1, depth):
+            chosen = jnp.where(shift == step, slots[step], chosen)
+        ordered.append(chosen)
+    return jnp.concatenate(ordered, axis=0)
+
+
+def low(tensor):
+    return tensor.astype(jnp.bfloat16)
+
+
+def wide(tensor):
+    return tensor.astype(jnp.float32)
+
+
+def pick(tensor, axis, place):
+    return lax.dynamic_index_in_dim(tensor, place, axis, keepdims=False)
+
+
+def reduce_begin(partial):
+    count = lax.axis_size("fsdp")
+    core_at = lax.rem(lax.axis_index("fsdp"), 2)
+    rows, columns = partial.shape
+    blocks = low(partial).reshape(count // 4, 2, 2, rows // count, columns)
+    return pick(blocks, 2, core_at), pick(blocks, 2, 1 - core_at)
+
+
+def reduce_end(kept, leaving):
+    count = lax.axis_size("fsdp")
+    depth = count // 4
+    owner = lax.axis_index("fsdp")
     x_at = lax.rem(lax.div(owner, 2), 2)
     z_at = lax.div(owner, 4)
-    columns = partial.shape[1]
-    blocks = low(partial).reshape(depth, 2, 2, partial.shape[0] // count, columns)
-
-    def pick(tensor, axis, place):
-        return lax.dynamic_index_in_dim(tensor, place, axis, keepdims=False)
-
-    arrived = lax.ppermute(pick(blocks, 2, 1 - core_at), "fsdp", swapped_pairs(count, 1))
-    kept = pick(blocks, 2, core_at)
+    arrived = lax.ppermute(leaving, "fsdp", swapped_pairs(count, 1))
     away = low(wide(pick(kept, 1, 1 - x_at)) + wide(pick(arrived, 1, 1 - x_at)))
     crossed = lax.ppermute(away, "fsdp", swapped_pairs(count, 2))
     here = wide(pick(kept, 1, x_at)) + wide(pick(arrived, 1, x_at))
@@ -691,10 +745,11 @@
         begin = end
     query_bias, value_bias, out_bias, up_bias, down_bias = biases
 
-    full_qkv = gather_rows(w_qkv)
-    full_out = gather_rows(w_out)
-    full_fc1 = gather_rows(w_fc1)
-    full_fc2 = gather_rows(w_fc2)
+    full_qkv, full_out = gather_rows(
+        jnp.concatenate([w_qkv, w_out], axis=1), w_qkv.shape[1], w_out.shape[1]
+    )
+    (full_fc1,) = gather_rows(w_fc1, w_fc1.shape[1])
+    (full_fc2,) = gather_rows(w_fc2, w_fc2.shape[1])
 
     inputs_full = whole_latent(latents).astype(jnp.float32)
     grad_output = whole_latent(out_cotangent).astype(jnp.float32)
@@ -711,13 +766,19 @@
     active_full, gelu_pull = jax.vjp(gelu_tanh, hidden)
     active = low(active_full)
     grad_branch_two = low(gate_two * grad_output)
-    sum_fc2 = reduce_rows(outer_sum(active, grad_branch_two))
+    kept_fc2, leaving_fc2 = reduce_begin(outer_sum(active, grad_branch_two))
+    active, grad_branch_two, leaving_fc2 = lax.optimization_barrier(
+        (active, grad_branch_two, leaving_fc2)
+    )
+    sum_fc2 = reduce_end(kept_fc2, leaving_fc2)
     branch_two = jnp.dot(active, full_fc2, preferred_element_type=jnp.float32) + down_bias
     result = both_halves(low(middle + gate_two * branch_two))
     grad_gate_two = jnp.sum(grad_output * branch_two, axis=0, keepdims=True)
     grad_active = compared_with(grad_branch_two, full_fc2)
     grad_hidden = low(gelu_pull(grad_active)[0])
-    sum_fc1 = reduce_rows(outer_sum(entry_two, grad_hidden))
+    kept_fc1, leaving_fc1 = reduce_begin(outer_sum(entry_two, grad_hidden))
+    grad_hidden, leaving_fc1 = lax.optimization_barrier((grad_hidden, leaving_fc1))
+    sum_fc1 = reduce_end(kept_fc1, leaving_fc1)
     grad_entry_two = compared_with(grad_hidden, full_fc1)
     grad_shift_two = jnp.sum(grad_entry_two, axis=0, keepdims=True)
     grad_scale_two = jnp.sum(grad_entry_two * normed_two, axis=0, keepdims=True)
@@ -725,11 +786,22 @@
         grad_entry_two * (1.0 + scale_two), normed_two, inverse_two
     )
     grad_gate_one = jnp.sum(grad_middle * branch_one, axis=0, keepdims=True)
+    grad_mod_early = gather_latents(
+        low(
+            jnp.concatenate(
+                [grad_gate_one, grad_shift_two, grad_scale_two, grad_gate_two], axis=1
+            )
+        )
+    )
     grad_branch_one = low(gate_one * grad_middle)
-    sum_out = reduce_rows(outer_sum(mixed, grad_branch_one))
+    kept_out, leaving_out = reduce_begin(outer_sum(mixed, grad_branch_one))
+    grad_branch_one, leaving_out = lax.optimization_barrier((grad_branch_one, leaving_out))
+    sum_out = reduce_end(kept_out, leaving_out)
     grad_mixed = low(compared_with(grad_branch_one, full_out))
     grad_project = jnp.concatenate(attend_local_back(projected, grad_mixed, log_totals), axis=1)
-    sum_qkv = reduce_rows(outer_sum(entry_one, grad_project))
+    kept_qkv, leaving_qkv = reduce_begin(outer_sum(entry_one, grad_project))
+    grad_project, leaving_qkv = lax.optimization_barrier((grad_project, leaving_qkv))
+    sum_qkv = reduce_end(kept_qkv, leaving_qkv)
     grad_entry_one = compared_with(grad_project, full_qkv)
     grad_shift_one = jnp.sum(grad_entry_one, axis=0, keepdims=True)
     grad_scale_one = jnp.sum(grad_entry_one * normed_one, axis=0, keepdims=True)
@@ -737,20 +809,8 @@
         grad_middle
         + normalize_back(grad_entry_one * (1.0 + scale_one), normed_one, inverse_one)
     )
-    grad_mod_mine = low(
-        jnp.concatenate(
-            [
-                grad_shift_one,
-                grad_scale_one,
-                grad_gate_one,
-                grad_shift_two,
-                grad_scale_two,
-                grad_gate_two,
-            ],
-            axis=1,
-        )
-    )
-    grad_mod_all = lax.all_gather(grad_mod_mine, ("fsdp", "seq"), axis=0, tiled=True)
+    grad_mod_late = low(jnp.concatenate([grad_shift_one, grad_scale_one], axis=1))
+    grad_mod_all = jnp.concatenate([gather_latents(grad_mod_late), grad_mod_early], axis=1)
     grad_w_mod = outer_sum(lifted, grad_mod_all)
     grad_b_mod = jnp.sum(
         lax.dynamic_slice_in_dim(grad_mod_all, owner * mod_cols, mod_cols, 1).astype(jnp.float32),

time: 1430 us -> 698 us (0.49)
  the two profiles are of different devices: /device:TPU:0 before, /device:TPU:12 now
where the time goes in v2:
time: 698 us; the launch traced here: 688 us
  waiting for transfers between devices  385 us (55%)
  matrix products  89.4 us (13%)
  Pallas kernels  66.4 us (10%)
  starting transfers between devices  62.3 us (9%)
  other arithmetic  44.1 us (6%)
  local copies, waits for them, and re-layouts  26.5 us (4%)
  between operations  15.1 us (2%)
    all_gather x3, waiting for transfers between devices, gather_rows(): lax.all_gather(weight, 'fsdp', axis=0, tiled=False, axis_index_groups=z_g...  131 us
    ppermute x12, waiting for transfers between devices, reduce_end(): total = total + wide(lax.ppermute(leaving, 'fsdp', pairs))  105 us
    ppermute x4, waiting for transfers between devices, reduce_end(): crossed = lax.ppermute(away, 'fsdp', swapped_pairs(count, 2))  81.7 us
    ppermute x3, waiting for transfers between devices, gather_rows(): across = lax.ppermute(own, 'fsdp', swapped_pairs(count, 2))  36.7 us
    pallas_call x3, Pallas kernels, gather_rows(): pl.pallas_call(assemble_kernel, grid_spec=pltpu.PrefetchScalarGridSpec(nu...  36.2 us
    dot_general x5, matrix products, compared_with(): lax.dot_general(earlier_value, latter, (((1,), (1,)), ((), ())), preferre...  32.7 us
    convert_element_type x14, other arithmetic, low(): return tensor.astype(jnp.bfloat16)  26.2 us
    dot_general x5, matrix products, outer_sum(): lax.dot_general(earlier_value, latter, (((0,), (0,)), ((), ())), preferre...  19.7 us
  transfers between devices with their start and end apart: 55, of which 22 were waited for; matrix products, arithmetic and copies ran while one was open for 14% of the time, Pallas kernels for 8%

profile of v2, /device:TPU:12, one launch (start us, length us, event | category | flops | bytes accessed | tf_op | source)
XLA Modules:
  0.0 688.3 jit_solution(12625554603544282079)
XLA Ops:
  12.0 43.6 %all-gather.7.cloned.1.call-done = bf16[256,4096]{1,0:T(8,128)(2,1)} async-done(((bf16[64,4096]{1,0:T(8,128)(2,1)}), bf16[256,4096]{1,0:T(8,128)(2,1)}) %all-gather.7.cloned.1.call-update) | async-done | bytes 2097168 | tf_op jit(solution)/shard_map/all_gather | solution.py:558
  58.4 6.1 all-to-all-start
  67.7 40.8 %all-gather.9.cloned.1.call-done = bf16[256,4096]{1,0:T(8,128)(2,1)} async-done(((bf16[64,4096]{1,0:T(8,128)(2,1)}), bf16[256,4096]{1,0:T(8,128)(2,1)}) %all-gather.9.cloned.1.call-update) | async-done | bytes 2097168 | tf_op jit(solution)/shard_map/all_gather | solution.py:558
  109.9 46.6 %all-gather.11.cloned.1.call-done = bf16[1024,1024]{1,0:T(8,128)(2,1)} async-done(((bf16[256,1024]{1,0:T(8,128)(2,1)}), bf16[1024,1024]{1,0:T(8,128)(2,1)}) %all-gather.11.cloned.1.call-update) | async-done | bytes 2097168 | tf_op jit(solution)/shard_map/all_gather | solution.py:558
  167.2 36.7 %collective-permute-done.9.p10 = bf16[4,256,1024]{2,1,0:T(8,128)(2,1)} collective-permute-done((bf16[4,256,1024]{2,1,0:T(8,128)(2,1)}, bf16[4,256,1024]{2,1,0:T(8,128)(2,1)}, u32[]{:S(2)}, u32[]{:S(2)}) %collective-permute-start.9) | collective-permute-done | bytes 2097184 | tf_op jit(solution)/shard_map/ppermute | solution.py:559
  203.9 12.9 %assemble.3 = (bf16[4,4,64,3072]{3,2,1,0:T(8,128)(2,1)}, bf16[4,4,64,1024]{3,2,1,0:T(8,128)(2,1)S(1)}) custom-call(s32[4]{0:T(128)S(1)} %iota_xor_fusion.place_ref, bf16[4,64,4096]{2,1,0:T(8,128)(2,1)} %bitcast.9.p00, bf16[4,64,4096]{2,1,0:T(8,128)(2,1)} %collective-permute-done.1.p01, bf16[4,64,4096]{2,1,0:T(8,128)(2,1)} %collective-permute-done.2.p10, ...), custom_call_target="tpu_custom_call" | custom-call | bytes 16777216 | tf_op jit(solution)/shard_map/assemble/pallas_call | solution.py:574
  216.9 7.2 %add_convert_fusion.q_ref.k_ref.v_ref = bf16[512,3072]{1,0:T(8,128)(2,1)S(1)} fusion(bf16[1024,3072]{1,0:T(8,128)(2,1)} %bitcast.300, f32[3072]{0:T(1024)S(1)} %bitcast.288, f32[1024]{0:T(1024)S(1)} %bitcast.291, f32[1024]{0:T(1024)S(1)} %bitcast.278, f32[512]{0:T(512)S(1)} %add_rsqrt_fusion.1, f32[512]{0:T(512)S(1)} %broadcast_multiply_fusion.5, ...), kind=kOutput, calls=%fused_computation.15 | convolution fusion | flops 3229089792 | bytes 10510336 | tf_op jit(solution)/shard_map/dot_general | solution.py:759
  224.0 13.0 %attend.1 = (bf16[512,1024]{1,0:T(8,128)(2,1)S(1)}, f32[8,2,512]{2,1,0:T(2,128)S(1)}) custom-call(bf16[512,3072]{1,0:T(8,128)(2,1)S(1)} %add_convert_fusion.q_ref.k_ref.v_ref, bf16[512,3072]{1,0:T(8,128)(2,1)S(1)} %add_convert_fusion.q_ref.k_ref.v_ref, bf16[512,3072]{1,0:T(8,128)(2,1)S(1)} %add_convert_fusion.q_ref.k_ref.v_ref), custom_call_target="tpu_custom_call" | custom-call | flops 4294967296 | bytes 4718592 | tf_op jit(solution)/shard_map/attend/pallas_call | solution.py:489
  240.1 11.7 %assemble.4 = bf16[4,4,64,4096]{3,2,1,0:T(8,128)(2,1)} custom-call(s32[4]{0:T(128)S(1)} %iota_xor_fusion.place_ref, bf16[4,64,4096]{2,1,0:T(8,128)(2,1)S(1)} %bitcast.250, bf16[4,64,4096]{2,1,0:T(8,128)(2,1)S(1)} %collective-permute-done.4.p01, bf16[4,64,4096]{2,1,0:T(8,128)(2,1)} %collective-permute-done.5.p10, bf16[4,64,4096]{2,1,0:T(8,128)(2,1)} %collective-permute-done.6.p11), custom_call_target="tpu_custom_call" | custom-call | bytes 16777216 | tf_op jit(solution)/shard_map/assemble/pallas_call | solution.py:574
  251.7 12.9 %multiply_convert_fusion = (bf16[512,4096]{1,0:T(8,128)(2,1)}, f32[512,4096]{1,0:T(8,128)}) fusion(f32[4096]{0:T(1024)S(1)} %bitcast.286, bf16[1024,4096]{1,0:T(8,128)(2,1)} %bitcast.264, f32[512,1024]{1,0:T(8,128)S(1)} %get-tuple-element.59, f32[1024]{0:T(1024)S(1)} %bitcast.297, f32[1024]{0:T(1024)S(1)} %bitcast.293, f32[512]{0:T(512)S(1)} %add_rsqrt_fusion, ...), kind=kOutput, calls=%fused_computation.11 | convolution fusion | flops 4318560256 | bytes 23097344 | tf_op jit(solution)/shard_map/dot_general | solution.py:765
  264.6 7.4 %convolution_convert_fusion.1 = bf16[4096,1024]{1,0:T(8,128)(2,1)S(1)} fusion(bf16[512,4096]{1,0:T(8,128)(2,1)} %get-tuple-element.33, bf16[512,1024]{1,0:T(8,128)(2,1)S(1)} %copy-done.14), kind=kOutput, calls=%fused_computation.13 | convolution fusion | flops 4299161600 | bytes 13631488 | tf_op jit(solution)/shard_map/dot_general | solution.py:46
  276.6 11.6 %assemble.5 = bf16[4,4,256,1024]{3,2,1,0:T(8,128)(2,1)} custom-call(s32[4]{0:T(128)S(1)} %iota_xor_fusion.place_ref, bf16[4,256,1024]{2,1,0:T(8,128)(2,1)S(1)} %bitcast.253, bf16[4,256,1024]{2,1,0:T(8,128)(2,1)S(1)} %collective-permute-done.8.p01, bf16[4,256,1024]{2,1,0:T(8,128)(2,1)} %collective-permute-done.9.p10, ...), custom_call_target="tpu_custom_call" | custom-call | bytes 16777216 | tf_op jit(solution)/shard_map/assemble/pallas_call | solution.py:574
  288.2 14.2 %fusion.3 = bf16[512,4096]{1,0:T(8,128)(2,1)S(1)} fusion(f32[512,4096]{1,0:T(8,128)} %get-tuple-element.132, f32[4096]{0:T(1024)S(1)} %bitcast.287, bf16[512,1024]{1,0:T(8,128)(2,1)S(1)} %copy-done.14, bf16[4096,1024]{1,0:T(8,128)(2,1)} %bitcast.262), kind=kOutput, calls=%fused_computation.7 | convolution fusion | flops 4347396096 | bytes 22036480 | tf_op jit(solution)/shard_map/dot_general | solution.py:52
  302.5 5.4 convolution_convert_fusion
  312.4 9.7 %multiply_reduce_fusion = (bf16[1024]{0:T(1024)(128)(2,1)S(1)}, f32[512]{0:T(512)S(1)}, f32[512]{0:T(512)S(1)}, bf16[1024]{0:T(1024)(128)(2,1)S(1)}, f32[512,1024]{1,0:T(8,128)}) fusion(f32[512,1024]{1,0:T(8,128)S(1)} %copy-done.19, f32[512]{0:T(512)S(1)} %add_rsqrt_fusion, f32[512]{0:T(512)S(1)} %broadcast_multiply_fusion.4, f32[1024]{0:T(1024)S(1)} %bitcast.295, ...), kind=kOutput, calls=%fused_computation.56 | convolution fusion | flops 4299682816 | bytes 16793600 | tf_op jit(solution)/shard_map/dot_general | solution.py:52
  322.1 12.7 %fusion.24 = (bf16[1024]{0:T(1024)(128)(2,1)S(1)}, bf16[512,1024]{1,0:T(8,128)(2,1)}, bf16[1024]{0:T(1024)(128)(2,1)S(1)}, f32[512,1024]{1,0:T(8,128)S(1)}) fusion(f32[1024]{0:T(1024)S(1)} %add.482, bf16[256,1024]{1,0:T(8,128)(2,1)} %collective-permute-done.7, bf16[256,1024]{1,0:T(8,128)(2,1)S(1)} %copy-done.20, f32[512,1024]{1,0:T(8,128)} %copy-done.18, ...), kind=kOutput, calls=%fused_computation.50 | convolution fusion | flops 4305975296 | bytes 23097344 | tf_op jit(solution)/shard_map/dot_general | solution.py:774
  341.1 17.2 %attend_back.1 = (bf16[512,1024]{1,0:T(8,128)(2,1)S(1)}, bf16[512,1024]{1,0:T(8,128)(2,1)S(1)}, bf16[512,1024]{1,0:T(8,128)(2,1)S(1)}) custom-call(bf16[512,3072]{1,0:T(8,128)(2,1)} %copy-done.3, bf16[512,3072]{1,0:T(8,128)(2,1)} %copy-done.3, bf16[512,3072]{1,0:T(8,128)(2,1)} %copy-done.3, bf16[512,1024]{1,0:T(8,128)(2,1)S(1)} %convolution_convert_fusion.4.do_ref, ...), custom_call_target="tpu_custom_call" | custom-call | flops 10737418240 | bytes 9437184 | tf_op jit(solution)/shard_map/attend_back/pallas_call | solution.py:517
  359.4 4.0 convolution_convert_fusion.2
  368.4 5.9 all-to-all-start.1
  374.3 7.2 %fusion.21 = (bf16[1024]{0:T(1024)(128)(2,1)S(1)}, f32[512]{0:T(512)S(1)}, f32[512]{0:T(512)S(1)}, bf16[1024]{0:T(1024)(128)(2,1)S(1)}, f32[512,1024]{1,0:T(8,128)S(1)}) fusion(f32[512]{0:T(512)S(1)} %add_rsqrt_fusion.1, f32[512]{0:T(512)S(1)} %broadcast_multiply_fusion.5, bf16[256,1024]{1,0:T(8,128)(2,1)S(1)} %copy-done.11, ...), kind=kOutput, calls=%fused_computation.47 | convolution fusion | flops 3228038144 | bytes 12599296 | tf_op jit(solution)/shard_map/dot_general | solution.py:52
  417.8 7.0 %fusion.6 = (bf16[4,256,1024]{2,1,0:T(8,128)(2,1)}, f32[4,256,1024]{2,1,0:T(8,128)S(1)}) fusion(bf16[4,2,256,1024]{3,2,0,1:T(8,128)(2,1)} %collective-permute-done.44, s32[]{:T(128)S(6)} %select_n.435, bf16[4,2,2,256,1024]{4,3,2,1,0:T(8,128)(2,1)} %bitcast.257, s32[]{:T(128)S(6)} %select_n.436, s32[]{:T(128)S(6)} %select_n.433, s32[]{:T(128)S(6)} %select_n.430, ...), kind=kLoop, calls=%fused_computation.18 | loop fusion | flops 7340032 | bytes 14680084 | tf_op jit(solution)/shard_map/convert_element_type | solution.py:633
  425.7 5.5 fusion.7
  435.4 10.2 %collective-permute-done.11 = bf16[256,1024]{1,0:T(8,128)(2,1)S(1)} collective-permute-done((bf16[256,1024]{1,0:T(8,128)(2,1)}, bf16[256,1024]{1,0:T(8,128)(2,1)S(1)}, u32[]{:S(2)}, u32[]{:S(2)}) %collective-permute-start.11) | collective-permute-done | bytes 524320 | tf_op jit(solution)/shard_map/ppermute | solution.py:703
  468.5 7.6 %collective-permute-done.45 = bf16[4,256,1024]{2,1,0:T(8,128)(2,1)} collective-permute-done((bf16[4,256,1024]{2,1,0:T(8,128)(2,1)}, bf16[4,256,1024]{2,1,0:T(8,128)(2,1)}, u32[]{:S(2)}, u32[]{:S(2)}) %collective-permute-start.45) | collective-permute-done | bytes 2097184 | tf_op jit(solution)/shard_map/ppermute | solution.py:660
  478.9 74.0 %collective-permute-done.26 = bf16[4,64,3072]{2,1,0:T(8,128)(2,1)S(1)} collective-permute-done((bf16[4,64,3072]{2,1,0:T(8,128)(2,1)S(1)}, bf16[4,64,3072]{2,1,0:T(8,128)(2,1)S(1)}, u32[]{:S(2)}, u32[]{:S(2)}) %collective-permute-start.26) | collective-permute-done | bytes 1572896 | tf_op jit(solution)/shard_map/ppermute | solution.py:660
  558.7 43.6 %collective-permute-done.27 = bf16[64,3072]{1,0:T(8,128)(2,1)S(1)} collective-permute-done((bf16[64,3072]{1,0:T(8,128)(2,1)S(1)}, bf16[64,3072]{1,0:T(8,128)(2,1)S(1)}, u32[]{:S(2)}, u32[]{:S(2)}) %collective-permute-start.27) | collective-permute-done | bytes 393248 | tf_op jit(solution)/shard_map/ppermute | solution.py:667
  602.2 8.5 %collective-permute-done.28 = bf16[64,3072]{1,0:T(8,128)(2,1)S(1)} collective-permute-done((bf16[64,3072]{1,0:T(8,128)(2,1)S(1)}, bf16[64,3072]{1,0:T(8,128)(2,1)S(1)}, u32[]{:S(2)}, u32[]{:S(2)}) %collective-permute-start.28) | collective-permute-done | bytes 393248 | tf_op jit(solution)/shard_map/ppermute | solution.py:667
  610.7 3.4 collective-permute-start.41
  616.4 28.0 %collective-permute-done.47 = bf16[256,1024]{1,0:T(8,128)(2,1)S(1)} collective-permute-done((bf16[256,1024]{1,0:T(8,128)(2,1)S(1)}, bf16[256,1024]{1,0:T(8,128)(2,1)S(1)}, u32[]{:S(2)}, u32[]{:S(2)}) %collective-permute-start.47) | collective-permute-done | bytes 524320 | tf_op jit(solution)/shard_map/ppermute | solution.py:667
  648.0 7.7 %collective-permute-done.40 = bf16[64,4096]{1,0:T(8,128)(2,1)S(1)} collective-permute-done((bf16[64,4096]{1,0:T(8,128)(2,1)S(1)}, bf16[64,4096]{1,0:T(8,128)(2,1)S(1)}, u32[]{:S(2)}, u32[]{:S(2)}) %collective-permute-start.40) | collective-permute-done | bytes 524320 | tf_op jit(solution)/shard_map/ppermute | solution.py:667
  655.7 8.9 %collective-permute-done.41 = bf16[64,4096]{1,0:T(8,128)(2,1)S(1)} collective-permute-done((bf16[64,4096]{1,0:T(8,128)(2,1)S(1)}, bf16[64,4096]{1,0:T(8,128)(2,1)S(1)}, u32[]{:S(2)}, u32[]{:S(2)}) %collective-permute-start.41) | collective-permute-done | bytes 524320 | tf_op jit(solution)/shard_map/ppermute | solution.py:667
  669.0 11.2 %collective-permute-done.43 = bf16[64,4096]{1,0:T(8,128)(2,1)S(1)} collective-permute-done((bf16[64,4096]{1,0:T(8,128)(2,1)S(1)}, bf16[64,4096]{1,0:T(8,128)(2,1)S(1)}, u32[]{:S(2)}, u32[]{:S(2)}) %collective-permute-start.43) | collective-permute-done | bytes 524320 | tf_op jit(solution)/shard_map/ppermute | solution.py:669
  (289 shorter events, 130.9 us)
Async XLA Ops:
  7.2 48.5 %all-gather.7.cloned.1.call-start = ((), (), s32[]{:S(2)}) async-start(), calls=%async_computation.2 | async-start | bytes 2621440 | tf_op jit(solution)/shard_map/all_gather | solution.py:558
  9.4 99.1 %all-gather.9.cloned.1.call-start = ((), (), s32[]{:S(2)}) async-start(), calls=%async_computation.3 | async-start | bytes 2621440 | tf_op jit(solution)/shard_map/all_gather | solution.py:558
  10.1 146.4 %all-gather.11.cloned.1.call-start = ((), (), s32[]{:S(2)}) async-start(), calls=%async_computation.4 | async-start | bytes 2621440 | tf_op jit(solution)/shard_map/all_gather | solution.py:558
  10.3 57.1 %collective-permute-start = (bf16[256,1024]{1,0:T(8,128)(2,1)S(1)}, bf16[256,1024]{1,0:T(8,128)(2,1)S(1)}, u32[]{:S(2)}, u32[]{:S(2)}) collective-permute-start(bf16[256,1024]{1,0:T(8,128)(2,1)S(1)} %get-tuple-element.91), channel_id=1, source_target_pairs={{0,16},{16,0},{1,17},{17,1},{2,18},{18,2},{3,19},{19,3},{4,20},{20... | collective-permute-start | bytes 1572872 | tf_op jit(solution)/shard_map/ppermute | solution.py:700
  55.7 102.3 %collective-permute-start.2 = (bf16[4,64,4096]{2,1,0:T(8,128)(2,1)}, bf16[4,64,4096]{2,1,0:T(8,128)(2,1)}, u32[]{:S(2)}, u32[]{:S(2)}) collective-permute-start(bf16[4,64,4096]{2,1,0:T(8,128)(2,1)} %bitcast.9.p00), channel_id=1, source_target_pairs={{0,2},{1,3},{2,0},{3,1},{4,6},{5,7},{6,4},{7,5},{8,10},{9,11},{10,... | collective-permute-start | bytes 6291464 | tf_op jit(solution)/shard_map/ppermute | solution.py:559
  58.4 101.1 %all-to-all-start = ((f32[16,1,6656]{2,1,0:T(1,128)}), f32[16,1,6656]{2,1,0:T(1,128)}, u32[]{:S(2)}, u32[]{:S(2)}) async-start(f32[16,1,6656]{2,1,0:T(1,128)} %copy.82), calls=%async_computation | async-start | bytes 851968 | tf_op jit(solution)/shard_map/all_to_all | solution.py:735
  66.8 96.9 %collective-permute-start.7 = (bf16[256,1024]{1,0:T(8,128)(2,1)}, bf16[256,1024]{1,0:T(8,128)(2,1)}, u32[]{:S(2)}, u32[]{:S(2)}) collective-permute-start(bf16[256,1024]{1,0:T(8,128)(2,1)} %get-tuple-element.89), channel_id=1, source_target_pairs={{0,16},{16,0},{1,17},{17,1},{2,18},{18,2},{3,19},{19,3},{4,20},{20... | collective-permute-start | bytes 1572872 | tf_op jit(solution)/shard_map/ppermute | solution.py:700
  67.6 99.1 %collective-permute-start.1 = (bf16[4,64,4096]{2,1,0:T(8,128)(2,1)}, bf16[4,64,4096]{2,1,0:T(8,128)(2,1)}, u32[]{:S(2)}, u32[]{:S(2)}) collective-permute-start(bf16[4,64,4096]{2,1,0:T(8,128)(2,1)} %bitcast.9.p00), channel_id=1, source_target_pairs={{0,1},{1,0},{2,3},{3,2},{4,5},{5,4},{6,7},{7,6},{8,9},{9,8},{10,11... | collective-permute-start | bytes 6291464 | tf_op jit(solution)/shard_map/ppermute | solution.py:560
  108.4 58.4 %collective-permute-start.5 = (bf16[4,64,4096]{2,1,0:T(8,128)(2,1)}, bf16[4,64,4096]{2,1,0:T(8,128)(2,1)}, u32[]{:S(2)}, u32[]{:S(2)}) collective-permute-start(bf16[4,64,4096]{2,1,0:T(8,128)(2,1)} %bitcast.248), channel_id=1, source_target_pairs={{0,2},{1,3},{2,0},{3,1},{4,6},{5,7},{6,4},{7,5},{8,10},{9,11},{10,... | collective-permute-start | bytes 6291464 | tf_op jit(solution)/shard_map/ppermute | solution.py:559
  156.5 47.4 %collective-permute-start.9 = (bf16[4,256,1024]{2,1,0:T(8,128)(2,1)}, bf16[4,256,1024]{2,1,0:T(8,128)(2,1)}, u32[]{:S(2)}, u32[]{:S(2)}) collective-permute-start(bf16[4,256,1024]{2,1,0:T(8,128)(2,1)} %bitcast.251), channel_id=1, source_target_pairs={{0,2},{1,3},{2,0},{3,1},{4,6},{5,7},{6,4},{7,5},{8,10},{9,11},{10,... | collective-permute-start | bytes 6291464 | tf_op jit(solution)/shard_map/ppermute | solution.py:559
  158.0 46.0 %collective-permute-start.3 = (bf16[4,64,4096]{2,1,0:T(8,128)(2,1)}, bf16[4,64,4096]{2,1,0:T(8,128)(2,1)}, u32[]{:S(2)}, u32[]{:S(2)}) collective-permute-start(bf16[4,64,4096]{2,1,0:T(8,128)(2,1)} %collective-permute-done.2.p10), channel_id=1, source_target_pairs={{0,1},{1,0},{2,3},{3,2},{4,5},{5,4},{6,7},{7,6},{8,9},{9,8},{10,11... | collective-permute-start | bytes 6291464 | tf_op jit(solution)/shard_map/ppermute | solution.py:561
  166.1 73.9 %collective-permute-start.4 = (bf16[4,64,4096]{2,1,0:T(8,128)(2,1)S(1)}, bf16[4,64,4096]{2,1,0:T(8,128)(2,1)S(1)}, u32[]{:S(2)}, u32[]{:S(2)}) collective-permute-start(bf16[4,64,4096]{2,1,0:T(8,128)(2,1)S(1)} %bitcast.249), channel_id=1, source_target_pairs={{0,1},{1,0},{2,3},{3,2},{4,5},{5,4},{6,7},{7,6},{8,9},{9,8},{10,11... | collective-permute-start | bytes 6291464 | tf_op jit(solution)/shard_map/ppermute | solution.py:560
  166.7 109.9 %collective-permute-start.8 = (bf16[4,256,1024]{2,1,0:T(8,128)(2,1)S(1)}, bf16[4,256,1024]{2,1,0:T(8,128)(2,1)S(1)}, u32[]{:S(2)}, u32[]{:S(2)}) collective-permute-start(bf16[4,256,1024]{2,1,0:T(8,128)(2,1)S(1)} %bitcast.252), channel_id=1, source_target_pairs={{0,1},{1,0},{2,3},{3,2},{4,5},{5,4},{6,7},{7,6},{8,9},{9,8},{10,11... | collective-permute-start | bytes 6291464 | tf_op jit(solution)/shard_map/ppermute | solution.py:560
  166.8 73.3 %collective-permute-start.6 = (bf16[4,64,4096]{2,1,0:T(8,128)(2,1)}, bf16[4,64,4096]{2,1,0:T(8,128)(2,1)}, u32[]{:S(2)}, u32[]{:S(2)}) collective-permute-start(bf16[4,64,4096]{2,1,0:T(8,128)(2,1)} %collective-permute-done.5.p10), channel_id=1, source_target_pairs={{0,1},{1,0},{2,3},{3,2},{4,5},{5,4},{6,7},{7,6},{8,9},{9,8},{10,11... | collective-permute-start | bytes 6291464 | tf_op jit(solution)/shard_map/ppermute | solution.py:561
  203.9 72.7 %collective-permute-start.10 = (bf16[4,256,1024]{2,1,0:T(8,128)(2,1)}, bf16[4,256,1024]{2,1,0:T(8,128)(2,1)}, u32[]{:S(2)}, u32[]{:S(2)}) collective-permute-start(bf16[4,256,1024]{2,1,0:T(8,128)(2,1)} %collective-permute-done.9.p10), channel_id=1, source_target_pairs={{0,1},{1,0},{2,3},{3,2},{4,5},{5,4},{6,7},{7,6},{8,9},{9,8},{10,11... | collective-permute-start | bytes 6291464 | tf_op jit(solution)/shard_map/ppermute | solution.py:561
  340.4 75.8 %collective-permute-start.44 = (bf16[4,2,256,1024]{3,2,0,1:T(8,128)(2,1)}, bf16[4,2,256,1024]{3,2,0,1:T(8,128)(2,1)}, u32[]{:S(2)}, u32[]{:S(2)}) collective-permute-start(bf16[4,2,256,1024]{3,2,0,1:T(8,128)(2,1)} %copy_bitcast_fusion.1), channel_id=1, source_target_pairs={{0,1},{1,0},{2,3},{3,2},{4,5},{5,4},{6,7},{7,6},{8,9},{9,8},{10,11... | collective-permute-start | bytes 12582920 | tf_op jit(solution)/shard_map/ppermute | solution.py:658
  341.0 83.7 %collective-permute-start.38 = (bf16[4,2,64,4096]{3,2,0,1:T(8,128)(2,1)}, bf16[4,2,64,4096]{3,2,0,1:T(8,128)(2,1)}, u32[]{:S(2)}, u32[]{:S(2)}) collective-permute-start(bf16[4,2,64,4096]{3,2,0,1:T(8,128)(2,1)} %copy_bitcast_fusion), channel_id=1, source_target_pairs={{0,1},{1,0},{2,3},{3,2},{4,5},{5,4},{6,7},{7,6},{8,9},{9,8},{10,11... | collective-permute-start | bytes 12582920 | tf_op jit(solution)/shard_map/ppermute | solution.py:658
  409.2 40.4 %collective-permute-start.12 = (f32[256,1024]{1,0:T(8,128)}, f32[256,1024]{1,0:T(8,128)}, u32[]{:S(2)}, u32[]{:S(2)}) collective-permute-start(f32[256,1024]{1,0:T(8,128)} %slice.127), channel_id=1, source_target_pairs={{0,16},{16,0},{1,17},{17,1},{2,18},{18,2},{3,19},{19,3},{4,20},{20... | collective-permute-start | bytes 3145736 | tf_op jit(solution)/shard_map/ppermute | solution.py:703
  413.3 32.3 %collective-permute-start.11 = (bf16[256,1024]{1,0:T(8,128)(2,1)}, bf16[256,1024]{1,0:T(8,128)(2,1)S(1)}, u32[]{:S(2)}, u32[]{:S(2)}) collective-permute-start(bf16[256,1024]{1,0:T(8,128)(2,1)} %slice.125), channel_id=1, source_target_pairs={{0,16},{16,0},{1,17},{17,1},{2,18},{18,2},{3,19},{19,3},{4,20},{20... | collective-permute-start | bytes 1572872 | tf_op jit(solution)/shard_map/ppermute | solution.py:703
  416.2 31.1 %collective-permute-start.33 = (bf16[4,64,1024]{2,1,0:T(8,128)(2,1)S(1)}, bf16[4,64,1024]{2,1,0:T(8,128)(2,1)}, u32[]{:S(2)}, u32[]{:S(2)}) collective-permute-start(bf16[4,64,1024]{2,1,0:T(8,128)(2,1)S(1)} %get-tuple-element.75), channel_id=1, source_target_pairs={{0,2},{1,3},{2,0},{3,1},{4,6},{5,7},{6,4},{7,5},{8,10},{9,11},{10,... | collective-permute-start | bytes 1572872 | tf_op jit(solution)/shard_map/ppermute | solution.py:660
  424.7 51.4 %collective-permute-start.45 = (bf16[4,256,1024]{2,1,0:T(8,128)(2,1)}, bf16[4,256,1024]{2,1,0:T(8,128)(2,1)}, u32[]{:S(2)}, u32[]{:S(2)}) collective-permute-start(bf16[4,256,1024]{2,1,0:T(8,128)(2,1)} %get-tuple-element.60), channel_id=1, source_target_pairs={{0,2},{1,3},{2,0},{3,1},{4,6},{5,7},{6,4},{7,5},{8,10},{9,11},{10,... | collective-permute-start | bytes 6291464 | tf_op jit(solution)/shard_map/ppermute | solution.py:660
  431.2 125.3 %collective-permute-start.39 = (bf16[4,64,4096]{2,1,0:T(8,128)(2,1)}, bf16[4,64,4096]{2,1,0:T(8,128)(2,1)S(1)}, u32[]{:S(2)}, u32[]{:S(2)}) collective-permute-start(bf16[4,64,4096]{2,1,0:T(8,128)(2,1)} %get-tuple-element.62), channel_id=1, source_target_pairs={{0,2},{1,3},{2,0},{3,1},{4,6},{5,7},{6,4},{7,5},{8,10},{9,11},{10,... | collective-permute-start | bytes 6291464 | tf_op jit(solution)/shard_map/ppermute | solution.py:660
  445.6 107.4 %collective-permute-start.26 = (bf16[4,64,3072]{2,1,0:T(8,128)(2,1)S(1)}, bf16[4,64,3072]{2,1,0:T(8,128)(2,1)S(1)}, u32[]{:S(2)}, u32[]{:S(2)}) collective-permute-start(bf16[4,64,3072]{2,1,0:T(8,128)(2,1)S(1)} %get-tuple-element.64), channel_id=1, source_target_pairs={{0,2},{1,3},{2,0},{3,1},{4,6},{5,7},{6,4},{7,5},{8,10},{9,11},{10,... | collective-permute-start | bytes 4718600 | tf_op jit(solution)/shard_map/ppermute | solution.py:660
  478.0 136.2 %collective-permute-start.46 = (bf16[256,1024]{1,0:T(8,128)(2,1)S(1)}, bf16[256,1024]{1,0:T(8,128)(2,1)S(1)}, u32[]{:S(2)}, u32[]{:S(2)}) collective-permute-start(bf16[256,1024]{1,0:T(8,128)(2,1)S(1)} %get-tuple-element.66), channel_id=1, source_target_pairs={{0,4},{1,5},{2,6},{3,7},{4,8},{5,9},{6,10},{7,11},{8,12},{9,13},{1... | collective-permute-start | bytes 1572872 | tf_op jit(solution)/shard_map/ppermute | solution.py:667
  553.3 49.0 %collective-permute-start.27 = (bf16[64,3072]{1,0:T(8,128)(2,1)S(1)}, bf16[64,3072]{1,0:T(8,128)(2,1)S(1)}, u32[]{:S(2)}, u32[]{:S(2)}) collective-permute-start(bf16[64,3072]{1,0:T(8,128)(2,1)S(1)} %get-tuple-element.72), channel_id=1, source_target_pairs={{0,4},{1,5},{2,6},{3,7},{4,8},{5,9},{6,10},{7,11},{8,12},{9,13},{1... | collective-permute-start | bytes 1179656 | tf_op jit(solution)/shard_map/ppermute | solution.py:667
  553.4 57.4 %collective-permute-start.28 = (bf16[64,3072]{1,0:T(8,128)(2,1)S(1)}, bf16[64,3072]{1,0:T(8,128)(2,1)S(1)}, u32[]{:S(2)}, u32[]{:S(2)}) collective-permute-start(bf16[64,3072]{1,0:T(8,128)(2,1)S(1)} %get-tuple-element.74), channel_id=1, source_target_pairs={{0,8},{1,9},{2,10},{3,11},{4,12},{5,13},{6,14},{7,15},{8,0},{9,1},... | collective-permute-start | bytes 1179656 | tf_op jit(solution)/shard_map/ppermute | solution.py:667
  555.4 55.4 %collective-permute-start.29 = (bf16[64,3072]{1,0:T(8,128)(2,1)S(1)}, bf16[64,3072]{1,0:T(8,128)(2,1)S(1)}, u32[]{:S(2)}, u32[]{:S(2)}) collective-permute-start(bf16[64,3072]{1,0:T(8,128)(2,1)S(1)} %get-tuple-element.73), channel_id=1, source_target_pairs={{0,12},{1,13},{2,14},{3,15},{4,0},{5,1},{6,2},{7,3},{8,4},{9,5},{1... | collective-permute-start | bytes 1179656 | tf_op jit(solution)/shard_map/ppermute | solution.py:667
  556.5 87.9 %collective-permute-start.47 = (bf16[256,1024]{1,0:T(8,128)(2,1)S(1)}, bf16[256,1024]{1,0:T(8,128)(2,1)S(1)}, u32[]{:S(2)}, u32[]{:S(2)}) collective-permute-start(bf16[256,1024]{1,0:T(8,128)(2,1)S(1)} %get-tuple-element.68), channel_id=1, source_target_pairs={{0,8},{1,9},{2,10},{3,11},{4,12},{5,13},{6,14},{7,15},{8,0},{9,1},... | collective-permute-start | bytes 1572872 | tf_op jit(solution)/shard_map/ppermute | solution.py:667
  602.2 42.7 %collective-permute-start.48 = (bf16[256,1024]{1,0:T(8,128)(2,1)S(1)}, bf16[256,1024]{1,0:T(8,128)(2,1)S(1)}, u32[]{:S(2)}, u32[]{:S(2)}) collective-permute-start(bf16[256,1024]{1,0:T(8,128)(2,1)S(1)} %get-tuple-element.67), channel_id=1, source_target_pairs={{0,12},{1,13},{2,14},{3,15},{4,0},{5,1},{6,2},{7,3},{8,4},{9,5},{1... | collective-permute-start | bytes 1572872 | tf_op jit(solution)/shard_map/ppermute | solution.py:667
  610.7 44.9 %collective-permute-start.40 = (bf16[64,4096]{1,0:T(8,128)(2,1)S(1)}, bf16[64,4096]{1,0:T(8,128)(2,1)S(1)}, u32[]{:S(2)}, u32[]{:S(2)}) collective-permute-start(bf16[64,4096]{1,0:T(8,128)(2,1)S(1)} %get-tuple-element.69), channel_id=1, source_target_pairs={{0,4},{1,5},{2,6},{3,7},{4,8},{5,9},{6,10},{7,11},{8,12},{9,13},{1... | collective-permute-start | bytes 1572872 | tf_op jit(solution)/shard_map/ppermute | solution.py:667
  610.7 53.8 %collective-permute-start.41 = (bf16[64,4096]{1,0:T(8,128)(2,1)S(1)}, bf16[64,4096]{1,0:T(8,128)(2,1)S(1)}, u32[]{:S(2)}, u32[]{:S(2)}) collective-permute-start(bf16[64,4096]{1,0:T(8,128)(2,1)S(1)} %get-tuple-element.71), channel_id=1, source_target_pairs={{0,8},{1,9},{2,10},{3,11},{4,12},{5,13},{6,14},{7,15},{8,0},{9,1},... | collective-permute-start | bytes 1572872 | tf_op jit(solution)/shard_map/ppermute | solution.py:667
  614.2 51.9 %collective-permute-start.42 = (bf16[64,4096]{1,0:T(8,128)(2,1)S(1)}, bf16[64,4096]{1,0:T(8,128)(2,1)S(1)}, u32[]{:S(2)}, u32[]{:S(2)}) collective-permute-start(bf16[64,4096]{1,0:T(8,128)(2,1)S(1)} %get-tuple-element.70), channel_id=1, source_target_pairs={{0,12},{1,13},{2,14},{3,15},{4,0},{5,1},{6,2},{7,3},{8,4},{9,5},{1... | collective-permute-start | bytes 1572872 | tf_op jit(solution)/shard_map/ppermute | solution.py:667
  (61 other events, 565.6 us)
Sparse Core Ops, SparseCore 0:
  10.2 45.4 all-gather.6
  57.2 51.1 all-gather.8
  110.0 46.4 all-gather.10

commit v3 on v2

--- a/solution.py
+++ b/solution.py
@@ -549,16 +549,22 @@
                 begin = end
 
 
-def gather_rows(weight, *widths):
-    rows, columns = weight.shape
-    count = lax.axis_size("fsdp")
-    depth = count // 4
+def gather_z(weight):
+    z_groups = [
+        [base + 4 * step for step in range(lax.axis_size("fsdp") // 4)] for base in range(4)
+    ]
+    return lax.all_gather(weight, "fsdp", axis=0, tiled=False, axis_index_groups=z_groups)
+
+
+def flip(tensor, bit):
+    return lax.ppermute(tensor, "fsdp", swapped_pairs(lax.axis_size("fsdp"), bit))
+
+
+def assemble(own, own_core, across, across_core, *widths):
+    depth, rows, columns = own.shape
+    count = 4 * depth
+    weight = own
     owner = lax.axis_index("fsdp")
-    z_groups = [[base + 4 * step for step in range(depth)] for base in range(4)]
-    own = lax.all_gather(weight, "fsdp", axis=0, tiled=False, axis_index_groups=z_groups)
-    across = lax.ppermute(own, "fsdp", swapped_pairs(count, 2))
-    own_core = lax.ppermute(own, "fsdp", swapped_pairs(count, 1))
-    across_core = lax.ppermute(across, "fsdp", swapped_pairs(count, 1))
     places = jnp.bitwise_xor(lax.rem(owner, 4), jnp.arange(4, dtype=jnp.int32))
 
     def piece_spec(which):
@@ -641,7 +647,7 @@
     return lax.dynamic_index_in_dim(tensor, place, axis, keepdims=False)
 
 
-def reduce_begin(partial):
+def split_core(partial):
     count = lax.axis_size("fsdp")
     core_at = lax.rem(lax.axis_index("fsdp"), 2)
     rows, columns = partial.shape
@@ -649,24 +655,42 @@
     return pick(blocks, 2, core_at), pick(blocks, 2, 1 - core_at)
 
 
-def reduce_end(kept, leaving):
-    count = lax.axis_size("fsdp")
-    depth = count // 4
-    owner = lax.axis_index("fsdp")
-    x_at = lax.rem(lax.div(owner, 2), 2)
-    z_at = lax.div(owner, 4)
-    arrived = lax.ppermute(leaving, "fsdp", swapped_pairs(count, 1))
-    away = low(wide(pick(kept, 1, 1 - x_at)) + wide(pick(arrived, 1, 1 - x_at)))
-    crossed = lax.ppermute(away, "fsdp", swapped_pairs(count, 2))
+def split_x(kept, arrived):
+    x_at = lax.rem(lax.div(lax.axis_index("fsdp"), 2), 2)
     here = wide(pick(kept, 1, x_at)) + wide(pick(arrived, 1, x_at))
-    total = pick(here, 0, z_at) + wide(pick(crossed, 0, z_at))
+    return here, low(wide(pick(kept, 1, 1 - x_at)) + wide(pick(arrived, 1, 1 - x_at)))
+
+
+def split_z(here, crossed):
+    depth = here.shape[0]
+    z_at = lax.div(lax.axis_index("fsdp"), 4)
+    leaving = []
     for shift in range(1, depth):
         target = lax.rem(z_at + shift, depth)
-        leaving = low(pick(here, 0, target) + wide(pick(crossed, 0, target)))
+        leaving.append(low(pick(here, 0, target) + wide(pick(crossed, 0, target))))
+    return pick(here, 0, z_at) + wide(pick(crossed, 0, z_at)), leaving
+
+
+def send_z(leaving):
+    count = lax.axis_size("fsdp")
+    arrived = []
+    for shift, part in enumerate(leaving, 1):
         pairs = [(place, (place + 4 * shift) % count) for place in range(count)]
-        total = total + wide(lax.ppermute(leaving, "fsdp", pairs))
-    mine = low(total)
+        arrived.append(lax.ppermute(part, "fsdp", pairs))
+    return arrived
+
+
+def sum_z(total, arrived):
+    for part in arrived:
+        total = total + wide(part)
+    return low(total)
+
+
+def sum_seq(mine):
     return wide(mine) + wide(lax.ppermute(mine, "seq", swapped_pairs(2, 1)))
+
+
+tied = lax.optimization_barrier
 
 
 def local_whole_latent(
@@ -745,40 +769,58 @@
         begin = end
     query_bias, value_bias, out_bias, up_bias, down_bias = biases
 
-    full_qkv, full_out = gather_rows(
-        jnp.concatenate([w_qkv, w_out], axis=1), w_qkv.shape[1], w_out.shape[1]
-    )
-    (full_fc1,) = gather_rows(w_fc1, w_fc1.shape[1])
-    (full_fc2,) = gather_rows(w_fc2, w_fc2.shape[1])
+    own_a = gather_z(jnp.concatenate([w_qkv, w_out], axis=1))
+    own_a, w_fc1 = tied((own_a, w_fc1))
+    own_b = gather_z(w_fc1)
+    core_a = flip(own_a, 1)
+    across_a = flip(own_a, 2)
 
     inputs_full = whole_latent(latents).astype(jnp.float32)
     grad_output = whole_latent(out_cotangent).astype(jnp.float32)
     normed_one, inverse_one = normalize_keep(inputs_full)
     entry_one = low(normed_one * (1.0 + scale_one) + shift_one)
+    entry_one, across_a = tied((entry_one, across_a))
+    across_core_a = flip(across_a, 1)
+    own_b, across_core_a, w_fc2 = tied((own_b, across_core_a, w_fc2))
+    own_c = gather_z(w_fc2)
+    core_b = flip(own_b, 1)
+    across_b = flip(own_b, 2)
+    full_qkv, full_out = assemble(
+        own_a, core_a, across_a, across_core_a, w_qkv.shape[1], w_out.shape[1]
+    )
     qkv_bias = jnp.concatenate([query_bias, jnp.zeros_like(query_bias), value_bias], axis=1)
     projected = low(jnp.dot(entry_one, full_qkv, preferred_element_type=jnp.float32) + qkv_bias)
     mixed, log_totals = attend_local(projected)
+    mixed, across_b, core_b = tied((mixed, across_b, core_b))
+    across_core_b = flip(across_b, 1)
     branch_one = jnp.dot(mixed, full_out, preferred_element_type=jnp.float32) + out_bias
     middle = inputs_full + gate_one * branch_one
     normed_two, inverse_two = normalize_keep(middle)
     entry_two = low(normed_two * (1.0 + scale_two) + shift_two)
+    entry_two, across_core_b, own_c = tied((entry_two, across_core_b, own_c))
+    core_c = flip(own_c, 1)
+    across_c = flip(own_c, 2)
+    (full_fc1,) = assemble(own_b, core_b, across_b, across_core_b, w_fc1.shape[1])
     hidden = jnp.dot(entry_two, full_fc1, preferred_element_type=jnp.float32) + up_bias
     active_full, gelu_pull = jax.vjp(gelu_tanh, hidden)
     active = low(active_full)
     grad_branch_two = low(gate_two * grad_output)
-    kept_fc2, leaving_fc2 = reduce_begin(outer_sum(active, grad_branch_two))
-    active, grad_branch_two, leaving_fc2 = lax.optimization_barrier(
-        (active, grad_branch_two, leaving_fc2)
-    )
-    sum_fc2 = reduce_end(kept_fc2, leaving_fc2)
+    kept_fc2, leaving_fc2 = split_core(outer_sum(active, grad_branch_two))
+    leaving_fc2, across_c, core_c = tied((leaving_fc2, across_c, core_c))
+    across_core_c = flip(across_c, 1)
+    arrived_fc2 = flip(leaving_fc2, 1)
+    (full_fc2,) = assemble(own_c, core_c, across_c, across_core_c, w_fc2.shape[1])
     branch_two = jnp.dot(active, full_fc2, preferred_element_type=jnp.float32) + down_bias
     result = both_halves(low(middle + gate_two * branch_two))
     grad_gate_two = jnp.sum(grad_output * branch_two, axis=0, keepdims=True)
     grad_active = compared_with(grad_branch_two, full_fc2)
     grad_hidden = low(gelu_pull(grad_active)[0])
-    kept_fc1, leaving_fc1 = reduce_begin(outer_sum(entry_two, grad_hidden))
-    grad_hidden, leaving_fc1 = lax.optimization_barrier((grad_hidden, leaving_fc1))
-    sum_fc1 = reduce_end(kept_fc1, leaving_fc1)
+    here_fc2, away_fc2 = split_x(kept_fc2, arrived_fc2)
+    grad_hidden, away_fc2 = tied((grad_hidden, away_fc2))
+    crossed_fc2 = flip(away_fc2, 2)
+    kept_fc1, leaving_fc1 = split_core(outer_sum(entry_two, grad_hidden))
+    grad_hidden, leaving_fc1 = tied((grad_hidden, leaving_fc1))
+    arrived_fc1 = flip(leaving_fc1, 1)
     grad_entry_two = compared_with(grad_hidden, full_fc1)
     grad_shift_two = jnp.sum(grad_entry_two, axis=0, keepdims=True)
     grad_scale_two = jnp.sum(grad_entry_two * normed_two, axis=0, keepdims=True)
@@ -794,15 +836,37 @@
         )
     )
     grad_branch_one = low(gate_one * grad_middle)
-    kept_out, leaving_out = reduce_begin(outer_sum(mixed, grad_branch_one))
-    grad_branch_one, leaving_out = lax.optimization_barrier((grad_branch_one, leaving_out))
-    sum_out = reduce_end(kept_out, leaving_out)
+    here_fc1, away_fc1 = split_x(kept_fc1, arrived_fc1)
+    grad_branch_one, away_fc1 = tied((grad_branch_one, away_fc1))
+    crossed_fc1 = flip(away_fc1, 2)
+    kept_out, leaving_out = split_core(outer_sum(mixed, grad_branch_one))
+    arrived_out = flip(leaving_out, 1)
     grad_mixed = low(compared_with(grad_branch_one, full_out))
+    total_fc2, leaving_fc2 = split_z(here_fc2, crossed_fc2)
+    here_out, away_out = split_x(kept_out, arrived_out)
+    grad_mixed, leaving_fc2, away_out = tied((grad_mixed, leaving_fc2, away_out))
+    landed_fc2 = send_z(leaving_fc2)
+    crossed_out = flip(away_out, 2)
     grad_project = jnp.concatenate(attend_local_back(projected, grad_mixed, log_totals), axis=1)
-    kept_qkv, leaving_qkv = reduce_begin(outer_sum(entry_one, grad_project))
-    grad_project, leaving_qkv = lax.optimization_barrier((grad_project, leaving_qkv))
-    sum_qkv = reduce_end(kept_qkv, leaving_qkv)
+    kept_qkv, leaving_qkv = split_core(outer_sum(entry_one, grad_project))
+    grad_project, leaving_qkv = tied((grad_project, leaving_qkv))
+    arrived_qkv = flip(leaving_qkv, 1)
+    here_qkv, away_qkv = split_x(kept_qkv, arrived_qkv)
     grad_entry_one = compared_with(grad_project, full_qkv)
+    grad_entry_one, away_qkv, here_fc1, total_fc2 = tied(
+        (grad_entry_one, away_qkv, here_fc1, total_fc2)
+    )
+    crossed_qkv = flip(away_qkv, 2)
+    total_fc1, leaving_fc1 = split_z(here_fc1, crossed_fc1)
+    landed_fc1 = send_z(leaving_fc1)
+    sum_fc2 = sum_seq(sum_z(total_fc2, landed_fc2))
+    total_out, leaving_out = split_z(here_out, crossed_out)
+    landed_out = send_z(leaving_out)
+    total_qkv, leaving_qkv = split_z(here_qkv, crossed_qkv)
+    landed_qkv = send_z(leaving_qkv)
+    sum_fc1 = sum_seq(sum_z(total_fc1, landed_fc1))
+    sum_out = sum_seq(sum_z(total_out, landed_out))
+    sum_qkv = sum_seq(sum_z(total_qkv, landed_qkv))
     grad_shift_one = jnp.sum(grad_entry_one, axis=0, keepdims=True)
     grad_scale_one = jnp.sum(grad_entry_one * normed_one, axis=0, keepdims=True)
     grad_latents = both_halves(

time: 698 us -> 603 us (0.86)
  the two profiles are of different devices: /device:TPU:12 before, /device:TPU:0 now
where the time goes in v3:
time: 603 us; the launch traced here: 593 us
  waiting for transfers between devices  244 us (40%)
  matrix products  91.7 us (15%)
  starting transfers between devices  69.6 us (12%)
  Pallas kernels  66.9 us (11%)
  other arithmetic  61.2 us (10%)
  local copies, waits for them, and re-layouts  43.8 us (7%)
  between operations  15.4 us (3%)
    ppermute x12, waiting for transfers between devices, send_z(): arrived.append(lax.ppermute(part, 'fsdp', pairs))  66.3 us
    all_gather x3, waiting for transfers between devices, gather_z(): lax.all_gather(weight, 'fsdp', axis=0, tiled=False, axis_index_groups=z_g...  45.2 us
    all_to_all x1, waiting for transfers between devices, local_whole_latent(): from_owners = lax.all_to_all(to_owners, 'fsdp', 0, 0, tiled=True)  44.3 us
    pallas_call x3, Pallas kernels, assemble(): pl.pallas_call(assemble_kernel, grid_spec=pltpu.PrefetchScalarGridSpec(nu...  36.5 us
    ppermute x17, waiting for transfers between devices, flip(): lax.ppermute(tensor, 'fsdp', swapped_pairs(lax.axis_size('fsdp'), bit))  34.2 us
    dot_general x5, matrix products, compared_with(): lax.dot_general(earlier_value, latter, (((1,), (1,)), ((), ())), preferre...  32.8 us
    ppermute x2, waiting for transfers between devices, gather_latents(): lax.ppermute(tensor, 'fsdp', swapped_pairs(count, 2))  31.9 us
    add x4, other arithmetic, split_x(): here = wide(pick(kept, 1, x_at)) + wide(pick(arrived, 1, x_at))  22.8 us
  transfers between devices with their start and end apart: 55, of which 23 were waited for; matrix products, arithmetic and copies ran while one was open for 25% of the time, Pallas kernels for 11%

profile of v3, /device:TPU:0, one launch (start us, length us, event | category | flops | bytes accessed | tf_op | source)
XLA Modules:
  0.0 592.7 jit_solution(16873206340604515815)
XLA Ops:
  14.8 44.1 %all-gather.7.cloned.1.call-done = bf16[256,4096]{1,0:T(8,128)(2,1)} async-done(((bf16[64,4096]{1,0:T(8,128)(2,1)}), bf16[256,4096]{1,0:T(8,128)(2,1)}) %all-gather.7.cloned.1.call-update) | async-done | bytes 2097168 | tf_op jit(solution)/shard_map/all_gather | solution.py:556
  66.5 44.3 %all-to-all-done = f32[16,1,6656]{2,1,0:T(1,128)S(1)} async-done(((f32[16,1,6656]{2,1,0:T(1,128)}), f32[16,1,6656]{2,1,0:T(1,128)S(1)}, u32[]{:S(2)}, u32[]{:S(2)}) %all-to-all-start) | async-done | bytes 426016 | tf_op jit(solution)/shard_map/all_to_all | solution.py:759
  114.9 5.1 collective-permute-done.3.p11
  124.1 13.0 %assemble.3 = (bf16[4,4,64,3072]{3,2,1,0:T(8,128)(2,1)}, bf16[4,4,64,1024]{3,2,1,0:T(8,128)(2,1)S(1)}) custom-call(s32[4]{0:T(128)S(1)} %iota_xor_fusion.place_ref, bf16[4,64,4096]{2,1,0:T(8,128)(2,1)} %bitcast.9.p00, bf16[4,64,4096]{2,1,0:T(8,128)(2,1)} %collective-permute-done.2.p01, bf16[4,64,4096]{2,1,0:T(8,128)(2,1)} %collective-permute-done.1.p10, ...), custom_call_target="tpu_custom_call" | custom-call | bytes 16777216 | tf_op jit(solution)/shard_map/assemble/pallas_call | solution.py:580
  138.4 6.4 %add_convert_fusion.q_ref.k_ref.v_ref = bf16[512,3072]{1,0:T(8,128)(2,1)S(1)} fusion(bf16[512,1024]{1,0:T(8,128)(2,1)S(1)} %copy-done.34, bf16[1024,3072]{1,0:T(8,128)(2,1)} %bitcast.294, f32[3072]{0:T(1024)S(1)} %bitcast.287), kind=kOutput, calls=%fused_computation.15 | convolution fusion | flops 3224371200 | bytes 10498048 | tf_op jit(solution)/shard_map/dot_general | solution.py:792
  144.9 13.0 %attend.1 = (bf16[512,1024]{1,0:T(8,128)(2,1)S(1)}, f32[8,2,512]{2,1,0:T(2,128)S(1)}) custom-call(bf16[512,3072]{1,0:T(8,128)(2,1)S(1)} %add_convert_fusion.q_ref.k_ref.v_ref, bf16[512,3072]{1,0:T(8,128)(2,1)S(1)} %add_convert_fusion.q_ref.k_ref.v_ref, bf16[512,3072]{1,0:T(8,128)(2,1)S(1)} %add_convert_fusion.q_ref.k_ref.v_ref), custom_call_target="tpu_custom_call" | custom-call | flops 4294967296 | bytes 4718592 | tf_op jit(solution)/shard_map/attend/pallas_call | solution.py:489
  158.8 10.8 %collective-permute-done.4.p10 = bf16[4,64,4096]{2,1,0:T(8,128)(2,1)} collective-permute-done((bf16[4,64,4096]{2,1,0:T(8,128)(2,1)}, bf16[4,64,4096]{2,1,0:T(8,128)(2,1)}, u32[]{:S(2)}, u32[]{:S(2)}) %collective-permute-start.4) | collective-permute-done | bytes 2097184 | tf_op jit(solution)/shard_map/ppermute | solution.py:560
  183.9 11.6 %assemble.4 = bf16[4,4,64,4096]{3,2,1,0:T(8,128)(2,1)} custom-call(s32[4]{0:T(128)S(1)} %iota_xor_fusion.place_ref, bf16[4,64,4096]{2,1,0:T(8,128)(2,1)S(1)} %bitcast.247, bf16[4,64,4096]{2,1,0:T(8,128)(2,1)S(1)} %copy-done.6, bf16[4,64,4096]{2,1,0:T(8,128)(2,1)} %collective-permute-done.4.p10, bf16[4,64,4096]{2,1,0:T(8,128)(2,1)} %collective-permute-done.6.p11), custom_call_target="tpu_custom_call" | custom-call | bytes 16777216 | tf_op jit(solution)/shard_map/assemble/pallas_call | solution.py:580
  195.5 10.4 %fusion.79 = f32[512,4096]{1,0:T(8,128)} fusion(bf16[512,1024]{1,0:T(8,128)(2,1)S(1)} %copy-done.36, bf16[1024,4096]{1,0:T(8,128)(2,1)} %bitcast.250), kind=kOutput, calls=%fused_computation.227 | convolution fusion | flops 4294967296 | bytes 17825792 | tf_op jit(solution)/shard_map/dot_general | solution.py:804
  205.9 10.4 %convolution_convert_fusion.1 = bf16[4096,1024]{1,0:T(8,128)(2,1)S(1)} fusion(f32[1024]{0:T(1024)S(1)} %bitcast.290, bf16[256,1024]{1,0:T(8,128)(2,1)} %collective-permute-done.7, bf16[256,1024]{1,0:T(8,128)(2,1)S(1)} %copy-done.43, f32[512,4096]{1,0:T(8,128)} %fusion.79, f32[4096]{0:T(1024)S(1)} %bitcast.284), kind=kOutput, calls=%fused_computation.13 | convolution fusion | flops 4323278848 | bytes 17846272 | tf_op jit(solution)/shard_map/dot_general | solution.py:46
  222.4 6.4 %collective-permute-done.8.p10 = bf16[4,256,1024]{2,1,0:T(8,128)(2,1)} collective-permute-done((bf16[4,256,1024]{2,1,0:T(8,128)(2,1)}, bf16[4,256,1024]{2,1,0:T(8,128)(2,1)}, u32[]{:S(2)}, u32[]{:S(2)}) %collective-permute-start.8) | collective-permute-done | bytes 2097184 | tf_op jit(solution)/shard_map/ppermute | solution.py:560
  234.9 11.9 %assemble.5 = bf16[4,4,256,1024]{3,2,1,0:T(8,128)(2,1)} custom-call(s32[4]{0:T(128)S(1)} %iota_xor_fusion.place_ref, bf16[4,256,1024]{2,1,0:T(8,128)(2,1)S(1)} %bitcast.244, bf16[4,256,1024]{2,1,0:T(8,128)(2,1)S(1)} %copy-done.3, bf16[4,256,1024]{2,1,0:T(8,128)(2,1)} %collective-permute-done.8.p10, bf16[4,256,1024]{2,1,0:T(8,128)(2,1)} %collective-permute-done.10.p11), custom_call_target="tpu_custom_call" | custom-call | bytes 16777216 | tf_op jit(solution)/shard_map/assemble/pallas_call | solution.py:580
  246.8 16.1 %fusion.3 = bf16[512,4096]{1,0:T(8,128)(2,1)} fusion(f32[512,4096]{1,0:T(8,128)} %fusion.79, f32[4096]{0:T(1024)S(1)} %bitcast.285, bf16[4096,1024]{1,0:T(8,128)(2,1)} %bitcast.260, f32[1024]{0:T(1024)S(1)} %bitcast.291, bf16[256,1024]{1,0:T(8,128)(2,1)} %collective-permute-done.7, bf16[256,1024]{1,0:T(8,128)(2,1)S(1)} %copy-done.44), kind=kOutput, calls=%fused_computation.7 | convolution fusion | flops 4350541824 | bytes 22040576 | tf_op jit(solution)/shard_map/dot_general | solution.py:52
  263.0 7.2 %convert_add_fusion.1 = (f32[4,256,1024]{2,1,0:T(8,128)}, bf16[4,256,1024]{2,1,0:T(8,128)(2,1)}) fusion(bf16[4,2,256,1024]{3,2,0,1:T(8,128)(2,1)} %collective-permute-done.12, s32[]{:T(128)S(6)} %select_n.366, bf16[4,2,2,256,1024]{4,3,2,1,0:T(8,128)(2,1)S(1)} %bitcast.257, s32[]{:T(128)S(6)} %select_n.367, s32[]{:T(128)S(6)} %select_n.365, ...), kind=kLoop, calls=%fused_computation.18 | loop fusion | flops 7340032 | bytes 14680084 | tf_op jit(solution)/shard_map/add | solution.py:660
  270.1 4.8 convolution_convert_fusion
  279.8 8.4 %multiply_reduce_fusion = (bf16[1024]{0:T(1024)(128)(2,1)S(1)}, f32[512]{0:T(512)S(1)}, f32[512]{0:T(512)S(1)}, bf16[1024]{0:T(1024)(128)(2,1)S(1)}, f32[512,1024]{1,0:T(8,128)}) fusion(f32[512,1024]{1,0:T(8,128)S(1)} %copy-done.19, f32[512]{0:T(512)S(1)} %add_rsqrt_fusion, f32[512]{0:T(512)S(1)} %broadcast_multiply_fusion.4, f32[1024]{0:T(1024)S(1)} %bitcast.280, ...), kind=kOutput, calls=%fused_computation.56 | convolution fusion | flops 4299682816 | bytes 16793600 | tf_op jit(solution)/shard_map/dot_general | solution.py:52
  288.4 13.7 %convert_reduce_fusion.2 = (f32[1024]{0:T(1024)S(1)}, bf16[1024]{0:T(1024)(128)(2,1)S(1)}, bf16[512,1024]{1,0:T(8,128)(2,1)}, bf16[1024]{0:T(1024)(128)(2,1)S(1)}, f32[512,1024]{1,0:T(8,128)}) fusion(f32[1024]{0:T(1024)S(1)} %bitcast.292, bf16[256,1024]{1,0:T(8,128)(2,1)} %collective-permute-done.7, bf16[256,1024]{1,0:T(8,128)(2,1)S(1)} %copy-done.44, ...), kind=kOutput, calls=%fused_computation.52 | convolution fusion | flops 4329042944 | bytes 27312128 | tf_op jit(solution)/shard_map/dot_general | solution.py:813
  311.4 7.7 %convert_add_fusion = (f32[4,64,4096]{2,1,0:T(8,128)}, bf16[4,64,4096]{2,1,0:T(8,128)(2,1)}) fusion(bf16[4,2,64,4096]{3,2,0,1:T(8,128)(2,1)} %collective-permute-done.13, s32[]{:T(128)S(6)} %select_n.366, bf16[4,2,2,64,4096]{4,3,2,1,0:T(8,128)(2,1)} %bitcast.259, s32[]{:T(128)S(6)} %select_n.367, s32[]{:T(128)S(6)} %select_n.365, s32[]{:T(128)S(6)} %select_n.362, ...), kind=kLoop, calls=%fused_computation.17 | loop fusion | flops 7340032 | bytes 14680084 | tf_op jit(solution)/shard_map/add | solution.py:660
  322.8 29.5 %collective-permute-done.26 = bf16[2,2,1,4096]{3,1,0,2:T(2,128)(2,1)S(1)} collective-permute-done((bf16[2,2,1,4096]{3,1,0,2:T(2,128)(2,1)S(1)}, bf16[2,2,1,4096]{3,1,0,2:T(2,128)(2,1)S(1)}, u32[]{:S(2)}, u32[]{:S(2)}) %collective-permute-start.26) | collective-permute-done | bytes 32800 | tf_op jit(solution)/shard_map/ppermute | solution.py:621
  365.5 17.4 %attend_back.1 = (bf16[512,1024]{1,0:T(8,128)(2,1)S(1)}, bf16[512,1024]{1,0:T(8,128)(2,1)S(1)}, bf16[512,1024]{1,0:T(8,128)(2,1)S(1)}) custom-call(bf16[512,3072]{1,0:T(8,128)(2,1)} %copy-done.11, bf16[512,3072]{1,0:T(8,128)(2,1)} %copy-done.11, bf16[512,3072]{1,0:T(8,128)(2,1)} %copy-done.11, bf16[512,1024]{1,0:T(8,128)(2,1)S(1)} %convolution_convert_fusion.4.do_ref, ...), custom_call_target="tpu_custom_call" | custom-call | flops 10737418240 | bytes 9437184 | tf_op jit(solution)/shard_map/attend_back/pallas_call | solution.py:517
  423.5 6.7 %fusion.80 = f32[512,1024]{1,0:T(8,128)S(1)} fusion(bf16[512,3072]{1,0:T(8,128)(2,1)} %copy-done.27, bf16[1024,3072]{1,0:T(8,128)(2,1)} %bitcast.295), kind=kOutput, calls=%fused_computation.228 | convolution fusion | flops 3221225472 | bytes 11534336 | tf_op jit(solution)/shard_map/dot_general | solution.py:52
  443.5 5.3 convert_add_fusion.4
  450.5 8.0 %collective-permute-done.41 = bf16[4,64,4096]{2,1,0:T(8,128)(2,1)} collective-permute-done((bf16[4,64,4096]{2,1,0:T(8,128)(2,1)}, bf16[4,64,4096]{2,1,0:T(8,128)(2,1)}, u32[]{:S(2)}, u32[]{:S(2)}) %collective-permute-start.41) | collective-permute-done | bytes 2097184 | tf_op jit(solution)/shard_map/ppermute | solution.py:560
  461.2 6.8 %collective-permute-done.47 = bf16[256,1024]{1,0:T(8,128)(2,1)S(1)} collective-permute-done((bf16[256,1024]{1,0:T(8,128)(2,1)S(1)}, bf16[256,1024]{1,0:T(8,128)(2,1)S(1)}, u32[]{:S(2)}, u32[]{:S(2)}) %collective-permute-start.47) | collective-permute-done | bytes 524320 | tf_op jit(solution)/shard_map/ppermute | solution.py:679
  474.3 11.6 %collective-permute-start.23 = (bf16[8,2048]{1,0:T(8,128)(2,1)}, bf16[8,2048]{1,0:T(8,128)(2,1)S(1)}, u32[]{:S(2)}, u32[]{:S(2)}) collective-permute-start(bf16[8,2048]{1,0:T(8,128)(2,1)} %reshape.398), channel_id=1, source_target_pairs={{0,4},{1,5},{2,6},{3,7},{4,8},{5,9},{6,10},{7,11},{8,12},{9,13},{1... | collective-permute-start | bytes 98312 | tf_op jit(solution)/shard_map/ppermute | solution.py:627
  500.6 7.8 %collective-permute-done.42 = bf16[64,4096]{1,0:T(8,128)(2,1)S(1)} collective-permute-done((bf16[64,4096]{1,0:T(8,128)(2,1)S(1)}, bf16[64,4096]{1,0:T(8,128)(2,1)S(1)}, u32[]{:S(2)}, u32[]{:S(2)}) %collective-permute-start.42) | collective-permute-done | bytes 524320 | tf_op jit(solution)/shard_map/ppermute | solution.py:679
  508.9 7.8 %collective-permute-done.44 = bf16[64,4096]{1,0:T(8,128)(2,1)S(1)} collective-permute-done((bf16[64,4096]{1,0:T(8,128)(2,1)S(1)}, bf16[64,4096]{1,0:T(8,128)(2,1)S(1)}, u32[]{:S(2)}, u32[]{:S(2)}) %collective-permute-start.44) | collective-permute-done | bytes 524320 | tf_op jit(solution)/shard_map/ppermute | solution.py:679
  516.7 21.6 %collective-permute-done.43 = bf16[64,4096]{1,0:T(8,128)(2,1)S(1)} collective-permute-done((bf16[64,4096]{1,0:T(8,128)(2,1)S(1)}, bf16[64,4096]{1,0:T(8,128)(2,1)S(1)}, u32[]{:S(2)}, u32[]{:S(2)}) %collective-permute-start.43) | collective-permute-done | bytes 524320 | tf_op jit(solution)/shard_map/ppermute | solution.py:679
  545.9 6.7 %collective-permute-done.45 = bf16[64,4096]{1,0:T(8,128)(2,1)S(1)} collective-permute-done((bf16[64,4096]{1,0:T(8,128)(2,1)S(1)}, bf16[64,4096]{1,0:T(8,128)(2,1)S(1)}, u32[]{:S(2)}, u32[]{:S(2)}) %collective-permute-start.45) | collective-permute-done | bytes 524320 | tf_op jit(solution)/shard_map/ppermute | solution.py:690
  555.9 6.2 %collective-permute-done.33 = bf16[64,3072]{1,0:T(8,128)(2,1)S(1)} collective-permute-done((bf16[64,3072]{1,0:T(8,128)(2,1)S(1)}, bf16[64,3072]{1,0:T(8,128)(2,1)S(1)}, u32[]{:S(2)}, u32[]{:S(2)}) %collective-permute-start.33) | collective-permute-done | bytes 393248 | tf_op jit(solution)/shard_map/ppermute | solution.py:679
  562.1 14.0 %collective-permute-done.32 = bf16[64,3072]{1,0:T(8,128)(2,1)S(1)} collective-permute-done((bf16[64,3072]{1,0:T(8,128)(2,1)S(1)}, bf16[64,3072]{1,0:T(8,128)(2,1)S(1)}, u32[]{:S(2)}, u32[]{:S(2)}) %collective-permute-start.32) | collective-permute-done | bytes 393248 | tf_op jit(solution)/shard_map/ppermute | solution.py:679
  579.5 5.3 collective-permute-done.34
  (365 shorter events, 177.6 us)
Async XLA Ops:
  7.3 51.6 %all-gather.7.cloned.1.call-start = ((), (), s32[]{:S(2)}) async-start(), calls=%async_computation.2 | async-start | bytes 2621440 | tf_op jit(solution)/shard_map/all_gather | solution.py:556
  9.5 55.8 %collective-permute-start = (bf16[256,1024]{1,0:T(8,128)(2,1)S(1)}, bf16[256,1024]{1,0:T(8,128)(2,1)S(1)}, u32[]{:S(2)}, u32[]{:S(2)}) collective-permute-start(bf16[256,1024]{1,0:T(8,128)(2,1)S(1)} %get-tuple-element.141), channel_id=1, source_target_pairs={{0,16},{16,0},{1,17},{17,1},{2,18},{18,2},{3,19},{19,3},{4,20},{20... | collective-permute-start | bytes 1572872 | tf_op jit(solution)/shard_map/ppermute | solution.py:724
  59.0 54.2 %collective-permute-start.1 = (bf16[4,64,4096]{2,1,0:T(8,128)(2,1)}, bf16[4,64,4096]{2,1,0:T(8,128)(2,1)}, u32[]{:S(2)}, u32[]{:S(2)}) collective-permute-start(bf16[4,64,4096]{2,1,0:T(8,128)(2,1)} %bitcast.9.p00), channel_id=1, source_target_pairs={{0,2},{1,3},{2,0},{3,1},{4,6},{5,7},{6,4},{7,5},{8,10},{9,11},{10,... | collective-permute-start | bytes 6291464 | tf_op jit(solution)/shard_map/ppermute | solution.py:560
  61.7 49.2 %all-to-all-start = ((f32[16,1,6656]{2,1,0:T(1,128)}), f32[16,1,6656]{2,1,0:T(1,128)S(1)}, u32[]{:S(2)}, u32[]{:S(2)}) async-start(f32[16,1,6656]{2,1,0:T(1,128)} %copy.82), calls=%async_computation | async-start | bytes 851968 | tf_op jit(solution)/shard_map/all_to_all | solution.py:759
  65.2 49.6 %all-gather.9.cloned.1.call-start = ((), (), s32[]{:S(2)}) async-start(), calls=%async_computation.3 | async-start | bytes 2621440 | tf_op jit(solution)/shard_map/all_gather | solution.py:556
  66.0 114.5 %all-gather.11.cloned.1.call-start = ((), (), s32[]{:S(2)}) async-start(), calls=%async_computation.4 | async-start | bytes 2621440 | tf_op jit(solution)/shard_map/all_gather | solution.py:556
  121.2 37.6 %collective-permute-start.5 = (bf16[4,64,4096]{2,1,0:T(8,128)(2,1)}, bf16[4,64,4096]{2,1,0:T(8,128)(2,1)S(1)}, u32[]{:S(2)}, u32[]{:S(2)}) collective-permute-start(bf16[4,64,4096]{2,1,0:T(8,128)(2,1)} %bitcast.245), channel_id=1, source_target_pairs={{0,1},{1,0},{2,3},{3,2},{4,5},{5,4},{6,7},{7,6},{8,9},{9,8},{10,11... | collective-permute-start | bytes 6291464 | tf_op jit(solution)/shard_map/ppermute | solution.py:560
  121.6 48.0 %collective-permute-start.4 = (bf16[4,64,4096]{2,1,0:T(8,128)(2,1)}, bf16[4,64,4096]{2,1,0:T(8,128)(2,1)}, u32[]{:S(2)}, u32[]{:S(2)}) collective-permute-start(bf16[4,64,4096]{2,1,0:T(8,128)(2,1)} %bitcast.246), channel_id=1, source_target_pairs={{0,2},{1,3},{2,0},{3,1},{4,6},{5,7},{6,4},{7,5},{8,10},{9,11},{10,... | collective-permute-start | bytes 6291464 | tf_op jit(solution)/shard_map/ppermute | solution.py:560
  170.6 35.2 %collective-permute-start.7 = (bf16[256,1024]{1,0:T(8,128)(2,1)}, bf16[256,1024]{1,0:T(8,128)(2,1)}, u32[]{:S(2)}, u32[]{:S(2)}) collective-permute-start(bf16[256,1024]{1,0:T(8,128)(2,1)} %get-tuple-element.139), channel_id=1, source_target_pairs={{0,16},{16,0},{1,17},{17,1},{2,18},{18,2},{3,19},{19,3},{4,20},{20... | collective-permute-start | bytes 1572872 | tf_op jit(solution)/shard_map/ppermute | solution.py:724
  180.5 40.6 %collective-permute-start.9 = (bf16[4,256,1024]{2,1,0:T(8,128)(2,1)}, bf16[4,256,1024]{2,1,0:T(8,128)(2,1)S(1)}, u32[]{:S(2)}, u32[]{:S(2)}) collective-permute-start(bf16[4,256,1024]{2,1,0:T(8,128)(2,1)} %bitcast.242), channel_id=1, source_target_pairs={{0,1},{1,0},{2,3},{3,2},{4,5},{5,4},{6,7},{7,6},{8,9},{9,8},{10,11... | collective-permute-start | bytes 6291464 | tf_op jit(solution)/shard_map/ppermute | solution.py:560
  180.7 48.1 %collective-permute-start.8 = (bf16[4,256,1024]{2,1,0:T(8,128)(2,1)}, bf16[4,256,1024]{2,1,0:T(8,128)(2,1)}, u32[]{:S(2)}, u32[]{:S(2)}) collective-permute-start(bf16[4,256,1024]{2,1,0:T(8,128)(2,1)} %bitcast.243), channel_id=1, source_target_pairs={{0,2},{1,3},{2,0},{3,1},{4,6},{5,7},{6,4},{7,5},{8,10},{9,11},{10,... | collective-permute-start | bytes 6291464 | tf_op jit(solution)/shard_map/ppermute | solution.py:560
  228.8 34.1 %collective-permute-start.12 = (bf16[4,2,256,1024]{3,2,0,1:T(8,128)(2,1)}, bf16[4,2,256,1024]{3,2,0,1:T(8,128)(2,1)}, u32[]{:S(2)}, u32[]{:S(2)}) collective-permute-start(bf16[4,2,256,1024]{3,2,0,1:T(8,128)(2,1)} %copy_bitcast_fusion.1), channel_id=1, source_target_pairs={{0,1},{1,0},{2,3},{3,2},{4,5},{5,4},{6,7},{7,6},{8,9},{9,8},{10,11... | collective-permute-start | bytes 12582920 | tf_op jit(solution)/shard_map/ppermute | solution.py:560
  288.2 23.2 %collective-permute-start.13 = (bf16[4,2,64,4096]{3,2,0,1:T(8,128)(2,1)}, bf16[4,2,64,4096]{3,2,0,1:T(8,128)(2,1)}, u32[]{:S(2)}, u32[]{:S(2)}) collective-permute-start(bf16[4,2,64,4096]{3,2,0,1:T(8,128)(2,1)} %copy_bitcast_fusion), channel_id=1, source_target_pairs={{0,1},{1,0},{2,3},{3,2},{4,5},{5,4},{6,7},{7,6},{8,9},{9,8},{10,11... | collective-permute-start | bytes 12582920 | tf_op jit(solution)/shard_map/ppermute | solution.py:560
  303.8 50.8 %collective-permute-start.14 = (bf16[4,256,1024]{2,1,0:T(8,128)(2,1)}, bf16[4,256,1024]{2,1,0:T(8,128)(2,1)}, u32[]{:S(2)}, u32[]{:S(2)}) collective-permute-start(bf16[4,256,1024]{2,1,0:T(8,128)(2,1)} %get-tuple-element.77), channel_id=1, source_target_pairs={{0,2},{1,3},{2,0},{3,1},{4,6},{5,7},{6,4},{7,5},{8,10},{9,11},{10,... | collective-permute-start | bytes 6291464 | tf_op jit(solution)/shard_map/ppermute | solution.py:560
  308.0 85.9 %collective-permute-start.11 = (bf16[256,1024]{1,0:T(8,128)(2,1)}, bf16[256,1024]{1,0:T(8,128)(2,1)}, u32[]{:S(2)}, u32[]{:S(2)}) collective-permute-start(bf16[256,1024]{1,0:T(8,128)(2,1)} %slice.125), channel_id=1, source_target_pairs={{0,16},{16,0},{1,17},{17,1},{2,18},{18,2},{3,19},{19,3},{4,20},{20... | collective-permute-start | bytes 1572872 | tf_op jit(solution)/shard_map/ppermute | solution.py:727
  310.9 41.4 %collective-permute-start.26 = (bf16[2,2,1,4096]{3,1,0,2:T(2,128)(2,1)S(1)}, bf16[2,2,1,4096]{3,1,0,2:T(2,128)(2,1)S(1)}, u32[]{:S(2)}, u32[]{:S(2)}) collective-permute-start(bf16[2,2,1,4096]{3,1,0,2:T(2,128)(2,1)S(1)} %pad_maximum_fusion.7), channel_id=1, source_target_pairs={{0,2},{1,3},{2,0},{3,1},{4,6},{5,7},{6,4},{7,5},{8,10},{9,11},{10,... | collective-permute-start | bytes 98312 | tf_op jit(solution)/shard_map/ppermute | solution.py:621
  322.8 39.7 %collective-permute-start.15 = (bf16[4,2,64,1024]{3,2,0,1:T(8,128)(2,1)}, bf16[4,2,64,1024]{3,2,0,1:T(8,128)(2,1)}, u32[]{:S(2)}, u32[]{:S(2)}) collective-permute-start(bf16[4,2,64,1024]{3,2,0,1:T(8,128)(2,1)} %copy_bitcast_fusion.3), channel_id=1, source_target_pairs={{0,1},{1,0},{2,3},{3,2},{4,5},{5,4},{6,7},{7,6},{8,9},{9,8},{10,11... | collective-permute-start | bytes 3145736 | tf_op jit(solution)/shard_map/ppermute | solution.py:560
  352.6 39.0 %collective-permute-start.29 = (bf16[8,4096]{1,0:T(8,128)(2,1)S(1)}, bf16[8,4096]{1,0:T(8,128)(2,1)S(1)}, u32[]{:S(2)}, u32[]{:S(2)}) collective-permute-start(bf16[8,4096]{1,0:T(8,128)(2,1)S(1)} %reshape.399), channel_id=1, source_target_pairs={{0,4},{1,5},{2,6},{3,7},{4,8},{5,9},{6,10},{7,11},{8,12},{9,13},{1... | collective-permute-start | bytes 196616 | tf_op jit(solution)/shard_map/ppermute | solution.py:627
  352.6 38.9 %collective-permute-start.28 = (bf16[8,4096]{1,0:T(8,128)(2,1)S(1)}, bf16[8,4096]{1,0:T(8,128)(2,1)S(1)}, u32[]{:S(2)}, u32[]{:S(2)}) collective-permute-start(bf16[8,4096]{1,0:T(8,128)(2,1)S(1)} %reshape.399), channel_id=1, source_target_pairs={{0,8},{1,9},{2,10},{3,11},{4,12},{5,13},{6,14},{7,15},{8,0},{9,1},... | collective-permute-start | bytes 196616 | tf_op jit(solution)/shard_map/ppermute | solution.py:627
  354.6 37.0 %collective-permute-start.27 = (bf16[8,4096]{1,0:T(8,128)(2,1)S(1)}, bf16[8,4096]{1,0:T(8,128)(2,1)S(1)}, u32[]{:S(2)}, u32[]{:S(2)}) collective-permute-start(bf16[8,4096]{1,0:T(8,128)(2,1)S(1)} %reshape.399), channel_id=1, source_target_pairs={{0,12},{1,13},{2,14},{3,15},{4,0},{5,1},{6,2},{7,3},{8,4},{9,5},{1... | collective-permute-start | bytes 196616 | tf_op jit(solution)/shard_map/ppermute | solution.py:627
  391.5 52.0 %collective-permute-start.16 = (bf16[4,2,64,3072]{3,2,0,1:T(8,128)(2,1)}, bf16[4,2,64,3072]{3,2,0,1:T(8,128)(2,1)}, u32[]{:S(2)}, u32[]{:S(2)}) collective-permute-start(bf16[4,2,64,3072]{3,2,0,1:T(8,128)(2,1)} %copy_bitcast_fusion.2), channel_id=1, source_target_pairs={{0,1},{1,0},{2,3},{3,2},{4,5},{5,4},{6,7},{7,6},{8,9},{9,8},{10,11... | collective-permute-start | bytes 9437192 | tf_op jit(solution)/shard_map/ppermute | solution.py:560
  392.2 25.9 %collective-permute-start.36 = (bf16[4,64,1024]{2,1,0:T(8,128)(2,1)}, bf16[4,64,1024]{2,1,0:T(8,128)(2,1)}, u32[]{:S(2)}, u32[]{:S(2)}) collective-permute-start(bf16[4,64,1024]{2,1,0:T(8,128)(2,1)} %get-tuple-element.87), channel_id=1, source_target_pairs={{0,2},{1,3},{2,0},{3,1},{4,6},{5,7},{6,4},{7,5},{8,10},{9,11},{10,... | collective-permute-start | bytes 1572872 | tf_op jit(solution)/shard_map/ppermute | solution.py:560
  410.3 48.3 %collective-permute-start.41 = (bf16[4,64,4096]{2,1,0:T(8,128)(2,1)}, bf16[4,64,4096]{2,1,0:T(8,128)(2,1)}, u32[]{:S(2)}, u32[]{:S(2)}) collective-permute-start(bf16[4,64,4096]{2,1,0:T(8,128)(2,1)} %get-tuple-element.89), channel_id=1, source_target_pairs={{0,2},{1,3},{2,0},{3,1},{4,6},{5,7},{6,4},{7,5},{8,10},{9,11},{10,... | collective-permute-start | bytes 6291464 | tf_op jit(solution)/shard_map/ppermute | solution.py:560
  430.9 30.3 %collective-permute-start.46 = (bf16[256,1024]{1,0:T(8,128)(2,1)S(1)}, bf16[256,1024]{1,0:T(8,128)(2,1)S(1)}, u32[]{:S(2)}, u32[]{:S(2)}) collective-permute-start(bf16[256,1024]{1,0:T(8,128)(2,1)S(1)} %copy-done.42), channel_id=1, source_target_pairs={{0,4},{1,5},{2,6},{3,7},{4,8},{5,9},{6,10},{7,11},{8,12},{9,13},{1... | collective-permute-start | bytes 1572872 | tf_op jit(solution)/shard_map/ppermute | solution.py:679
  431.6 36.5 %collective-permute-start.47 = (bf16[256,1024]{1,0:T(8,128)(2,1)S(1)}, bf16[256,1024]{1,0:T(8,128)(2,1)S(1)}, u32[]{:S(2)}, u32[]{:S(2)}) collective-permute-start(bf16[256,1024]{1,0:T(8,128)(2,1)S(1)} %copy-done.41), channel_id=1, source_target_pairs={{0,8},{1,9},{2,10},{3,11},{4,12},{5,13},{6,14},{7,15},{8,0},{9,1},... | collective-permute-start | bytes 1572872 | tf_op jit(solution)/shard_map/ppermute | solution.py:679
  439.9 28.1 %collective-permute-start.48 = (bf16[256,1024]{1,0:T(8,128)(2,1)S(1)}, bf16[256,1024]{1,0:T(8,128)(2,1)S(1)}, u32[]{:S(2)}, u32[]{:S(2)}) collective-permute-start(bf16[256,1024]{1,0:T(8,128)(2,1)S(1)} %copy-done.40), channel_id=1, source_target_pairs={{0,12},{1,13},{2,14},{3,15},{4,0},{5,1},{6,2},{7,3},{8,4},{9,5},{1... | collective-permute-start | bytes 1572872 | tf_op jit(solution)/shard_map/ppermute | solution.py:679
  470.6 69.9 %collective-permute-start.49 = (bf16[256,1024]{1,0:T(8,128)(2,1)S(1)}, bf16[256,1024]{1,0:T(8,128)(2,1)S(1)}, u32[]{:S(2)}, u32[]{:S(2)}) collective-permute-start(bf16[256,1024]{1,0:T(8,128)(2,1)S(1)} %add_convert_fusion.3), channel_id=1, source_target_pairs={{0,16},{16,0},{1,17},{17,1},{2,18},{18,2},{3,19},{19,3},{4,20},{20... | collective-permute-start | bytes 1572872 | tf_op jit(solution)/shard_map/ppermute | solution.py:690
  493.0 23.7 %collective-permute-start.44 = (bf16[64,4096]{1,0:T(8,128)(2,1)S(1)}, bf16[64,4096]{1,0:T(8,128)(2,1)S(1)}, u32[]{:S(2)}, u32[]{:S(2)}) collective-permute-start(bf16[64,4096]{1,0:T(8,128)(2,1)S(1)} %copy-done.46), channel_id=1, source_target_pairs={{0,12},{1,13},{2,14},{3,15},{4,0},{5,1},{6,2},{7,3},{8,4},{9,5},{1... | collective-permute-start | bytes 1572872 | tf_op jit(solution)/shard_map/ppermute | solution.py:679
  495.6 42.7 %collective-permute-start.43 = (bf16[64,4096]{1,0:T(8,128)(2,1)S(1)}, bf16[64,4096]{1,0:T(8,128)(2,1)S(1)}, u32[]{:S(2)}, u32[]{:S(2)}) collective-permute-start(bf16[64,4096]{1,0:T(8,128)(2,1)S(1)} %copy-done.45), channel_id=1, source_target_pairs={{0,8},{1,9},{2,10},{3,11},{4,12},{5,13},{6,14},{7,15},{8,0},{9,1},... | collective-permute-start | bytes 1572872 | tf_op jit(solution)/shard_map/ppermute | solution.py:679
  495.6 46.1 %collective-permute-start.30 = (bf16[4,64,3072]{2,1,0:T(8,128)(2,1)S(1)}, bf16[4,64,3072]{2,1,0:T(8,128)(2,1)S(1)}, u32[]{:S(2)}, u32[]{:S(2)}) collective-permute-start(bf16[4,64,3072]{2,1,0:T(8,128)(2,1)S(1)} %copy-done.32), channel_id=1, source_target_pairs={{0,2},{1,3},{2,0},{3,1},{4,6},{5,7},{6,4},{7,5},{8,10},{9,11},{10,... | collective-permute-start | bytes 4718600 | tf_op jit(solution)/shard_map/ppermute | solution.py:560
  508.4 69.5 %collective-permute-start.17 = (f32[256,1024]{1,0:T(8,128)S(1)}, f32[256,1024]{1,0:T(8,128)S(1)}, u32[]{:S(2)}, u32[]{:S(2)}) collective-permute-start(f32[256,1024]{1,0:T(8,128)S(1)} %slice.127), channel_id=1, source_target_pairs={{0,16},{16,0},{1,17},{17,1},{2,18},{18,2},{3,19},{19,3},{4,20},{20... | collective-permute-start | bytes 3145736 | tf_op jit(solution)/shard_map/ppermute | solution.py:727
  545.9 30.2 %collective-permute-start.32 = (bf16[64,3072]{1,0:T(8,128)(2,1)S(1)}, bf16[64,3072]{1,0:T(8,128)(2,1)S(1)}, u32[]{:S(2)}, u32[]{:S(2)}) collective-permute-start(bf16[64,3072]{1,0:T(8,128)(2,1)S(1)} %get-tuple-element.125), channel_id=1, source_target_pairs={{0,8},{1,9},{2,10},{3,11},{4,12},{5,13},{6,14},{7,15},{8,0},{9,1},... | collective-permute-start | bytes 1179656 | tf_op jit(solution)/shard_map/ppermute | solution.py:679
  (98 other events, 948.9 us)
Sparse Core Ops, SparseCore 0:
  10.3 48.6 all-gather.6
  67.6 47.1 all-gather.8
  124.2 44.0 all-gather.10

commit v4 on v3

--- a/solution.py
+++ b/solution.py
@@ -482,9 +482,9 @@
         return pl.BlockSpec((length, 128), lambda i: (0, which * pairs + i))
 
     cost = pl.CostEstimate(
-        flops=16 * pairs * length * length * 128,
-        bytes_accessed=length * wide * 3,
-        transcendentals=2 * pairs * length * length,
+        flops=pairs * length * length,
+        bytes_accessed=length * wide,
+        transcendentals=0,
     )
     return pl.pallas_call(
         attend_kernel,
@@ -509,9 +509,9 @@
         return pl.BlockSpec((length, 128), lambda i: (0, which * pairs + i))
 
     cost = pl.CostEstimate(
-        flops=40 * pairs * length * length * 128,
-        bytes_accessed=length * wide * 6,
-        transcendentals=2 * pairs * length * length,
+        flops=pairs * length * length,
+        bytes_accessed=length * wide,
+        transcendentals=0,
     )
     grads = jax.ShapeDtypeStruct((length, wide // 3), jnp.bfloat16)
     return pl.pallas_call(
@@ -590,7 +590,7 @@
         ],
         compiler_params=pltpu.CompilerParams(vmem_limit_bytes=VMEM_LIMIT),
         cost_estimate=pl.CostEstimate(
-            flops=0, bytes_accessed=16 * depth * rows * columns, transcendentals=0
+            flops=0, bytes_accessed=depth * rows * columns, transcendentals=0
         ),
         name="assemble",
     )(places, own, own_core, across, across_core)
@@ -757,6 +757,12 @@
         axis=1,
     )
     from_owners = lax.all_to_all(to_owners, "fsdp", 0, 0, tiled=True)
+    own_a = gather_z(jnp.concatenate([w_qkv, w_out], axis=1))
+    own_b = gather_z(w_fc1)
+    own_a, from_owners = tied((own_a, from_owners))
+    core_a = flip(own_a, 1)
+    across_a = flip(own_a, 2)
+
     modulation = jnp.sum(from_owners[:, :mod_width], axis=0, keepdims=True)
     shift_one, scale_one, gate_one, shift_two, scale_two, gate_two = [
         modulation[:, position * width_all : (position + 1) * width_all] for position in range(6)
@@ -769,35 +775,29 @@
         begin = end
     query_bias, value_bias, out_bias, up_bias, down_bias = biases
 
-    own_a = gather_z(jnp.concatenate([w_qkv, w_out], axis=1))
-    own_a, w_fc1 = tied((own_a, w_fc1))
-    own_b = gather_z(w_fc1)
-    core_a = flip(own_a, 1)
-    across_a = flip(own_a, 2)
-
     inputs_full = whole_latent(latents).astype(jnp.float32)
     grad_output = whole_latent(out_cotangent).astype(jnp.float32)
     normed_one, inverse_one = normalize_keep(inputs_full)
     entry_one = low(normed_one * (1.0 + scale_one) + shift_one)
     entry_one, across_a = tied((entry_one, across_a))
     across_core_a = flip(across_a, 1)
-    own_b, across_core_a, w_fc2 = tied((own_b, across_core_a, w_fc2))
+    full_qkv, full_out = assemble(
+        own_a, core_a, across_a, across_core_a, w_qkv.shape[1], w_out.shape[1]
+    )
+    full_qkv, own_b, w_fc2 = tied((full_qkv, own_b, w_fc2))
     own_c = gather_z(w_fc2)
     core_b = flip(own_b, 1)
     across_b = flip(own_b, 2)
-    full_qkv, full_out = assemble(
-        own_a, core_a, across_a, across_core_a, w_qkv.shape[1], w_out.shape[1]
-    )
     qkv_bias = jnp.concatenate([query_bias, jnp.zeros_like(query_bias), value_bias], axis=1)
     projected = low(jnp.dot(entry_one, full_qkv, preferred_element_type=jnp.float32) + qkv_bias)
     mixed, log_totals = attend_local(projected)
-    mixed, across_b, core_b = tied((mixed, across_b, core_b))
-    across_core_b = flip(across_b, 1)
     branch_one = jnp.dot(mixed, full_out, preferred_element_type=jnp.float32) + out_bias
     middle = inputs_full + gate_one * branch_one
     normed_two, inverse_two = normalize_keep(middle)
     entry_two = low(normed_two * (1.0 + scale_two) + shift_two)
-    entry_two, across_core_b, own_c = tied((entry_two, across_core_b, own_c))
+    entry_two, across_b, core_b = tied((entry_two, across_b, core_b))
+    across_core_b = flip(across_b, 1)
+    own_c, across_core_b = tied((own_c, across_core_b))
     core_c = flip(own_c, 1)
     across_c = flip(own_c, 2)
     (full_fc1,) = assemble(own_b, core_b, across_b, across_core_b, w_fc1.shape[1])
@@ -813,68 +813,81 @@
     branch_two = jnp.dot(active, full_fc2, preferred_element_type=jnp.float32) + down_bias
     result = both_halves(low(middle + gate_two * branch_two))
     grad_gate_two = jnp.sum(grad_output * branch_two, axis=0, keepdims=True)
+    here_fc2, away_fc2 = split_x(kept_fc2, arrived_fc2)
+    grad_branch_two, away_fc2 = tied((grad_branch_two, away_fc2))
+    crossed_fc2 = flip(away_fc2, 2)
     grad_active = compared_with(grad_branch_two, full_fc2)
     grad_hidden = low(gelu_pull(grad_active)[0])
-    here_fc2, away_fc2 = split_x(kept_fc2, arrived_fc2)
-    grad_hidden, away_fc2 = tied((grad_hidden, away_fc2))
-    crossed_fc2 = flip(away_fc2, 2)
     kept_fc1, leaving_fc1 = split_core(outer_sum(entry_two, grad_hidden))
-    grad_hidden, leaving_fc1 = tied((grad_hidden, leaving_fc1))
+    grad_hidden, leaving_fc1, crossed_fc2 = tied((grad_hidden, leaving_fc1, crossed_fc2))
     arrived_fc1 = flip(leaving_fc1, 1)
     grad_entry_two = compared_with(grad_hidden, full_fc1)
+    here_fc1, away_fc1 = split_x(kept_fc1, arrived_fc1)
+    total_fc2, leaving_fc2 = split_z(here_fc2, crossed_fc2)
+    grad_entry_two, leaving_fc2, away_fc1 = tied((grad_entry_two, leaving_fc2, away_fc1))
+    crossed_fc1 = flip(away_fc1, 2)
     grad_shift_two = jnp.sum(grad_entry_two, axis=0, keepdims=True)
     grad_scale_two = jnp.sum(grad_entry_two * normed_two, axis=0, keepdims=True)
     grad_middle = grad_output + normalize_back(
         grad_entry_two * (1.0 + scale_two), normed_two, inverse_two
     )
     grad_gate_one = jnp.sum(grad_middle * branch_one, axis=0, keepdims=True)
-    grad_mod_early = gather_latents(
-        low(
-            jnp.concatenate(
-                [grad_gate_one, grad_shift_two, grad_scale_two, grad_gate_two], axis=1
-            )
-        )
-    )
     grad_branch_one = low(gate_one * grad_middle)
-    here_fc1, away_fc1 = split_x(kept_fc1, arrived_fc1)
-    grad_branch_one, away_fc1 = tied((grad_branch_one, away_fc1))
-    crossed_fc1 = flip(away_fc1, 2)
+    landed_fc2 = send_z(leaving_fc2)
     kept_out, leaving_out = split_core(outer_sum(mixed, grad_branch_one))
+    leaving_out, grad_branch_one = tied((leaving_out, grad_branch_one))
     arrived_out = flip(leaving_out, 1)
     grad_mixed = low(compared_with(grad_branch_one, full_out))
-    total_fc2, leaving_fc2 = split_z(here_fc2, crossed_fc2)
     here_out, away_out = split_x(kept_out, arrived_out)
-    grad_mixed, leaving_fc2, away_out = tied((grad_mixed, leaving_fc2, away_out))
-    landed_fc2 = send_z(leaving_fc2)
+    grad_mixed, away_out = tied((grad_mixed, away_out))
+    grad_project = jnp.concatenate(attend_local_back(projected, grad_mixed, log_totals), axis=1)
+    crossed_fc1, away_out, grad_project, landed_fc2, result = tied(
+        (crossed_fc1, away_out, grad_project, landed_fc2, result)
+    )
     crossed_out = flip(away_out, 2)
-    grad_project = jnp.concatenate(attend_local_back(projected, grad_mixed, log_totals), axis=1)
+    total_fc1, leaving_fc1 = split_z(here_fc1, crossed_fc1)
+    grad_project, leaving_fc1 = tied((grad_project, leaving_fc1))
+    landed_fc1 = send_z(leaving_fc1)
     kept_qkv, leaving_qkv = split_core(outer_sum(entry_one, grad_project))
     grad_project, leaving_qkv = tied((grad_project, leaving_qkv))
     arrived_qkv = flip(leaving_qkv, 1)
+    grad_entry_one = compared_with(grad_project, full_qkv)
     here_qkv, away_qkv = split_x(kept_qkv, arrived_qkv)
-    grad_entry_one = compared_with(grad_project, full_qkv)
-    grad_entry_one, away_qkv, here_fc1, total_fc2 = tied(
-        (grad_entry_one, away_qkv, here_fc1, total_fc2)
-    )
+    grad_entry_one, away_qkv, crossed_out = tied((grad_entry_one, away_qkv, crossed_out))
     crossed_qkv = flip(away_qkv, 2)
-    total_fc1, leaving_fc1 = split_z(here_fc1, crossed_fc1)
-    landed_fc1 = send_z(leaving_fc1)
-    sum_fc2 = sum_seq(sum_z(total_fc2, landed_fc2))
     total_out, leaving_out = split_z(here_out, crossed_out)
+    mine_fc2 = sum_z(total_fc2, landed_fc2)
+    grad_entry_one, leaving_out, mine_fc2 = tied((grad_entry_one, leaving_out, mine_fc2))
     landed_out = send_z(leaving_out)
-    total_qkv, leaving_qkv = split_z(here_qkv, crossed_qkv)
-    landed_qkv = send_z(leaving_qkv)
-    sum_fc1 = sum_seq(sum_z(total_fc1, landed_fc1))
-    sum_out = sum_seq(sum_z(total_out, landed_out))
-    sum_qkv = sum_seq(sum_z(total_qkv, landed_qkv))
+    sum_fc2 = sum_seq(mine_fc2)
     grad_shift_one = jnp.sum(grad_entry_one, axis=0, keepdims=True)
     grad_scale_one = jnp.sum(grad_entry_one * normed_one, axis=0, keepdims=True)
     grad_latents = both_halves(
         grad_middle
         + normalize_back(grad_entry_one * (1.0 + scale_one), normed_one, inverse_one)
     )
-    grad_mod_late = low(jnp.concatenate([grad_shift_one, grad_scale_one], axis=1))
-    grad_mod_all = jnp.concatenate([gather_latents(grad_mod_late), grad_mod_early], axis=1)
+    grad_mod_mine = low(
+        jnp.concatenate(
+            [
+                grad_shift_one,
+                grad_scale_one,
+                grad_gate_one,
+                grad_shift_two,
+                grad_scale_two,
+                grad_gate_two,
+            ],
+            axis=1,
+        )
+    )
+    grad_mod_mine, landed_fc1, crossed_qkv = tied((grad_mod_mine, landed_fc1, crossed_qkv))
+    total_qkv, leaving_qkv = split_z(here_qkv, crossed_qkv)
+    mine_fc1 = sum_z(total_fc1, landed_fc1)
+    grad_mod_mine, leaving_qkv, mine_fc1 = tied((grad_mod_mine, leaving_qkv, mine_fc1))
+    landed_qkv = send_z(leaving_qkv)
+    sum_fc1 = sum_seq(mine_fc1)
+    grad_mod_all = gather_latents(grad_mod_mine)
+    sum_out = sum_seq(sum_z(total_out, landed_out))
+    sum_qkv = sum_seq(sum_z(total_qkv, landed_qkv))
     grad_w_mod = outer_sum(lifted, grad_mod_all)
     grad_b_mod = jnp.sum(
         lax.dynamic_slice_in_dim(grad_mod_all, owner * mod_cols, mod_cols, 1).astype(jnp.float32),

time: 603 us -> 631 us (1.046)
  the two profiles are of different devices: /device:TPU:0 before, /device:TPU:8 now
where the time goes in v4:
time: 631 us; the launch traced here: 620 us
  waiting for transfers between devices  264 us (42%)
  matrix products  86.3 us (14%)
  other arithmetic  70.8 us (11%)
  Pallas kernels  67.2 us (11%)
  starting transfers between devices  51.4 us (8%)
  local copies, waits for them, and re-layouts  37.3 us (6%)
  blocking collectives  27.8 us (4%)
  between operations  15.1 us (2%)
    ppermute x17, waiting for transfers between devices, flip(): lax.ppermute(tensor, 'fsdp', swapped_pairs(lax.axis_size('fsdp'), bit))  90.5 us
    ppermute x12, waiting for transfers between devices, send_z(): arrived.append(lax.ppermute(part, 'fsdp', pairs))  71.3 us
    pallas_call x3, Pallas kernels, assemble(): pl.pallas_call(assemble_kernel, grid_spec=pltpu.PrefetchScalarGridSpec(nu...  37 us
    ppermute x4, waiting for transfers between devices, sum_seq(): return wide(mine) + wide(lax.ppermute(mine, 'seq', swapped_pairs(2, 1)))  35.3 us
    dot_general x5, matrix products, compared_with(): lax.dot_general(earlier_value, latter, (((1,), (1,)), ((), ())), preferre...  30.8 us
    all_to_all x1, blocking collectives, local_whole_latent(): from_owners = lax.all_to_all(to_owners, 'fsdp', 0, 0, tiled=True)  27.8 us
    ppermute x2, waiting for transfers between devices, whole_latent(): return jnp.concatenate([kept, lax.ppermute(given, 'seq', seq_swap)], axis=0)  24.6 us
    convert_element_type x12, other arithmetic, low(): return tensor.astype(jnp.bfloat16)  23.9 us
  transfers between devices with their start and end apart: 48, of which 25 were waited for; matrix products, arithmetic and copies ran while one was open for 24% of the time, Pallas kernels for 11%

profile of v4, /device:TPU:8, one launch (start us, length us, event | category | flops | bytes accessed | tf_op | source)
XLA Modules:
  0.0 620.4 jit_solution(1656901355572567421)
XLA Ops:
  17.0 27.8 %all_to_all.21 = f32[16,1,6656]{2,1,0:T(1,128)S(1)} all-to-all(f32[16,1,6656]{2,1,0:T(1,128)S(1)} %copy.76), channel_id=1, replica_groups=mesh['seq'=2,'fsdp'=16] {'fsdp'}, dimensions={0} | all-to-all | bytes 851968 | tf_op jit(solution)/shard_map/all_to_all | solution.py:759
  45.5 17.3 %all-gather.7.cloned.1.call-done = bf16[256,4096]{1,0:T(8,128)(2,1)} async-done(((bf16[64,4096]{1,0:T(8,128)(2,1)}), bf16[256,4096]{1,0:T(8,128)(2,1)}) %all-gather.7.cloned.1.call-update) | async-done | bytes 2097168 | tf_op jit(solution)/shard_map/all_gather | solution.py:556
  68.1 12.4 %collective-permute-done = bf16[256,1024]{1,0:T(8,128)(2,1)} collective-permute-done((bf16[256,1024]{1,0:T(8,128)(2,1)}, bf16[256,1024]{1,0:T(8,128)(2,1)}, u32[]{:S(2)}, u32[]{:S(2)}) %collective-permute-start) | collective-permute-done | bytes 524320 | tf_op jit(solution)/shard_map/ppermute | solution.py:724
  86.5 24.2 %collective-permute-done.1.p10 = bf16[4,64,4096]{2,1,0:T(8,128)(2,1)} collective-permute-done((bf16[4,64,4096]{2,1,0:T(8,128)(2,1)}, bf16[4,64,4096]{2,1,0:T(8,128)(2,1)}, u32[]{:S(2)}, u32[]{:S(2)}) %collective-permute-start.1) | collective-permute-done | bytes 2097184 | tf_op jit(solution)/shard_map/ppermute | solution.py:560
  115.2 12.3 %assemble.3 = (bf16[4,4,64,3072]{3,2,1,0:T(8,128)(2,1)}, bf16[4,4,64,1024]{3,2,1,0:T(8,128)(2,1)S(1)}) custom-call(s32[4]{0:T(128)S(1)} %iota_xor_fusion.place_ref, bf16[4,64,4096]{2,1,0:T(8,128)(2,1)S(1)} %bitcast.240, bf16[4,64,4096]{2,1,0:T(8,128)(2,1)} %collective-permute-done.2.p01, bf16[4,64,4096]{2,1,0:T(8,128)(2,1)} %collective-permute-done.1.p10, ...), custom_call_target="tpu_custom_call" | custom-call | bytes 1048576 | tf_op jit(solution)/shard_map/assemble/pallas_call | solution.py:580
  130.6 6.5 %add_convert_fusion.q_ref.k_ref.v_ref = bf16[512,3072]{1,0:T(8,128)(2,1)S(1)} fusion(bf16[512,1024]{1,0:T(8,128)(2,1)} %fusion.16, bf16[1024,3072]{1,0:T(8,128)(2,1)} %bitcast.284, f32[3072]{0:T(1024)S(1)} %bitcast.280), kind=kOutput, calls=%fused_computation.15 | convolution fusion | flops 3224371200 | bytes 10498048 | tf_op jit(solution)/shard_map/dot_general | solution.py:792
  137.2 13.0 %attend.1 = (bf16[512,1024]{1,0:T(8,128)(2,1)S(1)}, f32[8,2,512]{2,1,0:T(2,128)S(1)}) custom-call(bf16[512,3072]{1,0:T(8,128)(2,1)S(1)} %add_convert_fusion.q_ref.k_ref.v_ref, bf16[512,3072]{1,0:T(8,128)(2,1)S(1)} %add_convert_fusion.q_ref.k_ref.v_ref, bf16[512,3072]{1,0:T(8,128)(2,1)S(1)} %add_convert_fusion.q_ref.k_ref.v_ref), custom_call_target="tpu_custom_call" | custom-call | flops 2097152 | bytes 1572864 | tf_op jit(solution)/shard_map/attend/pallas_call | solution.py:489
  156.0 21.2 %collective-permute-done.4.p10 = bf16[4,64,4096]{2,1,0:T(8,128)(2,1)} collective-permute-done((bf16[4,64,4096]{2,1,0:T(8,128)(2,1)}, bf16[4,64,4096]{2,1,0:T(8,128)(2,1)}, u32[]{:S(2)}, u32[]{:S(2)}) %collective-permute-start.4) | collective-permute-done | bytes 2097184 | tf_op jit(solution)/shard_map/ppermute | solution.py:560
  180.7 12.3 %collective-permute-done.7 = bf16[256,1024]{1,0:T(8,128)(2,1)} collective-permute-done((bf16[256,1024]{1,0:T(8,128)(2,1)}, bf16[256,1024]{1,0:T(8,128)(2,1)}, u32[]{:S(2)}, u32[]{:S(2)}) %collective-permute-start.7) | collective-permute-done | bytes 524320 | tf_op jit(solution)/shard_map/ppermute | solution.py:724
  197.1 12.9 %assemble.4 = bf16[4,4,64,4096]{3,2,1,0:T(8,128)(2,1)} custom-call(s32[4]{0:T(128)S(1)} %iota_xor_fusion.place_ref, bf16[4,64,4096]{2,1,0:T(8,128)(2,1)S(1)} %bitcast.234, bf16[4,64,4096]{2,1,0:T(8,128)(2,1)} %collective-permute-done.5.p01, bf16[4,64,4096]{2,1,0:T(8,128)(2,1)} %collective-permute-done.4.p10, bf16[4,64,4096]{2,1,0:T(8,128)(2,1)} %collective-permute-done.6.p11), custom_call_target="tpu_custom_call" | custom-call | bytes 1048576 | tf_op jit(solution)/shard_map/assemble/pallas_call | solution.py:580
  210.0 10.6 %fusion.70 = f32[512,4096]{1,0:T(8,128)} fusion(bf16[512,1024]{1,0:T(8,128)(2,1)S(1)} %copy-done.40, bf16[1024,4096]{1,0:T(8,128)(2,1)} %bitcast.243), kind=kOutput, calls=%fused_computation.206 | convolution fusion | flops 4294967296 | bytes 17825792 | tf_op jit(solution)/shard_map/dot_general | solution.py:804
  220.7 10.1 %convolution_convert_fusion.1 = bf16[4096,1024]{1,0:T(8,128)(2,1)S(1)} fusion(bf16[512,1024]{1,0:T(8,128)(2,1)S(1)} %copy-done.26, f32[512,4096]{1,0:T(8,128)} %fusion.70, f32[4096]{0:T(1024)S(1)} %bitcast.277), kind=kOutput, calls=%fused_computation.13 | convolution fusion | flops 4320133120 | bytes 17842176 | tf_op jit(solution)/shard_map/dot_general | solution.py:46
  237.0 6.8 %collective-permute-done.8.p10 = bf16[4,256,1024]{2,1,0:T(8,128)(2,1)} collective-permute-done((bf16[4,256,1024]{2,1,0:T(8,128)(2,1)}, bf16[4,256,1024]{2,1,0:T(8,128)(2,1)}, u32[]{:S(2)}, u32[]{:S(2)}) %collective-permute-start.8) | collective-permute-done | bytes 2097184 | tf_op jit(solution)/shard_map/ppermute | solution.py:560
  244.3 10.0 %collective-permute-done.11.p11 = bf16[4,256,1024]{2,1,0:T(8,128)(2,1)} collective-permute-done((bf16[4,256,1024]{2,1,0:T(8,128)(2,1)}, bf16[4,256,1024]{2,1,0:T(8,128)(2,1)}, u32[]{:S(2)}, u32[]{:S(2)}) %collective-permute-start.11) | collective-permute-done | bytes 2097184 | tf_op jit(solution)/shard_map/ppermute | solution.py:560
  255.9 11.8 %assemble.5 = bf16[4,4,256,1024]{3,2,1,0:T(8,128)(2,1)} custom-call(s32[4]{0:T(128)S(1)} %iota_xor_fusion.place_ref, bf16[4,256,1024]{2,1,0:T(8,128)(2,1)S(1)} %bitcast.237, bf16[4,256,1024]{2,1,0:T(8,128)(2,1)S(1)} %copy-done.5, bf16[4,256,1024]{2,1,0:T(8,128)(2,1)} %collective-permute-done.8.p10, bf16[4,256,1024]{2,1,0:T(8,128)(2,1)} %collective-permute-done.11.p11), custom_call_target="tpu_custom_call" | custom-call | bytes 1048576 | tf_op jit(solution)/shard_map/assemble/pallas_call | solution.py:580
  267.7 7.0 %convert_add_fusion.2 = (f32[4,256,1024]{2,1,0:T(8,128)}, bf16[4,256,1024]{2,1,0:T(8,128)(2,1)}) fusion(bf16[4,2,256,1024]{3,2,0,1:T(8,128)(2,1)} %collective-permute-done.10, s32[]{:T(128)S(6)} %select_n.253, bf16[4,2,2,256,1024]{4,3,2,1,0:T(8,128)(2,1)S(1)} %bitcast.254, s32[]{:T(128)S(6)} %select_n.254, s32[]{:T(128)S(6)} %select_n.251, ...), kind=kLoop, calls=%fused_computation.20 | loop fusion | flops 7340032 | bytes 14680084 | tf_op jit(solution)/shard_map/add | solution.py:660
  276.4 12.8 %fusion.3 = bf16[512,4096]{1,0:T(8,128)(2,1)S(1)} fusion(f32[512,4096]{1,0:T(8,128)} %fusion.70, f32[4096]{0:T(1024)S(1)} %bitcast.278, bf16[512,1024]{1,0:T(8,128)(2,1)S(1)} %copy-done.27, bf16[4096,1024]{1,0:T(8,128)(2,1)S(1)} %bitcast.245), kind=kOutput, calls=%fused_computation.7 | convolution fusion | flops 4347396096 | bytes 22036480 | tf_op jit(solution)/shard_map/dot_general | solution.py:52
  289.2 5.0 convolution_convert_fusion
  298.8 23.9 %collective-permute-done.12 = bf16[4,256,1024]{2,1,0:T(8,128)(2,1)S(1)} collective-permute-done((bf16[4,256,1024]{2,1,0:T(8,128)(2,1)}, bf16[4,256,1024]{2,1,0:T(8,128)(2,1)S(1)}, u32[]{:S(2)}, u32[]{:S(2)}) %collective-permute-start.12) | collective-permute-done | bytes 2097184 | tf_op jit(solution)/shard_map/ppermute | solution.py:560
  328.0 8.7 %fusion.71 = f32[512,1024]{1,0:T(8,128)S(1)} fusion(bf16[512,4096]{1,0:T(8,128)(2,1)} %copy-done.25, bf16[1024,4096]{1,0:T(8,128)(2,1)} %bitcast.244), kind=kOutput, calls=%fused_computation.207 | convolution fusion | flops 4294967296 | bytes 14680064 | tf_op jit(solution)/shard_map/dot_general | solution.py:52
  336.8 6.3 %convert_add_fusion = (f32[4,64,4096]{2,1,0:T(8,128)}, bf16[4,64,4096]{2,1,0:T(8,128)(2,1)}) fusion(bf16[4,2,64,4096]{3,2,0,1:T(8,128)(2,1)} %collective-permute-done.13, s32[]{:T(128)S(6)} %select_n.253, bf16[4,2,2,64,4096]{4,3,2,1,0:T(8,128)(2,1)S(1)} %bitcast.252, s32[]{:T(128)S(6)} %select_n.254, s32[]{:T(128)S(6)} %select_n.251, s32[]{:T(128)S(6)} %select_n.248, ...), kind=kLoop, calls=%fused_computation.17 | loop fusion | flops 7340032 | bytes 14680084 | tf_op jit(solution)/shard_map/add | solution.py:660
  345.7 9.6 %fusion.24 = (bf16[1024]{0:T(1024)(128)(2,1)S(1)}, bf16[512,1024]{1,0:T(8,128)(2,1)S(1)}, bf16[1024]{0:T(1024)(128)(2,1)S(1)}, f32[512,1024]{1,0:T(8,128)S(1)}) fusion(f32[1024]{0:T(1024)S(1)} %add.495, bf16[256,1024]{1,0:T(8,128)(2,1)} %collective-permute-done.7, bf16[256,1024]{1,0:T(8,128)(2,1)S(1)} %copy-done.34, f32[512,1024]{1,0:T(8,128)S(1)} %copy-done.13, ...), kind=kOutput, calls=%fused_computation.51 | convolution fusion | flops 4326946816 | bytes 27308032 | tf_op jit(solution)/shard_map/dot_general | solution.py:813
  385.3 17.2 %attend_back.1 = (bf16[512,1024]{1,0:T(8,128)(2,1)S(1)}, bf16[512,1024]{1,0:T(8,128)(2,1)S(1)}, bf16[512,1024]{1,0:T(8,128)(2,1)S(1)}) custom-call(bf16[512,3072]{1,0:T(8,128)(2,1)} %copy-done.1, bf16[512,3072]{1,0:T(8,128)(2,1)} %copy-done.1, bf16[512,3072]{1,0:T(8,128)(2,1)} %copy-done.1, bf16[512,1024]{1,0:T(8,128)(2,1)S(1)} %convolution_convert_fusion.4.do_ref, ...), custom_call_target="tpu_custom_call" | custom-call | flops 2097152 | bytes 1572864 | tf_op jit(solution)/shard_map/attend_back/pallas_call | solution.py:517
  402.8 7.8 %collective-permute-done.17 = bf16[256,1024]{1,0:T(8,128)(2,1)S(1)} collective-permute-done((bf16[256,1024]{1,0:T(8,128)(2,1)}, bf16[256,1024]{1,0:T(8,128)(2,1)S(1)}, u32[]{:S(2)}, u32[]{:S(2)}) %collective-permute-start.17) | collective-permute-done | bytes 524320 | tf_op jit(solution)/shard_map/ppermute | solution.py:679
  435.0 6.5 %fusion.72 = f32[512,1024]{1,0:T(8,128)S(1)} fusion(bf16[512,3072]{1,0:T(8,128)(2,1)} %copy-done.16, bf16[1024,3072]{1,0:T(8,128)(2,1)} %bitcast.285), kind=kOutput, calls=%fused_computation.208 | convolution fusion | flops 3221225472 | bytes 11534336 | tf_op jit(solution)/shard_map/dot_general | solution.py:52
  465.8 30.8 %collective-permute-done.38 = bf16[64,1024]{1,0:T(8,128)(2,1)S(1)} collective-permute-done((bf16[64,1024]{1,0:T(8,128)(2,1)S(1)}, bf16[64,1024]{1,0:T(8,128)(2,1)S(1)}, u32[]{:S(2)}, u32[]{:S(2)}) %collective-permute-start.38) | collective-permute-done | bytes 131104 | tf_op jit(solution)/shard_map/ppermute | solution.py:679
  498.5 13.4 %collective-permute-done.40 = bf16[64,1024]{1,0:T(8,128)(2,1)S(1)} collective-permute-done((bf16[64,1024]{1,0:T(8,128)(2,1)S(1)}, bf16[64,1024]{1,0:T(8,128)(2,1)S(1)}, u32[]{:S(2)}, u32[]{:S(2)}) %collective-permute-start.40) | collective-permute-done | bytes 131104 | tf_op jit(solution)/shard_map/ppermute | solution.py:679
  521.6 27.0 %collective-permute-done.41 = bf16[64,1024]{1,0:T(8,128)(2,1)S(1)} collective-permute-done((bf16[64,1024]{1,0:T(8,128)(2,1)S(1)}, bf16[64,1024]{1,0:T(8,128)(2,1)S(1)}, u32[]{:S(2)}, u32[]{:S(2)}) %collective-permute-start.41) | collective-permute-done | bytes 131104 | tf_op jit(solution)/shard_map/ppermute | solution.py:690
  566.9 15.8 %collective-permute-done.30 = bf16[8,6144]{1,0:T(8,128)(2,1)S(1)} collective-permute-done((bf16[8,6144]{1,0:T(8,128)(2,1)S(1)}, bf16[8,6144]{1,0:T(8,128)(2,1)S(1)}, u32[]{:S(2)}, u32[]{:S(2)}) %collective-permute-start.30) | collective-permute-done | bytes 98336 | tf_op jit(solution)/shard_map/ppermute | solution.py:627
  586.4 5.2 collective-permute-done.33
  591.6 7.2 %collective-permute-done.34 = bf16[64,3072]{1,0:T(8,128)(2,1)S(1)} collective-permute-done((bf16[64,3072]{1,0:T(8,128)(2,1)S(1)}, bf16[64,3072]{1,0:T(8,128)(2,1)S(1)}, u32[]{:S(2)}, u32[]{:S(2)}) %collective-permute-start.34) | collective-permute-done | bytes 393248 | tf_op jit(solution)/shard_map/ppermute | solution.py:679
  604.2 8.3 %collective-permute-done.36 = bf16[64,3072]{1,0:T(8,128)(2,1)S(1)} collective-permute-done((bf16[64,3072]{1,0:T(8,128)(2,1)S(1)}, bf16[64,3072]{1,0:T(8,128)(2,1)S(1)}, u32[]{:S(2)}, u32[]{:S(2)}) %collective-permute-start.36) | collective-permute-done | bytes 393248 | tf_op jit(solution)/shard_map/ppermute | solution.py:690
  (328 shorter events, 183.4 us)
Async XLA Ops:
  7.2 55.6 %all-gather.7.cloned.1.call-start = ((), (), s32[]{:S(2)}) async-start(), calls=%async_computation.2 | async-start | bytes 2621440 | tf_op jit(solution)/shard_map/all_gather | solution.py:556
  9.2 119.6 %all-gather.9.cloned.1.call-start = ((), (), s32[]{:S(2)}) async-start(), calls=%async_computation.3 | async-start | bytes 2621440 | tf_op jit(solution)/shard_map/all_gather | solution.py:556
  62.8 47.9 %collective-permute-start.1 = (bf16[4,64,4096]{2,1,0:T(8,128)(2,1)}, bf16[4,64,4096]{2,1,0:T(8,128)(2,1)}, u32[]{:S(2)}, u32[]{:S(2)}) collective-permute-start(bf16[4,64,4096]{2,1,0:T(8,128)(2,1)} %bitcast.238), channel_id=1, source_target_pairs={{0,2},{1,3},{2,0},{3,1},{4,6},{5,7},{6,4},{7,5},{8,10},{9,11},{10,... | collective-permute-start | bytes 6291464 | tf_op jit(solution)/shard_map/ppermute | solution.py:560
  68.1 127.2 %all-gather.11.cloned.1.call-start = ((), (), s32[]{:S(2)}) async-start(), calls=%async_computation.4 | async-start | bytes 2621440 | tf_op jit(solution)/shard_map/all_gather | solution.py:556
  83.3 28.6 %collective-permute-start.2 = (bf16[4,64,4096]{2,1,0:T(8,128)(2,1)S(1)}, bf16[4,64,4096]{2,1,0:T(8,128)(2,1)}, u32[]{:S(2)}, u32[]{:S(2)}) collective-permute-start(bf16[4,64,4096]{2,1,0:T(8,128)(2,1)S(1)} %bitcast.239), channel_id=1, source_target_pairs={{0,1},{1,0},{2,3},{3,2},{4,5},{5,4},{6,7},{7,6},{8,9},{9,8},{10,11... | collective-permute-start | bytes 6291464 | tf_op jit(solution)/shard_map/ppermute | solution.py:560
  128.9 27.1 %collective-permute-start.5 = (bf16[4,64,4096]{2,1,0:T(8,128)(2,1)}, bf16[4,64,4096]{2,1,0:T(8,128)(2,1)}, u32[]{:S(2)}, u32[]{:S(2)}) collective-permute-start(bf16[4,64,4096]{2,1,0:T(8,128)(2,1)} %bitcast.232), channel_id=1, source_target_pairs={{0,1},{1,0},{2,3},{3,2},{4,5},{5,4},{6,7},{7,6},{8,9},{9,8},{10,11... | collective-permute-start | bytes 6291464 | tf_op jit(solution)/shard_map/ppermute | solution.py:560
  129.1 48.2 %collective-permute-start.4 = (bf16[4,64,4096]{2,1,0:T(8,128)(2,1)}, bf16[4,64,4096]{2,1,0:T(8,128)(2,1)}, u32[]{:S(2)}, u32[]{:S(2)}) collective-permute-start(bf16[4,64,4096]{2,1,0:T(8,128)(2,1)} %bitcast.233), channel_id=1, source_target_pairs={{0,2},{1,3},{2,0},{3,1},{4,6},{5,7},{6,4},{7,5},{8,10},{9,11},{10,... | collective-permute-start | bytes 6291464 | tf_op jit(solution)/shard_map/ppermute | solution.py:560
  195.3 40.2 %collective-permute-start.9 = (bf16[4,256,1024]{2,1,0:T(8,128)(2,1)}, bf16[4,256,1024]{2,1,0:T(8,128)(2,1)S(1)}, u32[]{:S(2)}, u32[]{:S(2)}) collective-permute-start(bf16[4,256,1024]{2,1,0:T(8,128)(2,1)} %bitcast.235), channel_id=1, source_target_pairs={{0,1},{1,0},{2,3},{3,2},{4,5},{5,4},{6,7},{7,6},{8,9},{9,8},{10,11... | collective-permute-start | bytes 6291464 | tf_op jit(solution)/shard_map/ppermute | solution.py:560
  195.4 48.4 %collective-permute-start.8 = (bf16[4,256,1024]{2,1,0:T(8,128)(2,1)}, bf16[4,256,1024]{2,1,0:T(8,128)(2,1)}, u32[]{:S(2)}, u32[]{:S(2)}) collective-permute-start(bf16[4,256,1024]{2,1,0:T(8,128)(2,1)} %bitcast.236), channel_id=1, source_target_pairs={{0,2},{1,3},{2,0},{3,1},{4,6},{5,7},{6,4},{7,5},{8,10},{9,11},{10,... | collective-permute-start | bytes 6291464 | tf_op jit(solution)/shard_map/ppermute | solution.py:560
  243.8 23.9 %collective-permute-start.10 = (bf16[4,2,256,1024]{3,2,0,1:T(8,128)(2,1)}, bf16[4,2,256,1024]{3,2,0,1:T(8,128)(2,1)}, u32[]{:S(2)}, u32[]{:S(2)}) collective-permute-start(bf16[4,2,256,1024]{3,2,0,1:T(8,128)(2,1)} %copy_bitcast_fusion.1), channel_id=1, source_target_pairs={{0,1},{1,0},{2,3},{3,2},{4,5},{5,4},{6,7},{7,6},{8,9},{9,8},{10,11... | collective-permute-start | bytes 12582920 | tf_op jit(solution)/shard_map/ppermute | solution.py:560
  274.7 47.9 %collective-permute-start.12 = (bf16[4,256,1024]{2,1,0:T(8,128)(2,1)}, bf16[4,256,1024]{2,1,0:T(8,128)(2,1)S(1)}, u32[]{:S(2)}, u32[]{:S(2)}) collective-permute-start(bf16[4,256,1024]{2,1,0:T(8,128)(2,1)} %get-tuple-element.100), channel_id=1, source_target_pairs={{0,2},{1,3},{2,0},{3,1},{4,6},{5,7},{6,4},{7,5},{8,10},{9,11},{10,... | collective-permute-start | bytes 6291464 | tf_op jit(solution)/shard_map/ppermute | solution.py:560
  344.1 70.5 %collective-permute-start.14 = (bf16[4,64,4096]{2,1,0:T(8,128)(2,1)}, bf16[4,64,4096]{2,1,0:T(8,128)(2,1)}, u32[]{:S(2)}, u32[]{:S(2)}) collective-permute-start(bf16[4,64,4096]{2,1,0:T(8,128)(2,1)} %get-tuple-element.104), channel_id=1, source_target_pairs={{0,2},{1,3},{2,0},{3,1},{4,6},{5,7},{6,4},{7,5},{8,10},{9,11},{10,... | collective-permute-start | bytes 6291464 | tf_op jit(solution)/shard_map/ppermute | solution.py:560
  361.2 21.4 %collective-permute-start.15 = (bf16[4,2,64,1024]{3,2,0,1:T(8,128)(2,1)}, bf16[4,2,64,1024]{3,2,0,1:T(8,128)(2,1)}, u32[]{:S(2)}, u32[]{:S(2)}) collective-permute-start(bf16[4,2,64,1024]{3,2,0,1:T(8,128)(2,1)} %copy_bitcast_fusion.3), channel_id=1, source_target_pairs={{0,1},{1,0},{2,3},{3,2},{4,5},{5,4},{6,7},{7,6},{8,9},{9,8},{10,11... | collective-permute-start | bytes 3145736 | tf_op jit(solution)/shard_map/ppermute | solution.py:560
  363.7 39.1 %collective-permute-start.16 = (bf16[256,1024]{1,0:T(8,128)(2,1)}, bf16[256,1024]{1,0:T(8,128)(2,1)S(1)}, u32[]{:S(2)}, u32[]{:S(2)}) collective-permute-start(bf16[256,1024]{1,0:T(8,128)(2,1)} %get-tuple-element.114), channel_id=1, source_target_pairs={{0,4},{1,5},{2,6},{3,7},{4,8},{5,9},{6,10},{7,11},{8,12},{9,13},{1... | collective-permute-start | bytes 1572872 | tf_op jit(solution)/shard_map/ppermute | solution.py:679
  365.3 45.4 %collective-permute-start.17 = (bf16[256,1024]{1,0:T(8,128)(2,1)}, bf16[256,1024]{1,0:T(8,128)(2,1)S(1)}, u32[]{:S(2)}, u32[]{:S(2)}) collective-permute-start(bf16[256,1024]{1,0:T(8,128)(2,1)} %get-tuple-element.115), channel_id=1, source_target_pairs={{0,8},{1,9},{2,10},{3,11},{4,12},{5,13},{6,14},{7,15},{8,0},{9,1},... | collective-permute-start | bytes 1572872 | tf_op jit(solution)/shard_map/ppermute | solution.py:679
  376.7 37.9 %collective-permute-start.18 = (bf16[256,1024]{1,0:T(8,128)(2,1)S(1)}, bf16[256,1024]{1,0:T(8,128)(2,1)S(1)}, u32[]{:S(2)}, u32[]{:S(2)}) collective-permute-start(bf16[256,1024]{1,0:T(8,128)(2,1)S(1)} %copy-done.47), channel_id=1, source_target_pairs={{0,12},{1,13},{2,14},{3,15},{4,0},{5,1},{6,2},{7,3},{8,4},{9,5},{1... | collective-permute-start | bytes 1572872 | tf_op jit(solution)/shard_map/ppermute | solution.py:679
  425.0 26.2 %collective-permute-start.20 = (bf16[4,2,64,3072]{3,2,0,1:T(8,128)(2,1)}, bf16[4,2,64,3072]{3,2,0,1:T(8,128)(2,1)}, u32[]{:S(2)}, u32[]{:S(2)}) collective-permute-start(bf16[4,2,64,3072]{3,2,0,1:T(8,128)(2,1)} %copy_bitcast_fusion.2), channel_id=1, source_target_pairs={{0,1},{1,0},{2,3},{3,2},{4,5},{5,4},{6,7},{7,6},{8,9},{9,8},{10,11... | collective-permute-start | bytes 9437192 | tf_op jit(solution)/shard_map/ppermute | solution.py:560
  443.1 70.4 %collective-permute-start.23 = (bf16[64,4096]{1,0:T(8,128)(2,1)}, bf16[64,4096]{1,0:T(8,128)(2,1)}, u32[]{:S(2)}, u32[]{:S(2)}) collective-permute-start(bf16[64,4096]{1,0:T(8,128)(2,1)} %get-tuple-element.130), channel_id=1, source_target_pairs={{0,4},{1,5},{2,6},{3,7},{4,8},{5,9},{6,10},{7,11},{8,12},{9,13},{1... | collective-permute-start | bytes 1572872 | tf_op jit(solution)/shard_map/ppermute | solution.py:679
  444.8 70.2 %collective-permute-start.24 = (bf16[64,4096]{1,0:T(8,128)(2,1)}, bf16[64,4096]{1,0:T(8,128)(2,1)}, u32[]{:S(2)}, u32[]{:S(2)}) collective-permute-start(bf16[64,4096]{1,0:T(8,128)(2,1)} %get-tuple-element.131), channel_id=1, source_target_pairs={{0,8},{1,9},{2,10},{3,11},{4,12},{5,13},{6,14},{7,15},{8,0},{9,1},... | collective-permute-start | bytes 1572872 | tf_op jit(solution)/shard_map/ppermute | solution.py:679
  457.4 58.2 %collective-permute-start.26 = (bf16[4,64,3072]{2,1,0:T(8,128)(2,1)S(1)}, bf16[4,64,3072]{2,1,0:T(8,128)(2,1)S(1)}, u32[]{:S(2)}, u32[]{:S(2)}) collective-permute-start(bf16[4,64,3072]{2,1,0:T(8,128)(2,1)S(1)} %get-tuple-element.133), channel_id=1, source_target_pairs={{0,2},{1,3},{2,0},{3,1},{4,6},{5,7},{6,4},{7,5},{8,10},{9,11},{10,... | collective-permute-start | bytes 4718600 | tf_op jit(solution)/shard_map/ppermute | solution.py:560
  460.8 35.9 %collective-permute-start.38 = (bf16[64,1024]{1,0:T(8,128)(2,1)S(1)}, bf16[64,1024]{1,0:T(8,128)(2,1)S(1)}, u32[]{:S(2)}, u32[]{:S(2)}) collective-permute-start(bf16[64,1024]{1,0:T(8,128)(2,1)S(1)} %get-tuple-element.143), channel_id=1, source_target_pairs={{0,4},{1,5},{2,6},{3,7},{4,8},{5,9},{6,10},{7,11},{8,12},{9,13},{1... | collective-permute-start | bytes 393224 | tf_op jit(solution)/shard_map/ppermute | solution.py:679
  462.3 36.1 %collective-permute-start.39 = (bf16[64,1024]{1,0:T(8,128)(2,1)S(1)}, bf16[64,1024]{1,0:T(8,128)(2,1)S(1)}, u32[]{:S(2)}, u32[]{:S(2)}) collective-permute-start(bf16[64,1024]{1,0:T(8,128)(2,1)S(1)} %get-tuple-element.144), channel_id=1, source_target_pairs={{0,8},{1,9},{2,10},{3,11},{4,12},{5,13},{6,14},{7,15},{8,0},{9,1},... | collective-permute-start | bytes 393224 | tf_op jit(solution)/shard_map/ppermute | solution.py:679
  496.7 19.0 %collective-permute-start.25 = (bf16[64,4096]{1,0:T(8,128)(2,1)S(1)}, bf16[64,4096]{1,0:T(8,128)(2,1)S(1)}, u32[]{:S(2)}, u32[]{:S(2)}) collective-permute-start(bf16[64,4096]{1,0:T(8,128)(2,1)S(1)} %copy-done.46), channel_id=1, source_target_pairs={{0,12},{1,13},{2,14},{3,15},{4,0},{5,1},{6,2},{7,3},{8,4},{9,5},{1... | collective-permute-start | bytes 1572872 | tf_op jit(solution)/shard_map/ppermute | solution.py:679
  511.9 37.6 %collective-permute-start.43 = (bf16[256,1024]{1,0:T(8,128)(2,1)S(1)}, bf16[256,1024]{1,0:T(8,128)(2,1)S(1)}, u32[]{:S(2)}, u32[]{:S(2)}) collective-permute-start(bf16[256,1024]{1,0:T(8,128)(2,1)S(1)} %fusion.31), channel_id=1, source_target_pairs={{0,16},{16,0},{1,17},{17,1},{2,18},{18,2},{3,19},{19,3},{4,20},{20... | collective-permute-start | bytes 1572872 | tf_op jit(solution)/shard_map/ppermute | solution.py:690
  513.6 37.9 %collective-permute-start.22 = (f32[256,1024]{1,0:T(8,128)S(1)}, f32[256,1024]{1,0:T(8,128)S(1)}, u32[]{:S(2)}, u32[]{:S(2)}) collective-permute-start(f32[256,1024]{1,0:T(8,128)S(1)} %slice.121), channel_id=1, source_target_pairs={{0,16},{16,0},{1,17},{17,1},{2,18},{18,2},{3,19},{19,3},{4,20},{20... | collective-permute-start | bytes 3145736 | tf_op jit(solution)/shard_map/ppermute | solution.py:727
  515.0 33.5 %collective-permute-start.41 = (bf16[64,1024]{1,0:T(8,128)(2,1)S(1)}, bf16[64,1024]{1,0:T(8,128)(2,1)S(1)}, u32[]{:S(2)}, u32[]{:S(2)}) collective-permute-start(bf16[64,1024]{1,0:T(8,128)(2,1)S(1)} %fusion.46), channel_id=1, source_target_pairs={{0,16},{16,0},{1,17},{17,1},{2,18},{18,2},{3,19},{19,3},{4,20},{20... | collective-permute-start | bytes 393224 | tf_op jit(solution)/shard_map/ppermute | solution.py:690
  520.1 29.2 %collective-permute-start.27 = (bf16[1,6144]{1,0:T(2,128)(2,1)S(1)}, bf16[1,6144]{1,0:T(2,128)(2,1)S(1)}, u32[]{:S(2)}, u32[]{:S(2)}) collective-permute-start(bf16[1,6144]{1,0:T(2,128)(2,1)S(1)} %constant_dynamic-update-slice_fusion), channel_id=1, source_target_pairs={{0,16},{16,0},{1,17},{17,1},{2,18},{18,2},{3,19},{19,3},{4,20},{20... | collective-permute-start | bytes 36872 | tf_op jit(solution)/shard_map/ppermute | solution.py:612
  557.3 25.4 %collective-permute-start.30 = (bf16[8,6144]{1,0:T(8,128)(2,1)S(1)}, bf16[8,6144]{1,0:T(8,128)(2,1)S(1)}, u32[]{:S(2)}, u32[]{:S(2)}) collective-permute-start(bf16[8,6144]{1,0:T(8,128)(2,1)S(1)} %reshape.391), channel_id=1, source_target_pairs={{0,12},{1,13},{2,14},{3,15},{4,0},{5,1},{6,2},{7,3},{8,4},{9,5},{1... | collective-permute-start | bytes 294920 | tf_op jit(solution)/shard_map/ppermute | solution.py:627
  559.9 31.7 %collective-permute-start.33 = (bf16[64,3072]{1,0:T(8,128)(2,1)S(1)}, bf16[64,3072]{1,0:T(8,128)(2,1)S(1)}, u32[]{:S(2)}, u32[]{:S(2)}) collective-permute-start(bf16[64,3072]{1,0:T(8,128)(2,1)S(1)} %copy-done.50), channel_id=1, source_target_pairs={{0,4},{1,5},{2,6},{3,7},{4,8},{5,9},{6,10},{7,11},{8,12},{9,13},{1... | collective-permute-start | bytes 1179656 | tf_op jit(solution)/shard_map/ppermute | solution.py:679
  560.9 37.9 %collective-permute-start.34 = (bf16[64,3072]{1,0:T(8,128)(2,1)S(1)}, bf16[64,3072]{1,0:T(8,128)(2,1)S(1)}, u32[]{:S(2)}, u32[]{:S(2)}) collective-permute-start(bf16[64,3072]{1,0:T(8,128)(2,1)S(1)} %copy-done.49), channel_id=1, source_target_pairs={{0,8},{1,9},{2,10},{3,11},{4,12},{5,13},{6,14},{7,15},{8,0},{9,1},... | collective-permute-start | bytes 1179656 | tf_op jit(solution)/shard_map/ppermute | solution.py:679
  565.2 34.8 %collective-permute-start.35 = (bf16[64,3072]{1,0:T(8,128)(2,1)S(1)}, bf16[64,3072]{1,0:T(8,128)(2,1)S(1)}, u32[]{:S(2)}, u32[]{:S(2)}) collective-permute-start(bf16[64,3072]{1,0:T(8,128)(2,1)S(1)} %copy-done.48), channel_id=1, source_target_pairs={{0,12},{1,13},{2,14},{3,15},{4,0},{5,1},{6,2},{7,3},{8,4},{9,5},{1... | collective-permute-start | bytes 1179656 | tf_op jit(solution)/shard_map/ppermute | solution.py:679
  566.3 35.8 %collective-permute-start.42 = (bf16[64,4096]{1,0:T(8,128)(2,1)}, bf16[64,4096]{1,0:T(8,128)(2,1)S(1)}, u32[]{:S(2)}, u32[]{:S(2)}) collective-permute-start(bf16[64,4096]{1,0:T(8,128)(2,1)} %fusion.28), channel_id=1, source_target_pairs={{0,16},{16,0},{1,17},{17,1},{2,18},{18,2},{3,19},{19,3},{4,20},{20... | collective-permute-start | bytes 1572872 | tf_op jit(solution)/shard_map/ppermute | solution.py:690
  (83 other events, 885.5 us)
Sparse Core Ops, SparseCore 0:
  10.2 52.5 all-gather.6
  68.2 44.6 all-gather.8
  130.7 45.5 all-gather.10

commit v5 on v4

--- a/solution.py
+++ b/solution.py
@@ -536,36 +536,50 @@
     return [(place, place ^ bit) for place in range(count)]
 
 
-def assemble_kernel(place_ref, p00, p01, p10, p11, *out_refs):
+def assemble_kernel(place_ref, *refs):
     del place_ref
-    for which, piece in enumerate((p00, p01, p10, p11)):
+    pieces, out_refs = refs[:8], refs[8:]
+    for which, piece in enumerate(pieces):
 
         @pl.when(pl.program_id(0) == which)
         def _():
             begin = 0
             for out_ref in out_refs:
                 end = begin + out_ref.shape[-1]
-                out_ref[0, 0] = piece[0, :, begin:end]
+                out_ref[0, 0, 0] = piece[0, :, begin:end]
                 begin = end
 
 
-def gather_z(weight):
+def gather_half(weight):
+    rows = weight.shape[0] // 2
+    half = lax.dynamic_slice_in_dim(weight, lax.axis_index("seq") * rows, rows, 0)
     z_groups = [
         [base + 4 * step for step in range(lax.axis_size("fsdp") // 4)] for base in range(4)
     ]
-    return lax.all_gather(weight, "fsdp", axis=0, tiled=False, axis_index_groups=z_groups)
+    return lax.all_gather(half, "fsdp", axis=0, tiled=False, axis_index_groups=z_groups)
 
 
 def flip(tensor, bit):
     return lax.ppermute(tensor, "fsdp", swapped_pairs(lax.axis_size("fsdp"), bit))
 
 
-def assemble(own, own_core, across, across_core, *widths):
-    depth, rows, columns = own.shape
+def flip_seq(tensor):
+    return lax.ppermute(tensor, "seq", swapped_pairs(2, 1))
+
+
+def assemble(own, by_seq, by_x, by_both, *widths):
+    depth, rows, columns = own[0].shape
     count = 4 * depth
-    weight = own
+    pieces = [*own, *by_seq, *by_x, *by_both]
     owner = lax.axis_index("fsdp")
-    places = jnp.bitwise_xor(lax.rem(owner, 4), jnp.arange(4, dtype=jnp.int32))
+    flips = jnp.asarray([0, 1, 0, 1, 2, 3, 2, 3], jnp.int32)
+    halves = jnp.asarray([0, 0, 1, 1, 0, 0, 1, 1], jnp.int32)
+    places = jnp.concatenate(
+        [
+            jnp.bitwise_xor(lax.rem(owner, 4), flips),
+            jnp.bitwise_xor(lax.axis_index("seq"), halves),
+        ]
+    )
 
     def piece_spec(which):
         def block(p, z, place_ref):
@@ -575,26 +589,26 @@
         return pl.BlockSpec((1, rows, columns), block)
 
     def out_block(p, z, place_ref):
-        return (z, place_ref[p], 0, 0)
+        return (z, place_ref[p], place_ref[8 + p], 0, 0)
 
     whole = pl.pallas_call(
         assemble_kernel,
         grid_spec=pltpu.PrefetchScalarGridSpec(
             num_scalar_prefetch=1,
-            grid=(4, depth),
-            in_specs=[piece_spec(which) for which in range(4)],
-            out_specs=[pl.BlockSpec((1, 1, rows, width), out_block) for width in widths],
+            grid=(8, depth),
+            in_specs=[piece_spec(which) for which in range(8)],
+            out_specs=[pl.BlockSpec((1, 1, 1, rows, width), out_block) for width in widths],
         ),
         out_shape=[
-            jax.ShapeDtypeStruct((depth, 4, rows, width), weight.dtype) for width in widths
+            jax.ShapeDtypeStruct((depth, 4, 2, rows, width), own[0].dtype) for width in widths
         ],
         compiler_params=pltpu.CompilerParams(vmem_limit_bytes=VMEM_LIMIT),
         cost_estimate=pl.CostEstimate(
             flops=0, bytes_accessed=depth * rows * columns, transcendentals=0
         ),
         name="assemble",
-    )(places, own, own_core, across, across_core)
-    return [part.reshape(count * rows, -1) for part in whole]
+    )(places, *pieces)
+    return [part.reshape(2 * count * rows, -1) for part in whole]
 
 
 def gather_latents(line):
@@ -757,11 +771,20 @@
         axis=1,
     )
     from_owners = lax.all_to_all(to_owners, "fsdp", 0, 0, tiled=True)
-    own_a = gather_z(jnp.concatenate([w_qkv, w_out], axis=1))
-    own_b = gather_z(w_fc1)
-    own_a, from_owners = tied((own_a, from_owners))
-    core_a = flip(own_a, 1)
-    across_a = flip(own_a, 2)
+    input_tokens = whole_latent(latents)
+    cotangent_tokens = whole_latent(out_cotangent)
+    own_a = gather_half(jnp.concatenate([w_qkv, w_out], axis=1))
+    own_b = gather_half(w_fc1)
+    own_a, from_owners, input_tokens, cotangent_tokens, w_fc2 = tied(
+        (own_a, from_owners, input_tokens, cotangent_tokens, w_fc2)
+    )
+    own_c = gather_half(w_fc2)
+    seq_a = flip_seq(own_a)
+    x_a = flip(own_a, 2)
+    own_b, seq_a = tied((own_b, seq_a))
+    both_a = flip(seq_a, 2)
+    seq_b = flip_seq(own_b)
+    x_b = flip(own_b, 2)
 
     modulation = jnp.sum(from_owners[:, :mod_width], axis=0, keepdims=True)
     shift_one, scale_one, gate_one, shift_two, scale_two, gate_two = [
@@ -775,41 +798,53 @@
         begin = end
     query_bias, value_bias, out_bias, up_bias, down_bias = biases
 
-    inputs_full = whole_latent(latents).astype(jnp.float32)
-    grad_output = whole_latent(out_cotangent).astype(jnp.float32)
+    inputs_full = wide(input_tokens)
+    grad_output = wide(cotangent_tokens)
     normed_one, inverse_one = normalize_keep(inputs_full)
     entry_one = low(normed_one * (1.0 + scale_one) + shift_one)
-    entry_one, across_a = tied((entry_one, across_a))
-    across_core_a = flip(across_a, 1)
     full_qkv, full_out = assemble(
-        own_a, core_a, across_a, across_core_a, w_qkv.shape[1], w_out.shape[1]
-    )
-    full_qkv, own_b, w_fc2 = tied((full_qkv, own_b, w_fc2))
-    own_c = gather_z(w_fc2)
-    core_b = flip(own_b, 1)
-    across_b = flip(own_b, 2)
+        (own_a, flip(own_a, 1)),
+        (seq_a, flip(seq_a, 1)),
+        (x_a, flip(x_a, 1)),
+        (both_a, flip(both_a, 1)),
+        w_qkv.shape[1],
+        w_out.shape[1],
+    )
+    full_qkv, x_b, seq_b, own_c = tied((full_qkv, x_b, seq_b, own_c))
+    both_b = flip_seq(x_b)
+    seq_c = flip_seq(own_c)
+    x_c = flip(own_c, 2)
     qkv_bias = jnp.concatenate([query_bias, jnp.zeros_like(query_bias), value_bias], axis=1)
     projected = low(jnp.dot(entry_one, full_qkv, preferred_element_type=jnp.float32) + qkv_bias)
     mixed, log_totals = attend_local(projected)
+    mixed, both_b, seq_c = tied((mixed, both_b, seq_c))
+    both_c = flip(seq_c, 2)
     branch_one = jnp.dot(mixed, full_out, preferred_element_type=jnp.float32) + out_bias
     middle = inputs_full + gate_one * branch_one
     normed_two, inverse_two = normalize_keep(middle)
     entry_two = low(normed_two * (1.0 + scale_two) + shift_two)
-    entry_two, across_b, core_b = tied((entry_two, across_b, core_b))
-    across_core_b = flip(across_b, 1)
-    own_c, across_core_b = tied((own_c, across_core_b))
-    core_c = flip(own_c, 1)
-    across_c = flip(own_c, 2)
-    (full_fc1,) = assemble(own_b, core_b, across_b, across_core_b, w_fc1.shape[1])
+    (full_fc1,) = assemble(
+        (own_b, flip(own_b, 1)),
+        (seq_b, flip(seq_b, 1)),
+        (x_b, flip(x_b, 1)),
+        (both_b, flip(both_b, 1)),
+        w_fc1.shape[1],
+    )
+    full_fc1, x_c = tied((full_fc1, x_c))
     hidden = jnp.dot(entry_two, full_fc1, preferred_element_type=jnp.float32) + up_bias
     active_full, gelu_pull = jax.vjp(gelu_tanh, hidden)
     active = low(active_full)
     grad_branch_two = low(gate_two * grad_output)
     kept_fc2, leaving_fc2 = split_core(outer_sum(active, grad_branch_two))
-    leaving_fc2, across_c, core_c = tied((leaving_fc2, across_c, core_c))
-    across_core_c = flip(across_c, 1)
+    leaving_fc2, both_c = tied((leaving_fc2, both_c))
     arrived_fc2 = flip(leaving_fc2, 1)
-    (full_fc2,) = assemble(own_c, core_c, across_c, across_core_c, w_fc2.shape[1])
+    (full_fc2,) = assemble(
+        (own_c, flip(own_c, 1)),
+        (seq_c, flip(seq_c, 1)),
+        (x_c, flip(x_c, 1)),
+        (both_c, flip(both_c, 1)),
+        w_fc2.shape[1],
+    )
     branch_two = jnp.dot(active, full_fc2, preferred_element_type=jnp.float32) + down_bias
     result = both_halves(low(middle + gate_two * branch_two))
     grad_gate_two = jnp.sum(grad_output * branch_two, axis=0, keepdims=True)
@@ -838,28 +873,28 @@
     leaving_out, grad_branch_one = tied((leaving_out, grad_branch_one))
     arrived_out = flip(leaving_out, 1)
     grad_mixed = low(compared_with(grad_branch_one, full_out))
-    here_out, away_out = split_x(kept_out, arrived_out)
-    grad_mixed, away_out = tied((grad_mixed, away_out))
+    grad_mixed, arrived_out = tied((grad_mixed, arrived_out))
     grad_project = jnp.concatenate(attend_local_back(projected, grad_mixed, log_totals), axis=1)
-    crossed_fc1, away_out, grad_project, landed_fc2, result = tied(
-        (crossed_fc1, away_out, grad_project, landed_fc2, result)
-    )
-    crossed_out = flip(away_out, 2)
+    crossed_fc1, grad_project, landed_fc2, result = tied(
+        (crossed_fc1, grad_project, landed_fc2, result)
+    )
     total_fc1, leaving_fc1 = split_z(here_fc1, crossed_fc1)
     grad_project, leaving_fc1 = tied((grad_project, leaving_fc1))
     landed_fc1 = send_z(leaving_fc1)
     kept_qkv, leaving_qkv = split_core(outer_sum(entry_one, grad_project))
-    grad_project, leaving_qkv = tied((grad_project, leaving_qkv))
+    grad_project, leaving_qkv, landed_first = tied((grad_project, leaving_qkv, landed_fc1[0]))
     arrived_qkv = flip(leaving_qkv, 1)
     grad_entry_one = compared_with(grad_project, full_qkv)
-    here_qkv, away_qkv = split_x(kept_qkv, arrived_qkv)
-    grad_entry_one, away_qkv, crossed_out = tied((grad_entry_one, away_qkv, crossed_out))
-    crossed_qkv = flip(away_qkv, 2)
-    total_out, leaving_out = split_z(here_out, crossed_out)
-    mine_fc2 = sum_z(total_fc2, landed_fc2)
-    grad_entry_one, leaving_out, mine_fc2 = tied((grad_entry_one, leaving_out, mine_fc2))
-    landed_out = send_z(leaving_out)
-    sum_fc2 = sum_seq(mine_fc2)
+    grad_entry_one, arrived_qkv, landed_second = tied(
+        (grad_entry_one, arrived_qkv, landed_fc1[1])
+    )
+    here_last, away_last = [
+        jnp.concatenate(parts, axis=-1)
+        for parts in zip(split_x(kept_qkv, arrived_qkv), split_x(kept_out, arrived_out))
+    ]
+    grad_entry_one, away_last = tied((grad_entry_one, away_last))
+    crossed_last = flip(away_last, 2)
+    sum_fc2 = sum_seq(sum_z(total_fc2, landed_fc2))
     grad_shift_one = jnp.sum(grad_entry_one, axis=0, keepdims=True)
     grad_scale_one = jnp.sum(grad_entry_one * normed_one, axis=0, keepdims=True)
     grad_latents = both_halves(
@@ -879,15 +914,19 @@
             axis=1,
         )
     )
-    grad_mod_mine, landed_fc1, crossed_qkv = tied((grad_mod_mine, landed_fc1, crossed_qkv))
-    total_qkv, leaving_qkv = split_z(here_qkv, crossed_qkv)
-    mine_fc1 = sum_z(total_fc1, landed_fc1)
-    grad_mod_mine, leaving_qkv, mine_fc1 = tied((grad_mod_mine, leaving_qkv, mine_fc1))
-    landed_qkv = send_z(leaving_qkv)
+    mine_fc1 = sum_z(total_fc1, [landed_first, landed_second, *landed_fc1[2:]])
+    grad_mod_mine, mine_fc1, crossed_last = tied((grad_mod_mine, mine_fc1, crossed_last))
     sum_fc1 = sum_seq(mine_fc1)
+    total_last, leaving_last = split_z(here_last, crossed_last)
+    grad_mod_mine, leaving_last, small_inputs = tied(
+        (grad_mod_mine, leaving_last, (grad_project, grad_branch_one, grad_hidden, grad_branch_two))
+    )
+    landed_last = send_z(leaving_last)
     grad_mod_all = gather_latents(grad_mod_mine)
-    sum_out = sum_seq(sum_z(total_out, landed_out))
-    sum_qkv = sum_seq(sum_z(total_qkv, landed_qkv))
+    sum_last = sum_seq(sum_z(total_last, landed_last))
+    sum_qkv = sum_last[:, : 3 * width_all]
+    sum_out = sum_last[:, 3 * width_all :]
+    grad_project, grad_branch_one, grad_hidden, grad_branch_two = small_inputs
     grad_w_mod = outer_sum(lifted, grad_mod_all)
     grad_b_mod = jnp.sum(
         lax.dynamic_slice_in_dim(grad_mod_all, owner * mod_cols, mod_cols, 1).astype(jnp.float32),

time: 631 us -> 632 us (level)
  the two profiles are of different devices: /device:TPU:8 before, /device:TPU:14 now
where the time goes in v5:
time: 632 us; the launch traced here: 620 us
  waiting for transfers between devices  281 us (44%)
  Pallas kernels  86.7 us (14%)
  matrix products  85.4 us (14%)
  other arithmetic  60.9 us (10%)
  starting transfers between devices  48.4 us (8%)
  local copies, waits for them, and re-layouts  42.6 us (7%)
  between operations  15.2 us (2%)
    ppermute x24, waiting for transfers between devices, flip(): lax.ppermute(tensor, 'fsdp', swapped_pairs(lax.axis_size('fsdp'), bit))  75.3 us
    ppermute x9, waiting for transfers between devices, send_z(): arrived.append(lax.ppermute(part, 'fsdp', pairs))  61 us
    pallas_call x3, Pallas kernels, assemble(): pl.pallas_call(assemble_kernel, grid_spec=pltpu.PrefetchScalarGridSpec(nu...  56.1 us
    ppermute x2, waiting for transfers between devices, both_halves(): given = lax.ppermute(tokens[rows_here:], 'seq', seq_swap)  30.4 us
    dot_general x5, matrix products, compared_with(): lax.dot_general(earlier_value, latter, (((1,), (1,)), ((), ())), preferre...  30.3 us
    ppermute x4, waiting for transfers between devices, flip_seq(): return lax.ppermute(tensor, 'seq', swapped_pairs(2, 1))  25.5 us
    all_gather x3, waiting for transfers between devices, gather_half(): lax.all_gather(half, 'fsdp', axis=0, tiled=False, axis_index_groups=z_gro...  23.5 us
    dot_general x5, matrix products, outer_sum(): lax.dot_general(earlier_value, latter, (((0,), (0,)), ((), ())), preferre...  22.4 us
  transfers between devices with their start and end apart: 56, of which 28 were waited for; matrix products, arithmetic and copies ran while one was open for 23% of the time, Pallas kernels for 14%

profile of v5, /device:TPU:14, one launch (start us, length us, event | category | flops | bytes accessed | tf_op | source)
XLA Modules:
  0.0 620.1 jit_solution(14012630230662270119)
XLA Ops:
  18.1 6.2 %all-to-all-start = ((f32[16,1,6656]{2,1,0:T(1,128)}), f32[16,1,6656]{2,1,0:T(1,128)S(1)}, u32[]{:S(2)}, u32[]{:S(2)}) async-start(f32[16,1,6656]{2,1,0:T(1,128)} %copy.82), calls=%async_computation | async-start | bytes 851968 | tf_op jit(solution)/shard_map/all_to_all | solution.py:773
  30.4 9.8 %collective-permute-done = bf16[256,1024]{1,0:T(8,128)(2,1)S(1)} collective-permute-done((bf16[256,1024]{1,0:T(8,128)(2,1)}, bf16[256,1024]{1,0:T(8,128)(2,1)S(1)}, u32[]{:S(2)}, u32[]{:S(2)}) %collective-permute-start) | collective-permute-done | bytes 524320 | tf_op jit(solution)/shard_map/ppermute | solution.py:738
  41.2 9.5 %collective-permute-done.1 = bf16[256,1024]{1,0:T(8,128)(2,1)} collective-permute-done((bf16[256,1024]{1,0:T(8,128)(2,1)S(1)}, bf16[256,1024]{1,0:T(8,128)(2,1)}, u32[]{:S(2)}, u32[]{:S(2)}) %collective-permute-start.1) | collective-permute-done | bytes 524320 | tf_op jit(solution)/shard_map/ppermute | solution.py:738
  54.4 23.5 %all-gather.9.cloned.1.call-done = bf16[128,4096]{1,0:T(8,128)(2,1)} async-done(((bf16[32,4096]{1,0:T(8,128)(2,1)}), bf16[128,4096]{1,0:T(8,128)(2,1)}) %all-gather.9.cloned.1.call-update) | async-done | bytes 1048592 | tf_op jit(solution)/shard_map/all_gather | solution.py:559
  83.9 20.3 %collective-permute-done.7.refs_6_ = bf16[4,32,4096]{2,1,0:T(8,128)(2,1)} collective-permute-done((bf16[4,32,4096]{2,1,0:T(8,128)(2,1)}, bf16[4,32,4096]{2,1,0:T(8,128)(2,1)}, u32[]{:S(2)}, u32[]{:S(2)}) %collective-permute-start.7) | collective-permute-done | bytes 1048608 | tf_op jit(solution)/shard_map/ppermute | solution.py:563
  110.4 18.3 %assemble.3 = (bf16[4,4,2,32,3072]{4,3,2,1,0:T(8,128)(2,1)}, bf16[4,4,2,32,1024]{4,3,2,1,0:T(8,128)(2,1)}) custom-call(s32[16]{0:T(128)S(1)} %pad_add_fusion.place_ref, bf16[4,32,4096]{2,1,0:T(8,128)(2,1)S(1)} %bitcast.219, bf16[4,32,4096]{2,1,0:T(8,128)(2,1)S(1)} %copy-done.6, bf16[4,32,4096]{2,1,0:T(8,128)(2,1)} %collective-permute-done.3.refs_2_, ...), custom_call_target="tpu_custom_call" | custom-call | bytes 524288 | tf_op jit(solution)/shard_map/assemble/pallas_call | solution.py:594
  132.0 6.7 %add_convert_fusion.q_ref.k_ref.v_ref = bf16[512,3072]{1,0:T(8,128)(2,1)S(1)} fusion(bf16[1024,3072]{1,0:T(8,128)(2,1)} %bitcast.275, f32[3072]{0:T(1024)S(1)} %bitcast.267, bf16[512,1024]{1,0:T(8,128)(2,1)} %pad_maximum_fusion.3, f32[1024]{0:T(1024)S(1)} %bitcast.270, f32[1024]{0:T(1024)S(1)} %bitcast.252, f32[512]{0:T(512)S(1)} %add_rsqrt_fusion.1, ...), kind=kOutput, calls=%fused_computation.19 | convolution fusion | flops 3227516928 | bytes 10510336 | tf_op jit(solution)/shard_map/dot_general | solution.py:818
  138.7 13.0 %attend.1 = (bf16[512,1024]{1,0:T(8,128)(2,1)S(1)}, f32[8,2,512]{2,1,0:T(2,128)S(1)}) custom-call(bf16[512,3072]{1,0:T(8,128)(2,1)S(1)} %add_convert_fusion.q_ref.k_ref.v_ref, bf16[512,3072]{1,0:T(8,128)(2,1)S(1)} %add_convert_fusion.q_ref.k_ref.v_ref, bf16[512,3072]{1,0:T(8,128)(2,1)S(1)} %add_convert_fusion.q_ref.k_ref.v_ref), custom_call_target="tpu_custom_call" | custom-call | flops 2097152 | bytes 1572864 | tf_op jit(solution)/shard_map/attend/pallas_call | solution.py:489
  155.1 22.1 %collective-permute-done.12.refs_2_ = bf16[4,128,1024]{2,1,0:T(8,128)(2,1)} collective-permute-done((bf16[4,128,1024]{2,1,0:T(8,128)(2,1)}, bf16[4,128,1024]{2,1,0:T(8,128)(2,1)}, u32[]{:S(2)}, u32[]{:S(2)}) %collective-permute-start.12) | collective-permute-done | bytes 1048608 | tf_op jit(solution)/shard_map/ppermute | solution.py:567
  182.8 18.4 %assemble.4 = bf16[4,4,2,32,4096]{4,3,2,1,0:T(8,128)(2,1)} custom-call(s32[16]{0:T(128)S(1)} %pad_add_fusion.place_ref, bf16[4,32,4096]{2,1,0:T(8,128)(2,1)S(1)} %bitcast.223, bf16[4,32,4096]{2,1,0:T(8,128)(2,1)S(1)} %collective-permute-done.13.refs_1_, bf16[4,32,4096]{2,1,0:T(8,128)(2,1)} %collective-permute-done.10.refs_2_, ...), custom_call_target="tpu_custom_call" | custom-call | bytes 524288 | tf_op jit(solution)/shard_map/assemble/pallas_call | solution.py:594
  201.2 10.8 %fusion.77 = f32[512,4096]{1,0:T(8,128)} fusion(bf16[1024,4096]{1,0:T(8,128)(2,1)} %bitcast.228, f32[512,1024]{1,0:T(8,128)S(1)} %get-tuple-element.163, f32[1024]{0:T(1024)S(1)} %bitcast.272, f32[1024]{0:T(1024)S(1)} %bitcast.263, f32[512]{0:T(512)S(1)} %add_rsqrt_fusion, f32[512]{0:T(512)S(1)} %broadcast_multiply_fusion.4), kind=kOutput, calls=%fused_computation.216 | convolution fusion | flops 4297588736 | bytes 18886656 | tf_op jit(solution)/shard_map/dot_general | solution.py:834
  212.0 10.1 %convolution_convert_fusion.1 = bf16[4096,1024]{1,0:T(8,128)(2,1)S(1)} fusion(bf16[512,1024]{1,0:T(8,128)(2,1)S(1)} %copy-done.26, f32[512,4096]{1,0:T(8,128)} %fusion.77, f32[4096]{0:T(1024)S(1)} %bitcast.260), kind=kOutput, calls=%fused_computation.17 | convolution fusion | flops 4320133120 | bytes 17842176 | tf_op jit(solution)/shard_map/dot_general | solution.py:46
  227.8 5.9 collective-permute-done.20.refs_1_
  240.1 19.4 %assemble.5 = bf16[4,4,2,128,1024]{4,3,2,1,0:T(8,128)(2,1)} custom-call(s32[16]{0:T(128)S(1)} %pad_add_fusion.place_ref, bf16[4,128,1024]{2,1,0:T(8,128)(2,1)S(1)} %bitcast.227, bf16[4,128,1024]{2,1,0:T(8,128)(2,1)S(1)} %collective-permute-done.20.refs_1_, bf16[4,128,1024]{2,1,0:T(8,128)(2,1)} %collective-permute-done.12.refs_2_, ...), custom_call_target="tpu_custom_call" | custom-call | bytes 524288 | tf_op jit(solution)/shard_map/assemble/pallas_call | solution.py:594
  259.5 7.7 %convert_add_fusion.2 = (f32[4,256,1024]{2,1,0:T(8,128)}, bf16[4,256,1024]{2,1,0:T(8,128)(2,1)S(1)}) fusion(bf16[4,2,256,1024]{3,2,0,1:T(8,128)(2,1)} %collective-permute-done.19, s32[]{:T(128)S(6)} %select_n.250, bf16[4,2,2,256,1024]{4,3,2,1,0:T(8,128)(2,1)} %bitcast.235, s32[]{:T(128)S(6)} %select_n.251, s32[]{:T(128)S(6)} %select_n.248, ...), kind=kLoop, calls=%fused_computation.28 | loop fusion | flops 7340032 | bytes 14680084 | tf_op jit(solution)/shard_map/add | solution.py:674
  268.4 12.8 %fusion.3 = bf16[512,4096]{1,0:T(8,128)(2,1)S(1)} fusion(f32[512,4096]{1,0:T(8,128)} %fusion.77, f32[4096]{0:T(1024)S(1)} %bitcast.261, bf16[512,1024]{1,0:T(8,128)(2,1)S(1)} %copy-done.27, bf16[4096,1024]{1,0:T(8,128)(2,1)S(1)} %bitcast.230), kind=kOutput, calls=%fused_computation.7 | convolution fusion | flops 4347396096 | bytes 22036480 | tf_op jit(solution)/shard_map/dot_general | solution.py:52
  291.3 23.6 %collective-permute-done.24 = bf16[4,256,1024]{2,1,0:T(8,128)(2,1)} collective-permute-done((bf16[4,256,1024]{2,1,0:T(8,128)(2,1)S(1)}, bf16[4,256,1024]{2,1,0:T(8,128)(2,1)}, u32[]{:S(2)}, u32[]{:S(2)}) %collective-permute-start.24) | collective-permute-done | bytes 2097184 | tf_op jit(solution)/shard_map/ppermute | solution.py:563
  318.9 8.7 %fusion.81 = f32[512,1024]{1,0:T(8,128)S(1)} fusion(bf16[512,4096]{1,0:T(8,128)(2,1)} %copy-done.24, bf16[1024,4096]{1,0:T(8,128)(2,1)} %bitcast.229), kind=kOutput, calls=%fused_computation.220 | convolution fusion | flops 4294967296 | bytes 14680064 | tf_op jit(solution)/shard_map/dot_general | solution.py:52
  327.7 6.2 %convert_add_fusion = (f32[4,64,4096]{2,1,0:T(8,128)}, bf16[4,64,4096]{2,1,0:T(8,128)(2,1)}) fusion(bf16[4,2,64,4096]{3,2,0,1:T(8,128)(2,1)} %collective-permute-done.25, s32[]{:T(128)S(6)} %select_n.250, bf16[4,2,2,64,4096]{4,3,2,1,0:T(8,128)(2,1)S(1)} %bitcast.239, s32[]{:T(128)S(6)} %select_n.251, s32[]{:T(128)S(6)} %select_n.248, s32[]{:T(128)S(6)} %select_n.245, ...), kind=kLoop, calls=%fused_computation.25 | loop fusion | flops 7340032 | bytes 14680084 | tf_op jit(solution)/shard_map/add | solution.py:674
  336.6 9.5 %fusion.24 = (bf16[1024]{0:T(1024)(128)(2,1)S(1)}, bf16[512,1024]{1,0:T(8,128)(2,1)S(1)}, bf16[1024]{0:T(1024)(128)(2,1)S(1)}, f32[512,1024]{1,0:T(8,128)S(1)}) fusion(bf16[512,1024]{1,0:T(8,128)(2,1)S(1)} %copy-done.30, f32[1024]{0:T(1024)S(1)} %add.458, f32[512,1024]{1,0:T(8,128)S(1)} %copy-done.20, f32[1024]{0:T(1024)S(1)} %bitcast.259, ...), kind=kOutput, calls=%fused_computation.59 | convolution fusion | flops 4325373952 | bytes 27308032 | tf_op jit(solution)/shard_map/dot_general | solution.py:848
  359.2 7.9 %collective-permute-done.31 = bf16[256,1024]{1,0:T(8,128)(2,1)S(1)} collective-permute-done((bf16[256,1024]{1,0:T(8,128)(2,1)}, bf16[256,1024]{1,0:T(8,128)(2,1)S(1)}, u32[]{:S(2)}, u32[]{:S(2)}) %collective-permute-start.31) | collective-permute-done | bytes 524320 | tf_op jit(solution)/shard_map/ppermute | solution.py:741
  368.8 17.6 %attend_back.1 = (bf16[512,1024]{1,0:T(8,128)(2,1)S(1)}, bf16[512,1024]{1,0:T(8,128)(2,1)S(1)}, bf16[512,1024]{1,0:T(8,128)(2,1)S(1)}) custom-call(bf16[512,3072]{1,0:T(8,128)(2,1)} %copy-done.1, bf16[512,3072]{1,0:T(8,128)(2,1)} %copy-done.1, bf16[512,3072]{1,0:T(8,128)(2,1)} %copy-done.1, bf16[512,1024]{1,0:T(8,128)(2,1)S(1)} %convolution_convert_fusion.4.do_ref, ...), custom_call_target="tpu_custom_call" | custom-call | flops 2097152 | bytes 1572864 | tf_op jit(solution)/shard_map/attend_back/pallas_call | solution.py:517
  389.6 10.4 %collective-permute-done.29 = bf16[256,1024]{1,0:T(8,128)(2,1)S(1)} collective-permute-done((bf16[256,1024]{1,0:T(8,128)(2,1)}, bf16[256,1024]{1,0:T(8,128)(2,1)S(1)}, u32[]{:S(2)}, u32[]{:S(2)}) %collective-permute-start.29) | collective-permute-done | bytes 524320 | tf_op jit(solution)/shard_map/ppermute | solution.py:693
  413.0 6.0 collective-permute-done.32
  439.7 20.7 %collective-permute-done.34 = bf16[64,4096]{1,0:T(8,128)(2,1)S(1)} collective-permute-done((bf16[64,4096]{1,0:T(8,128)(2,1)S(1)}, bf16[64,4096]{1,0:T(8,128)(2,1)S(1)}, u32[]{:S(2)}, u32[]{:S(2)}) %collective-permute-start.34) | collective-permute-done | bytes 524320 | tf_op jit(solution)/shard_map/ppermute | solution.py:693
  469.2 22.4 %collective-permute-done.35 = f32[256,1024]{1,0:T(8,128)S(1)} collective-permute-done((f32[256,1024]{1,0:T(8,128)S(1)}, f32[256,1024]{1,0:T(8,128)S(1)}, u32[]{:S(2)}, u32[]{:S(2)}) %collective-permute-start.35) | collective-permute-done | bytes 1048608 | tf_op jit(solution)/shard_map/ppermute | solution.py:741
  492.8 19.0 %collective-permute-done.37 = bf16[4,64,4096]{2,1,0:T(8,128)(2,1)S(1)} collective-permute-done((bf16[4,64,4096]{2,1,0:T(8,128)(2,1)S(1)}, bf16[4,64,4096]{2,1,0:T(8,128)(2,1)S(1)}, u32[]{:S(2)}, u32[]{:S(2)}) %collective-permute-start.37) | collective-permute-done | bytes 2097184 | tf_op jit(solution)/shard_map/ppermute | solution.py:563
  522.1 7.1 %all-to-all-start.1 = ((f32[16,1,512]{2,1,0:T(1,128)}), f32[16,1,512]{2,1,0:T(1,128)S(1)}, u32[]{:S(2)}, u32[]{:S(2)}) async-start(f32[16,1,512]{2,1,0:T(1,128)} %all_to_all.17), calls=%async_computation.1 | async-start | bytes 65536 | tf_op jit(solution)/shard_map/all_to_all | solution.py:954
  548.1 7.4 %collective-permute-done.43 = bf16[8,6144]{1,0:T(8,128)(2,1)S(1)} collective-permute-done((bf16[8,6144]{1,0:T(8,128)(2,1)S(1)}, bf16[8,6144]{1,0:T(8,128)(2,1)S(1)}, u32[]{:S(2)}, u32[]{:S(2)}) %collective-permute-start.43) | collective-permute-done | bytes 98336 | tf_op jit(solution)/shard_map/ppermute | solution.py:641
  556.9 14.1 %collective-permute-done.42 = bf16[8,6144]{1,0:T(8,128)(2,1)S(1)} collective-permute-done((bf16[8,6144]{1,0:T(8,128)(2,1)S(1)}, bf16[8,6144]{1,0:T(8,128)(2,1)S(1)}, u32[]{:S(2)}, u32[]{:S(2)}) %collective-permute-start.42) | collective-permute-done | bytes 98336 | tf_op jit(solution)/shard_map/ppermute | solution.py:641
  577.1 15.2 %collective-permute-done.45 = bf16[64,4096]{1,0:T(8,128)(2,1)S(1)} collective-permute-done((bf16[64,4096]{1,0:T(8,128)(2,1)}, bf16[64,4096]{1,0:T(8,128)(2,1)S(1)}, u32[]{:S(2)}, u32[]{:S(2)}) %collective-permute-start.45) | collective-permute-done | bytes 524320 | tf_op jit(solution)/shard_map/ppermute | solution.py:693
  598.9 12.5 %collective-permute-done.47 = bf16[64,4096]{1,0:T(8,128)(2,1)S(1)} collective-permute-done((bf16[64,4096]{1,0:T(8,128)(2,1)S(1)}, bf16[64,4096]{1,0:T(8,128)(2,1)S(1)}, u32[]{:S(2)}, u32[]{:S(2)}) %collective-permute-start.47) | collective-permute-done | bytes 524320 | tf_op jit(solution)/shard_map/ppermute | solution.py:704
  (348 shorter events, 181.9 us)
Async XLA Ops:
  7.2 45.7 %all-gather.7.cloned.1.call-start = ((), (), s32[]{:S(2)}) async-start(), calls=%async_computation.2 | async-start | bytes 1310720 | tf_op jit(solution)/shard_map/all_gather | solution.py:559
  18.1 34.8 %all-to-all-start = ((f32[16,1,6656]{2,1,0:T(1,128)}), f32[16,1,6656]{2,1,0:T(1,128)S(1)}, u32[]{:S(2)}, u32[]{:S(2)}) async-start(f32[16,1,6656]{2,1,0:T(1,128)} %copy.82), calls=%async_computation | async-start | bytes 851968 | tf_op jit(solution)/shard_map/all_to_all | solution.py:773
  24.3 53.6 %all-gather.9.cloned.1.call-start = ((), (), s32[]{:S(2)}) async-start(), calls=%async_computation.3 | async-start | bytes 1310720 | tf_op jit(solution)/shard_map/all_gather | solution.py:559
  30.3 98.4 %all-gather.11.cloned.1.call-start = ((), (), s32[]{:S(2)}) async-start(), calls=%async_computation.4 | async-start | bytes 1310720 | tf_op jit(solution)/shard_map/all_gather | solution.py:559
  53.6 28.9 %collective-permute-start.5 = (bf16[4,32,4096]{2,1,0:T(8,128)(2,1)}, bf16[4,32,4096]{2,1,0:T(8,128)(2,1)}, u32[]{:S(2)}, u32[]{:S(2)}) collective-permute-start(bf16[4,32,4096]{2,1,0:T(8,128)(2,1)} %bitcast.217), channel_id=1, source_target_pairs={{0,2},{1,3},{2,0},{3,1},{4,6},{5,7},{6,4},{7,5},{8,10},{9,11},{10,... | collective-permute-start | bytes 3145736 | tf_op jit(solution)/shard_map/ppermute | solution.py:563
  54.1 29.8 %collective-permute-start.2 = (bf16[4,32,4096]{2,1,0:T(8,128)(2,1)}, bf16[4,32,4096]{2,1,0:T(8,128)(2,1)S(1)}, u32[]{:S(2)}, u32[]{:S(2)}) collective-permute-start(bf16[4,32,4096]{2,1,0:T(8,128)(2,1)} %bitcast.218), channel_id=1, source_target_pairs={{0,1},{1,0},{2,3},{3,2},{4,5},{5,4},{6,7},{7,6},{8,9},{9,8},{10,11... | collective-permute-start | bytes 3145736 | tf_op jit(solution)/shard_map/ppermute | solution.py:563
  77.9 26.4 %collective-permute-start.7 = (bf16[4,32,4096]{2,1,0:T(8,128)(2,1)}, bf16[4,32,4096]{2,1,0:T(8,128)(2,1)}, u32[]{:S(2)}, u32[]{:S(2)}) collective-permute-start(bf16[4,32,4096]{2,1,0:T(8,128)(2,1)} %collective-permute-done.3.refs_2_), channel_id=1, source_target_pairs={{0,2},{1,3},{2,0},{3,1},{4,6},{5,7},{6,4},{7,5},{8,10},{9,11},{10,... | collective-permute-start | bytes 3145736 | tf_op jit(solution)/shard_map/ppermute | solution.py:563
  81.8 25.4 %collective-permute-start.4 = (bf16[4,32,4096]{2,1,0:T(8,128)(2,1)}, bf16[4,32,4096]{2,1,0:T(8,128)(2,1)S(1)}, u32[]{:S(2)}, u32[]{:S(2)}) collective-permute-start(bf16[4,32,4096]{2,1,0:T(8,128)(2,1)} %collective-permute-done.3.refs_2_), channel_id=1, source_target_pairs={{0,1},{1,0},{2,3},{3,2},{4,5},{5,4},{6,7},{7,6},{8,9},{9,8},{10,11... | collective-permute-start | bytes 3145736 | tf_op jit(solution)/shard_map/ppermute | solution.py:563
  81.8 46.9 %collective-permute-start.10 = (bf16[4,32,4096]{2,1,0:T(8,128)(2,1)}, bf16[4,32,4096]{2,1,0:T(8,128)(2,1)}, u32[]{:S(2)}, u32[]{:S(2)}) collective-permute-start(bf16[4,32,4096]{2,1,0:T(8,128)(2,1)} %bitcast.220), channel_id=1, source_target_pairs={{0,16},{16,0},{1,17},{17,1},{2,18},{18,2},{3,19},{19,3},{4,20},{20... | collective-permute-start | bytes 3145736 | tf_op jit(solution)/shard_map/ppermute | solution.py:567
  82.4 46.3 %collective-permute-start.9 = (bf16[4,32,4096]{2,1,0:T(8,128)(2,1)}, bf16[4,32,4096]{2,1,0:T(8,128)(2,1)}, u32[]{:S(2)}, u32[]{:S(2)}) collective-permute-start(bf16[4,32,4096]{2,1,0:T(8,128)(2,1)} %bitcast.221), channel_id=1, source_target_pairs={{0,2},{1,3},{2,0},{3,1},{4,6},{5,7},{6,4},{7,5},{8,10},{9,11},{10,... | collective-permute-start | bytes 3145736 | tf_op jit(solution)/shard_map/ppermute | solution.py:563
  128.8 26.3 %collective-permute-start.11 = (bf16[4,32,4096]{2,1,0:T(8,128)(2,1)}, bf16[4,32,4096]{2,1,0:T(8,128)(2,1)}, u32[]{:S(2)}, u32[]{:S(2)}) collective-permute-start(bf16[4,32,4096]{2,1,0:T(8,128)(2,1)} %collective-permute-done.9.refs_4_), channel_id=1, source_target_pairs={{0,16},{16,0},{1,17},{17,1},{2,18},{18,2},{3,19},{19,3},{4,20},{20... | collective-permute-start | bytes 3145736 | tf_op jit(solution)/shard_map/ppermute | solution.py:567
  129.3 47.9 %collective-permute-start.12 = (bf16[4,128,1024]{2,1,0:T(8,128)(2,1)}, bf16[4,128,1024]{2,1,0:T(8,128)(2,1)}, u32[]{:S(2)}, u32[]{:S(2)}) collective-permute-start(bf16[4,128,1024]{2,1,0:T(8,128)(2,1)} %bitcast.224), channel_id=1, source_target_pairs={{0,16},{16,0},{1,17},{17,1},{2,18},{18,2},{3,19},{19,3},{4,20},{20... | collective-permute-start | bytes 3145736 | tf_op jit(solution)/shard_map/ppermute | solution.py:567
  130.9 49.3 %collective-permute-start.13 = (bf16[4,32,4096]{2,1,0:T(8,128)(2,1)S(1)}, bf16[4,32,4096]{2,1,0:T(8,128)(2,1)S(1)}, u32[]{:S(2)}, u32[]{:S(2)}) collective-permute-start(bf16[4,32,4096]{2,1,0:T(8,128)(2,1)S(1)} %bitcast.222), channel_id=1, source_target_pairs={{0,1},{1,0},{2,3},{3,2},{4,5},{5,4},{6,7},{7,6},{8,9},{9,8},{10,11... | collective-permute-start | bytes 3145736 | tf_op jit(solution)/shard_map/ppermute | solution.py:563
  131.0 49.9 %collective-permute-start.15 = (bf16[4,32,4096]{2,1,0:T(8,128)(2,1)}, bf16[4,32,4096]{2,1,0:T(8,128)(2,1)S(1)}, u32[]{:S(2)}, u32[]{:S(2)}) collective-permute-start(bf16[4,32,4096]{2,1,0:T(8,128)(2,1)} %collective-permute-done.9.refs_4_), channel_id=1, source_target_pairs={{0,1},{1,0},{2,3},{3,2},{4,5},{5,4},{6,7},{7,6},{8,9},{9,8},{10,11... | collective-permute-start | bytes 3145736 | tf_op jit(solution)/shard_map/ppermute | solution.py:563
  131.5 69.7 %collective-permute-start.17 = (bf16[4,128,1024]{2,1,0:T(8,128)(2,1)}, bf16[4,128,1024]{2,1,0:T(8,128)(2,1)}, u32[]{:S(2)}, u32[]{:S(2)}) collective-permute-start(bf16[4,128,1024]{2,1,0:T(8,128)(2,1)} %bitcast.225), channel_id=1, source_target_pairs={{0,2},{1,3},{2,0},{3,1},{4,6},{5,7},{6,4},{7,5},{8,10},{9,11},{10,... | collective-permute-start | bytes 3145736 | tf_op jit(solution)/shard_map/ppermute | solution.py:563
  155.1 25.7 %collective-permute-start.14 = (bf16[4,32,4096]{2,1,0:T(8,128)(2,1)}, bf16[4,32,4096]{2,1,0:T(8,128)(2,1)S(1)}, u32[]{:S(2)}, u32[]{:S(2)}) collective-permute-start(bf16[4,32,4096]{2,1,0:T(8,128)(2,1)} %collective-permute-done.10.refs_2_), channel_id=1, source_target_pairs={{0,1},{1,0},{2,3},{3,2},{4,5},{5,4},{6,7},{7,6},{8,9},{9,8},{10,11... | collective-permute-start | bytes 3145736 | tf_op jit(solution)/shard_map/ppermute | solution.py:563
  180.3 46.3 %collective-permute-start.18 = (bf16[4,128,1024]{2,1,0:T(8,128)(2,1)}, bf16[4,128,1024]{2,1,0:T(8,128)(2,1)}, u32[]{:S(2)}, u32[]{:S(2)}) collective-permute-start(bf16[4,128,1024]{2,1,0:T(8,128)(2,1)} %collective-permute-done.12.refs_2_), channel_id=1, source_target_pairs={{0,2},{1,3},{2,0},{3,1},{4,6},{5,7},{6,4},{7,5},{8,10},{9,11},{10,... | collective-permute-start | bytes 3145736 | tf_op jit(solution)/shard_map/ppermute | solution.py:563
  226.6 32.9 %collective-permute-start.19 = (bf16[4,2,256,1024]{3,2,0,1:T(8,128)(2,1)}, bf16[4,2,256,1024]{3,2,0,1:T(8,128)(2,1)}, u32[]{:S(2)}, u32[]{:S(2)}) collective-permute-start(bf16[4,2,256,1024]{3,2,0,1:T(8,128)(2,1)} %copy_bitcast_fusion.1), channel_id=1, source_target_pairs={{0,1},{1,0},{2,3},{3,2},{4,5},{5,4},{6,7},{7,6},{8,9},{9,8},{10,11... | collective-permute-start | bytes 12582920 | tf_op jit(solution)/shard_map/ppermute | solution.py:563
  267.2 47.8 %collective-permute-start.24 = (bf16[4,256,1024]{2,1,0:T(8,128)(2,1)S(1)}, bf16[4,256,1024]{2,1,0:T(8,128)(2,1)}, u32[]{:S(2)}, u32[]{:S(2)}) collective-permute-start(bf16[4,256,1024]{2,1,0:T(8,128)(2,1)S(1)} %get-tuple-element.104), channel_id=1, source_target_pairs={{0,2},{1,3},{2,0},{3,1},{4,6},{5,7},{6,4},{7,5},{8,10},{9,11},{10,... | collective-permute-start | bytes 6291464 | tf_op jit(solution)/shard_map/ppermute | solution.py:563
  334.9 67.2 %collective-permute-start.26 = (bf16[4,64,4096]{2,1,0:T(8,128)(2,1)}, bf16[4,64,4096]{2,1,0:T(8,128)(2,1)}, u32[]{:S(2)}, u32[]{:S(2)}) collective-permute-start(bf16[4,64,4096]{2,1,0:T(8,128)(2,1)} %get-tuple-element.108), channel_id=1, source_target_pairs={{0,2},{1,3},{2,0},{3,1},{4,6},{5,7},{6,4},{7,5},{8,10},{9,11},{10,... | collective-permute-start | bytes 6291464 | tf_op jit(solution)/shard_map/ppermute | solution.py:563
  353.2 36.4 %collective-permute-start.28 = (bf16[256,1024]{1,0:T(8,128)(2,1)}, bf16[256,1024]{1,0:T(8,128)(2,1)S(1)}, u32[]{:S(2)}, u32[]{:S(2)}) collective-permute-start(bf16[256,1024]{1,0:T(8,128)(2,1)} %get-tuple-element.117), channel_id=1, source_target_pairs={{0,4},{1,5},{2,6},{3,7},{4,8},{5,9},{6,10},{7,11},{8,12},{9,13},{1... | collective-permute-start | bytes 1572872 | tf_op jit(solution)/shard_map/ppermute | solution.py:693
  354.7 45.4 %collective-permute-start.29 = (bf16[256,1024]{1,0:T(8,128)(2,1)}, bf16[256,1024]{1,0:T(8,128)(2,1)S(1)}, u32[]{:S(2)}, u32[]{:S(2)}) collective-permute-start(bf16[256,1024]{1,0:T(8,128)(2,1)} %get-tuple-element.118), channel_id=1, source_target_pairs={{0,8},{1,9},{2,10},{3,11},{4,12},{5,13},{6,14},{7,15},{8,0},{9,1},... | collective-permute-start | bytes 1572872 | tf_op jit(solution)/shard_map/ppermute | solution.py:693
  367.2 34.9 %collective-permute-start.30 = (bf16[256,1024]{1,0:T(8,128)(2,1)S(1)}, bf16[256,1024]{1,0:T(8,128)(2,1)S(1)}, u32[]{:S(2)}, u32[]{:S(2)}) collective-permute-start(bf16[256,1024]{1,0:T(8,128)(2,1)S(1)} %copy-done.50), channel_id=1, source_target_pairs={{0,12},{1,13},{2,14},{3,15},{4,0},{5,1},{6,2},{7,3},{8,4},{9,5},{1... | collective-permute-start | bytes 1572872 | tf_op jit(solution)/shard_map/ppermute | solution.py:693
  419.8 40.6 %collective-permute-start.33 = (bf16[4,2,64,3072]{3,2,0,1:T(8,128)(2,1)}, bf16[4,2,64,3072]{3,2,0,1:T(8,128)(2,1)}, u32[]{:S(2)}, u32[]{:S(2)}) collective-permute-start(bf16[4,2,64,3072]{3,2,0,1:T(8,128)(2,1)} %copy_bitcast_fusion.2), channel_id=1, source_target_pairs={{0,1},{1,0},{2,3},{3,2},{4,5},{5,4},{6,7},{7,6},{8,9},{9,8},{10,11... | collective-permute-start | bytes 9437192 | tf_op jit(solution)/shard_map/ppermute | solution.py:563
  425.7 34.7 %collective-permute-start.34 = (bf16[64,4096]{1,0:T(8,128)(2,1)S(1)}, bf16[64,4096]{1,0:T(8,128)(2,1)S(1)}, u32[]{:S(2)}, u32[]{:S(2)}) collective-permute-start(bf16[64,4096]{1,0:T(8,128)(2,1)S(1)} %copy-done.52), channel_id=1, source_target_pairs={{0,8},{1,9},{2,10},{3,11},{4,12},{5,13},{6,14},{7,15},{8,0},{9,1},... | collective-permute-start | bytes 1572872 | tf_op jit(solution)/shard_map/ppermute | solution.py:693
  426.4 41.1 %collective-permute-start.36 = (bf16[64,4096]{1,0:T(8,128)(2,1)S(1)}, bf16[64,4096]{1,0:T(8,128)(2,1)S(1)}, u32[]{:S(2)}, u32[]{:S(2)}) collective-permute-start(bf16[64,4096]{1,0:T(8,128)(2,1)S(1)} %copy-done.49), channel_id=1, source_target_pairs={{0,12},{1,13},{2,14},{3,15},{4,0},{5,1},{6,2},{7,3},{8,4},{9,5},{1... | collective-permute-start | bytes 1572872 | tf_op jit(solution)/shard_map/ppermute | solution.py:693
  464.6 47.1 %collective-permute-start.37 = (bf16[4,64,4096]{2,1,0:T(8,128)(2,1)S(1)}, bf16[4,64,4096]{2,1,0:T(8,128)(2,1)S(1)}, u32[]{:S(2)}, u32[]{:S(2)}) collective-permute-start(bf16[4,64,4096]{2,1,0:T(8,128)(2,1)S(1)} %pad_maximum_fusion.1), channel_id=1, source_target_pairs={{0,2},{1,3},{2,0},{3,1},{4,6},{5,7},{6,4},{7,5},{8,10},{9,11},{10,... | collective-permute-start | bytes 6291464 | tf_op jit(solution)/shard_map/ppermute | solution.py:563
  536.6 61.2 %collective-permute-start.49 = (bf16[64,4096]{1,0:T(8,128)(2,1)S(1)}, bf16[64,4096]{1,0:T(8,128)(2,1)S(1)}, u32[]{:S(2)}, u32[]{:S(2)}) collective-permute-start(bf16[64,4096]{1,0:T(8,128)(2,1)S(1)} %fusion.47), channel_id=1, source_target_pairs={{0,16},{16,0},{1,17},{17,1},{2,18},{18,2},{3,19},{19,3},{4,20},{20... | collective-permute-start | bytes 1572872 | tf_op jit(solution)/shard_map/ppermute | solution.py:704
  538.4 38.8 %collective-permute-start.44 = (bf16[64,4096]{1,0:T(8,128)(2,1)}, bf16[64,4096]{1,0:T(8,128)(2,1)S(1)}, u32[]{:S(2)}, u32[]{:S(2)}) collective-permute-start(bf16[64,4096]{1,0:T(8,128)(2,1)} %get-tuple-element.139), channel_id=1, source_target_pairs={{0,4},{1,5},{2,6},{3,7},{4,8},{5,9},{6,10},{7,11},{8,12},{9,13},{1... | collective-permute-start | bytes 1572872 | tf_op jit(solution)/shard_map/ppermute | solution.py:693
  542.3 28.7 %collective-permute-start.42 = (bf16[8,6144]{1,0:T(8,128)(2,1)S(1)}, bf16[8,6144]{1,0:T(8,128)(2,1)S(1)}, u32[]{:S(2)}, u32[]{:S(2)}) collective-permute-start(bf16[8,6144]{1,0:T(8,128)(2,1)S(1)} %reshape.380), channel_id=1, source_target_pairs={{0,8},{1,9},{2,10},{3,11},{4,12},{5,13},{6,14},{7,15},{8,0},{9,1},... | collective-permute-start | bytes 294920 | tf_op jit(solution)/shard_map/ppermute | solution.py:641
  545.5 28.0 %collective-permute-start.41 = (bf16[8,6144]{1,0:T(8,128)(2,1)S(1)}, bf16[8,6144]{1,0:T(8,128)(2,1)S(1)}, u32[]{:S(2)}, u32[]{:S(2)}) collective-permute-start(bf16[8,6144]{1,0:T(8,128)(2,1)S(1)} %reshape.380), channel_id=1, source_target_pairs={{0,12},{1,13},{2,14},{3,15},{4,0},{5,1},{6,2},{7,3},{8,4},{9,5},{1... | collective-permute-start | bytes 294920 | tf_op jit(solution)/shard_map/ppermute | solution.py:641
  555.5 36.8 %collective-permute-start.45 = (bf16[64,4096]{1,0:T(8,128)(2,1)}, bf16[64,4096]{1,0:T(8,128)(2,1)S(1)}, u32[]{:S(2)}, u32[]{:S(2)}) collective-permute-start(bf16[64,4096]{1,0:T(8,128)(2,1)} %get-tuple-element.140), channel_id=1, source_target_pairs={{0,8},{1,9},{2,10},{3,11},{4,12},{5,13},{6,14},{7,15},{8,0},{9,1},... | collective-permute-start | bytes 1572872 | tf_op jit(solution)/shard_map/ppermute | solution.py:693
  (91 other events, 1299.3 us)
Sparse Core Ops, SparseCore 0:
  10.2 35.8 all-gather.6
  48.2 29.6 all-gather.8
  80.2 28.5 all-gather.10

commit v6 on v5

--- a/solution.py
+++ b/solution.py
@@ -546,7 +546,7 @@
             begin = 0
             for out_ref in out_refs:
                 end = begin + out_ref.shape[-1]
-                out_ref[0, 0, 0] = piece[0, :, begin:end]
+                out_ref[:, 0, 0] = piece[:, :, begin:end]
                 begin = end
 
 
@@ -581,23 +581,18 @@
         ]
     )
 
-    def piece_spec(which):
-        def block(p, z, place_ref):
-            del place_ref
-            return (jnp.where(p == which, z, jnp.where(p < which, 0, depth - 1)), 0, 0)
-
-        return pl.BlockSpec((1, rows, columns), block)
-
-    def out_block(p, z, place_ref):
-        return (z, place_ref[p], place_ref[8 + p], 0, 0)
+    piece_spec = pl.BlockSpec((depth, rows, columns), lambda p, place_ref: (0, 0, 0))
+
+    def out_block(p, place_ref):
+        return (0, place_ref[p], place_ref[8 + p], 0, 0)
 
     whole = pl.pallas_call(
         assemble_kernel,
         grid_spec=pltpu.PrefetchScalarGridSpec(
             num_scalar_prefetch=1,
-            grid=(8, depth),
-            in_specs=[piece_spec(which) for which in range(8)],
-            out_specs=[pl.BlockSpec((1, 1, 1, rows, width), out_block) for width in widths],
+            grid=(8,),
+            in_specs=[piece_spec] * 8,
+            out_specs=[pl.BlockSpec((depth, 1, 1, rows, width), out_block) for width in widths],
         ),
         out_shape=[
             jax.ShapeDtypeStruct((depth, 4, 2, rows, width), own[0].dtype) for width in widths
@@ -611,30 +606,20 @@
     return [part.reshape(2 * count * rows, -1) for part in whole]
 
 
+def doubled(tensor, place, axis, other):
+    first = jnp.where(place == 0, tensor, other)
+    second = jnp.where(place == 0, other, tensor)
+    return jnp.stack([first, second], axis=axis)
+
+
 def gather_latents(line):
     count = lax.axis_size("fsdp")
     depth = count // 4
     owner = lax.axis_index("fsdp")
     z_at = lax.div(owner, 4)
-
-    def doubled(tensor, place, axis, other):
-        first = jnp.where(place == 0, tensor, other)
-        second = jnp.where(place == 0, other, tensor)
-        return jnp.stack([first, second], axis=axis)
-
-    tensor = doubled(
-        line, lax.axis_index("seq"), 0, lax.ppermute(line, "seq", swapped_pairs(2, 1))
-    )
-    tensor = doubled(
-        tensor, lax.rem(owner, 2), 0, lax.ppermute(tensor, "fsdp", swapped_pairs(count, 1))
-    )
-    tensor = doubled(
-        tensor,
-        lax.rem(lax.div(owner, 2), 2),
-        0,
-        lax.ppermute(tensor, "fsdp", swapped_pairs(count, 2)),
-    )
-    tensor = tensor.reshape(8, -1)
+    tensor = doubled(line, lax.axis_index("seq"), 0, flip_seq(line))
+    tensor = doubled(tensor, lax.rem(owner, 2), 0, flip(tensor, 1))
+    tensor = tensor.reshape(4, -1)
     slots = [tensor]
     for shift in range(1, depth):
         pairs = [(place, (place + 4 * shift) % count) for place in range(count)]
@@ -646,7 +631,13 @@
         for step in range(1, depth):
             chosen = jnp.where(shift == step, slots[step], chosen)
         ordered.append(chosen)
-    return jnp.concatenate(ordered, axis=0)
+    return jnp.stack(ordered, axis=0)
+
+
+def gather_latents_x(tensor):
+    x_at = lax.rem(lax.div(lax.axis_index("fsdp"), 2), 2)
+    both = doubled(tensor, x_at, 1, flip(tensor, 2))
+    return both.reshape(8 * tensor.shape[0], -1)
 
 
 def low(tensor):
@@ -817,8 +808,7 @@
     qkv_bias = jnp.concatenate([query_bias, jnp.zeros_like(query_bias), value_bias], axis=1)
     projected = low(jnp.dot(entry_one, full_qkv, preferred_element_type=jnp.float32) + qkv_bias)
     mixed, log_totals = attend_local(projected)
-    mixed, both_b, seq_c = tied((mixed, both_b, seq_c))
-    both_c = flip(seq_c, 2)
+    mixed, both_b = tied((mixed, both_b))
     branch_one = jnp.dot(mixed, full_out, preferred_element_type=jnp.float32) + out_bias
     middle = inputs_full + gate_one * branch_one
     normed_two, inverse_two = normalize_keep(middle)
@@ -830,7 +820,8 @@
         (both_b, flip(both_b, 1)),
         w_fc1.shape[1],
     )
-    full_fc1, x_c = tied((full_fc1, x_c))
+    full_fc1, x_c, seq_c = tied((full_fc1, x_c, seq_c))
+    both_c = flip(seq_c, 2)
     hidden = jnp.dot(entry_two, full_fc1, preferred_element_type=jnp.float32) + up_bias
     active_full, gelu_pull = jax.vjp(gelu_tanh, hidden)
     active = low(active_full)
@@ -838,6 +829,9 @@
     kept_fc2, leaving_fc2 = split_core(outer_sum(active, grad_branch_two))
     leaving_fc2, both_c = tied((leaving_fc2, both_c))
     arrived_fc2 = flip(leaving_fc2, 1)
+    here_fc2, away_fc2 = split_x(kept_fc2, arrived_fc2)
+    own_c, away_fc2 = tied((own_c, away_fc2))
+    crossed_fc2 = flip(away_fc2, 2)
     (full_fc2,) = assemble(
         (own_c, flip(own_c, 1)),
         (seq_c, flip(seq_c, 1)),
@@ -848,9 +842,6 @@
     branch_two = jnp.dot(active, full_fc2, preferred_element_type=jnp.float32) + down_bias
     result = both_halves(low(middle + gate_two * branch_two))
     grad_gate_two = jnp.sum(grad_output * branch_two, axis=0, keepdims=True)
-    here_fc2, away_fc2 = split_x(kept_fc2, arrived_fc2)
-    grad_branch_two, away_fc2 = tied((grad_branch_two, away_fc2))
-    crossed_fc2 = flip(away_fc2, 2)
     grad_active = compared_with(grad_branch_two, full_fc2)
     grad_hidden = low(gelu_pull(grad_active)[0])
     kept_fc1, leaving_fc1 = split_core(outer_sum(entry_two, grad_hidden))
@@ -885,15 +876,18 @@
     grad_project, leaving_qkv, landed_first = tied((grad_project, leaving_qkv, landed_fc1[0]))
     arrived_qkv = flip(leaving_qkv, 1)
     grad_entry_one = compared_with(grad_project, full_qkv)
-    grad_entry_one, arrived_qkv, landed_second = tied(
-        (grad_entry_one, arrived_qkv, landed_fc1[1])
-    )
+    grad_entry_one, arrived_qkv = tied((grad_entry_one, arrived_qkv))
     here_last, away_last = [
         jnp.concatenate(parts, axis=-1)
         for parts in zip(split_x(kept_qkv, arrived_qkv), split_x(kept_out, arrived_out))
     ]
-    grad_entry_one, away_last = tied((grad_entry_one, away_last))
-    crossed_last = flip(away_last, 2)
+    small_inputs = (grad_project, grad_branch_one, grad_hidden, grad_branch_two)
+    grad_entry_one, away_last, small_inputs, total_fc1 = tied(
+        (grad_entry_one, away_last, small_inputs, total_fc1)
+    )
+    middle_row = away_last.shape[1] // 2
+    crossed_early = flip(away_last[:, :middle_row], 2)
+    crossed_late = flip(away_last[:, middle_row:], 2)
     sum_fc2 = sum_seq(sum_z(total_fc2, landed_fc2))
     grad_shift_one = jnp.sum(grad_entry_one, axis=0, keepdims=True)
     grad_scale_one = jnp.sum(grad_entry_one * normed_one, axis=0, keepdims=True)
@@ -914,32 +908,11 @@
             axis=1,
         )
     )
-    mine_fc1 = sum_z(total_fc1, [landed_first, landed_second, *landed_fc1[2:]])
-    grad_mod_mine, mine_fc1, crossed_last = tied((grad_mod_mine, mine_fc1, crossed_last))
-    sum_fc1 = sum_seq(mine_fc1)
-    total_last, leaving_last = split_z(here_last, crossed_last)
-    grad_mod_mine, leaving_last, small_inputs = tied(
-        (grad_mod_mine, leaving_last, (grad_project, grad_branch_one, grad_hidden, grad_branch_two))
-    )
-    landed_last = send_z(leaving_last)
-    grad_mod_all = gather_latents(grad_mod_mine)
-    sum_last = sum_seq(sum_z(total_last, landed_last))
-    sum_qkv = sum_last[:, : 3 * width_all]
-    sum_out = sum_last[:, 3 * width_all :]
+    grad_mod_mine, small_inputs, crossed_early = tied(
+        (grad_mod_mine, small_inputs, crossed_early)
+    )
+    grad_mod_z = gather_latents(grad_mod_mine)
     grad_project, grad_branch_one, grad_hidden, grad_branch_two = small_inputs
-    grad_w_mod = outer_sum(lifted, grad_mod_all)
-    grad_b_mod = jnp.sum(
-        lax.dynamic_slice_in_dim(grad_mod_all, owner * mod_cols, mod_cols, 1).astype(jnp.float32),
-        axis=0,
-    )
-    grad_lifted = compared_with(grad_mod_all, w_mod)
-    grad_condition = lift_pull(grad_lifted)[0]
-    grad_table = jnp.dot(
-        one_hot.astype(jnp.float32).T,
-        grad_condition,
-        precision=lax.Precision.HIGHEST,
-        preferred_element_type=jnp.float32,
-    )
     grad_small = [
         wide(grad_project[:, :width_all]),
         wide(grad_project[:, 2 * width_all :]),
@@ -953,12 +926,37 @@
     small_here = jnp.sum(
         lax.all_to_all(small_sums, "fsdp", 0, 0, tiled=True), axis=0, keepdims=True
     )
+    mine_fc1 = sum_z(total_fc1, [landed_first, *landed_fc1[1:]])
+    mine_fc1, crossed_late, small_here, grad_mod_z, grad_latents = tied(
+        (mine_fc1, crossed_late, small_here, grad_mod_z, grad_latents)
+    )
+    crossed_last = jnp.concatenate([crossed_early, crossed_late], axis=1)
+    sum_fc1 = sum_seq(mine_fc1)
+    total_last, leaving_last = split_z(here_last, crossed_last)
+    landed_last = send_z(leaving_last)
+    grad_mod_all = gather_latents_x(grad_mod_z)
+    sum_last = sum_seq(sum_z(total_last, landed_last))
+    sum_qkv = sum_last[:, : 3 * width_all]
+    sum_out = sum_last[:, 3 * width_all :]
     small_total = (small_here + lax.ppermute(small_here, "seq", seq_swap))[0]
     small_grads = []
     begin = 0
     for part in small:
         small_grads.append(small_total[begin : begin + part.shape[0]])
         begin += part.shape[0]
+    grad_w_mod = outer_sum(lifted, grad_mod_all)
+    grad_b_mod = jnp.sum(
+        lax.dynamic_slice_in_dim(grad_mod_all, owner * mod_cols, mod_cols, 1).astype(jnp.float32),
+        axis=0,
+    )
+    grad_lifted = compared_with(grad_mod_all, w_mod)
+    grad_condition = lift_pull(grad_lifted)[0]
+    grad_table = jnp.dot(
+        one_hot.astype(jnp.float32).T,
+        grad_condition,
+        precision=lax.Precision.HIGHEST,
+        preferred_element_type=jnp.float32,
+    )
     return (
         result,
         grad_latents,

time: 632 us -> 554 us (0.88)
  the two profiles are of different devices: /device:TPU:14 before, /device:TPU:0 now
where the time goes in v6:
time: 554 us; the launch traced here: 543 us
  waiting for transfers between devices  202 us (36%)
  matrix products  87.2 us (16%)
  starting transfers between devices  71.2 us (13%)
  other arithmetic  68.5 us (12%)
  Pallas kernels  53.7 us (10%)
  local copies, waits for them, and re-layouts  45.9 us (8%)
  between operations  15.2 us (3%)
    ppermute x27, waiting for transfers between devices, flip(): lax.ppermute(tensor, 'fsdp', swapped_pairs(lax.axis_size('fsdp'), bit))  79 us
    ppermute x9, waiting for transfers between devices, send_z(): arrived.append(lax.ppermute(part, 'fsdp', pairs))  47.2 us
    dot_general x5, matrix products, compared_with(): lax.dot_general(earlier_value, latter, (((1,), (1,)), ((), ())), preferre...  32.5 us
    ppermute x9, starting transfers between devices, send_z(): arrived.append(lax.ppermute(part, 'fsdp', pairs))  23.6 us
    pallas_call x3, Pallas kernels, assemble(): pl.pallas_call(assemble_kernel, grid_spec=pltpu.PrefetchScalarGridSpec(nu...  23.2 us
    dot_general x5, matrix products, outer_sum(): lax.dot_general(earlier_value, latter, (((0,), (0,)), ((), ())), preferre...  22.3 us
    all_gather x3, waiting for transfers between devices, gather_half(): lax.all_gather(half, 'fsdp', axis=0, tiled=False, axis_index_groups=z_gro...  21.6 us
    add x4, other arithmetic, split_x(): here = wide(pick(kept, 1, x_at)) + wide(pick(arrived, 1, x_at))  20.3 us
  transfers between devices with their start and end apart: 57, of which 22 were waited for; matrix products, arithmetic and copies ran while one was open for 31% of the time, Pallas kernels for 10%

profile of v6, /device:TPU:0, one launch (start us, length us, event | category | flops | bytes accessed | tf_op | source)
XLA Modules:
  0.0 543.3 jit_solution(7528273537109785186)
XLA Ops:
  18.1 7.4 %all-to-all-start = ((f32[16,1,6656]{2,1,0:T(1,128)}), f32[16,1,6656]{2,1,0:T(1,128)S(1)}, u32[]{:S(2)}, u32[]{:S(2)}) async-start(f32[16,1,6656]{2,1,0:T(1,128)} %copy.65), calls=%async_computation | async-start | bytes 851968 | tf_op jit(solution)/shard_map/all_to_all | solution.py:764
  31.5 9.8 %collective-permute-done = bf16[256,1024]{1,0:T(8,128)(2,1)S(1)} collective-permute-done((bf16[256,1024]{1,0:T(8,128)(2,1)}, bf16[256,1024]{1,0:T(8,128)(2,1)S(1)}, u32[]{:S(2)}, u32[]{:S(2)}) %collective-permute-start) | collective-permute-done | bytes 524320 | tf_op jit(solution)/shard_map/ppermute | solution.py:729
  42.3 9.8 %collective-permute-done.1 = bf16[256,1024]{1,0:T(8,128)(2,1)} collective-permute-done((bf16[256,1024]{1,0:T(8,128)(2,1)S(1)}, bf16[256,1024]{1,0:T(8,128)(2,1)}, u32[]{:S(2)}, u32[]{:S(2)}) %collective-permute-start.1) | collective-permute-done | bytes 524320 | tf_op jit(solution)/shard_map/ppermute | solution.py:729
  57.9 21.6 %all-gather.9.cloned.1.call-done = bf16[128,4096]{1,0:T(8,128)(2,1)} async-done(((bf16[32,4096]{1,0:T(8,128)(2,1)}), bf16[128,4096]{1,0:T(8,128)(2,1)}) %all-gather.9.cloned.1.call-update) | async-done | bytes 1048592 | tf_op jit(solution)/shard_map/all_gather | solution.py:559
  86.5 19.4 %collective-permute-done.7.refs_6_ = bf16[4,32,4096]{2,1,0:T(8,128)(2,1)} collective-permute-done((bf16[4,32,4096]{2,1,0:T(8,128)(2,1)}, bf16[4,32,4096]{2,1,0:T(8,128)(2,1)}, u32[]{:S(2)}, u32[]{:S(2)}) %collective-permute-start.7) | collective-permute-done | bytes 1048608 | tf_op jit(solution)/shard_map/ppermute | solution.py:563
  110.7 7.9 %assemble.3 = (bf16[4,4,2,32,3072]{4,3,2,1,0:T(8,128)(2,1)}, bf16[4,4,2,32,1024]{4,3,2,1,0:T(8,128)(2,1)}) custom-call(s32[16]{0:T(128)S(1)} %pad_add_fusion.place_ref, bf16[4,32,4096]{2,1,0:T(8,128)(2,1)S(1)} %bitcast.221, bf16[4,32,4096]{2,1,0:T(8,128)(2,1)} %collective-permute-done.2.refs_1_, bf16[4,32,4096]{2,1,0:T(8,128)(2,1)} %collective-permute-done.3.refs_2_, ...), custom_call_target="tpu_custom_call" | custom-call | bytes 524288 | tf_op jit(solution)/shard_map/assemble/pallas_call | solution.py:589
  118.6 8.4 %collective-permute-done.9.refs_4_ = bf16[4,32,4096]{2,1,0:T(8,128)(2,1)} collective-permute-done((bf16[4,32,4096]{2,1,0:T(8,128)(2,1)}, bf16[4,32,4096]{2,1,0:T(8,128)(2,1)}, u32[]{:S(2)}, u32[]{:S(2)}) %collective-permute-start.9) | collective-permute-done | bytes 1048608 | tf_op jit(solution)/shard_map/ppermute | solution.py:563
  130.7 6.6 %add_convert_fusion.q_ref.k_ref.v_ref = bf16[512,3072]{1,0:T(8,128)(2,1)S(1)} fusion(bf16[1024,3072]{1,0:T(8,128)(2,1)} %bitcast.277, f32[3072]{0:T(1024)S(1)} %bitcast.269, bf16[512,1024]{1,0:T(8,128)(2,1)} %pad_maximum_fusion.3, f32[1024]{0:T(1024)S(1)} %bitcast.272, f32[1024]{0:T(1024)S(1)} %bitcast.254, f32[512]{0:T(512)S(1)} %add_rsqrt_fusion.1, ...), kind=kOutput, calls=%fused_computation.19 | convolution fusion | flops 3227516928 | bytes 10510336 | tf_op jit(solution)/shard_map/dot_general | solution.py:809
  137.4 13.0 %attend.1 = (bf16[512,1024]{1,0:T(8,128)(2,1)S(1)}, f32[8,2,512]{2,1,0:T(2,128)S(1)}) custom-call(bf16[512,3072]{1,0:T(8,128)(2,1)S(1)} %add_convert_fusion.q_ref.k_ref.v_ref, bf16[512,3072]{1,0:T(8,128)(2,1)S(1)} %add_convert_fusion.q_ref.k_ref.v_ref, bf16[512,3072]{1,0:T(8,128)(2,1)S(1)} %add_convert_fusion.q_ref.k_ref.v_ref), custom_call_target="tpu_custom_call" | custom-call | flops 2097152 | bytes 1572864 | tf_op jit(solution)/shard_map/attend/pallas_call | solution.py:489
  159.3 8.1 %assemble.4 = bf16[4,4,2,32,4096]{4,3,2,1,0:T(8,128)(2,1)} custom-call(s32[16]{0:T(128)S(1)} %pad_add_fusion.place_ref, bf16[4,32,4096]{2,1,0:T(8,128)(2,1)S(1)} %bitcast.225, bf16[4,32,4096]{2,1,0:T(8,128)(2,1)} %collective-permute-done.12.refs_1_, bf16[4,32,4096]{2,1,0:T(8,128)(2,1)} %collective-permute-done.10.refs_2_, ...), custom_call_target="tpu_custom_call" | custom-call | bytes 524288 | tf_op jit(solution)/shard_map/assemble/pallas_call | solution.py:589
  167.4 6.2 %collective-permute-done.17.refs_2_ = bf16[4,128,1024]{2,1,0:T(8,128)(2,1)S(1)} collective-permute-done((bf16[4,128,1024]{2,1,0:T(8,128)(2,1)}, bf16[4,128,1024]{2,1,0:T(8,128)(2,1)S(1)}, u32[]{:S(2)}, u32[]{:S(2)}) %collective-permute-start.17) | collective-permute-done | bytes 1048608 | tf_op jit(solution)/shard_map/ppermute | solution.py:567
  175.1 10.6 %fusion.72 = f32[512,4096]{1,0:T(8,128)} fusion(bf16[1024,4096]{1,0:T(8,128)(2,1)} %bitcast.230, f32[512,1024]{1,0:T(8,128)S(1)} %get-tuple-element.171, f32[1024]{0:T(1024)S(1)} %bitcast.274, f32[1024]{0:T(1024)S(1)} %bitcast.265, f32[512]{0:T(512)S(1)} %add_rsqrt_fusion, f32[512]{0:T(512)S(1)} %broadcast_multiply_fusion.4), kind=kOutput, calls=%fused_computation.214 | convolution fusion | flops 4297588736 | bytes 18886656 | tf_op jit(solution)/shard_map/dot_general | solution.py:825
  185.7 10.0 %convolution_convert_fusion.1 = bf16[4096,1024]{1,0:T(8,128)(2,1)S(1)} fusion(bf16[512,1024]{1,0:T(8,128)(2,1)S(1)} %copy-done.25, f32[512,4096]{1,0:T(8,128)} %fusion.72, f32[4096]{0:T(1024)S(1)} %bitcast.262), kind=kOutput, calls=%fused_computation.17 | convolution fusion | flops 4320133120 | bytes 17842176 | tf_op jit(solution)/shard_map/dot_general | solution.py:46
  202.3 11.0 %collective-permute-done.19 = bf16[4,2,256,1024]{3,2,0,1:T(8,128)(2,1)} collective-permute-done((bf16[4,2,256,1024]{3,2,0,1:T(8,128)(2,1)}, bf16[4,2,256,1024]{3,2,0,1:T(8,128)(2,1)}, u32[]{:S(2)}, u32[]{:S(2)}) %collective-permute-start.19) | collective-permute-done | bytes 4194336 | tf_op jit(solution)/shard_map/ppermute | solution.py:563
  213.3 7.4 %convert_add_fusion.2 = (f32[4,256,1024]{2,1,0:T(8,128)}, bf16[4,256,1024]{2,1,0:T(8,128)(2,1)S(1)}) fusion(bf16[4,2,256,1024]{3,2,0,1:T(8,128)(2,1)} %collective-permute-done.19, s32[]{:T(128)S(6)} %select_n.250, bf16[4,2,2,256,1024]{4,3,2,1,0:T(8,128)(2,1)} %bitcast.241, s32[]{:T(128)S(6)} %select_n.251, s32[]{:T(128)S(6)} %select_n.248, ...), kind=kLoop, calls=%fused_computation.28 | loop fusion | flops 7340032 | bytes 14680084 | tf_op jit(solution)/shard_map/add | solution.py:665
  223.4 7.1 %assemble.5 = bf16[4,4,2,128,1024]{4,3,2,1,0:T(8,128)(2,1)} custom-call(s32[16]{0:T(128)S(1)} %pad_add_fusion.place_ref, bf16[4,128,1024]{2,1,0:T(8,128)(2,1)S(1)} %bitcast.229, bf16[4,128,1024]{2,1,0:T(8,128)(2,1)S(1)} %collective-permute-done.20.refs_1_, bf16[4,128,1024]{2,1,0:T(8,128)(2,1)S(1)} %collective-permute-done.17.refs_2_, ...), custom_call_target="tpu_custom_call" | custom-call | bytes 524288 | tf_op jit(solution)/shard_map/assemble/pallas_call | solution.py:589
  230.5 14.7 %fusion.3 = bf16[512,4096]{1,0:T(8,128)(2,1)S(1)} fusion(f32[512,4096]{1,0:T(8,128)} %fusion.72, f32[4096]{0:T(1024)S(1)} %bitcast.263, bf16[512,1024]{1,0:T(8,128)(2,1)S(1)} %copy-done.26, bf16[4096,1024]{1,0:T(8,128)(2,1)} %bitcast.232), kind=kOutput, calls=%fused_computation.7 | convolution fusion | flops 4347396096 | bytes 22036480 | tf_op jit(solution)/shard_map/dot_general | solution.py:52
  245.2 5.3 convolution_convert_fusion
  255.0 13.7 %collective-permute-done.24 = bf16[4,256,1024]{2,1,0:T(8,128)(2,1)S(1)} collective-permute-done((bf16[4,256,1024]{2,1,0:T(8,128)(2,1)S(1)}, bf16[4,256,1024]{2,1,0:T(8,128)(2,1)S(1)}, u32[]{:S(2)}, u32[]{:S(2)}) %collective-permute-start.24) | collective-permute-done | bytes 2097184 | tf_op jit(solution)/shard_map/ppermute | solution.py:563
  274.1 8.9 %fusion.77 = f32[512,1024]{1,0:T(8,128)S(1)} fusion(bf16[512,4096]{1,0:T(8,128)(2,1)} %copy-done.24, bf16[1024,4096]{1,0:T(8,128)(2,1)} %bitcast.231), kind=kOutput, calls=%fused_computation.219 | convolution fusion | flops 4294967296 | bytes 14680064 | tf_op jit(solution)/shard_map/dot_general | solution.py:52
  283.1 6.2 %convert_add_fusion = (f32[4,64,4096]{2,1,0:T(8,128)}, bf16[4,64,4096]{2,1,0:T(8,128)(2,1)}) fusion(bf16[4,2,64,4096]{3,2,0,1:T(8,128)(2,1)} %collective-permute-done.25, s32[]{:T(128)S(6)} %select_n.250, bf16[4,2,2,64,4096]{4,3,2,1,0:T(8,128)(2,1)S(1)} %bitcast.239, s32[]{:T(128)S(6)} %select_n.251, s32[]{:T(128)S(6)} %select_n.248, s32[]{:T(128)S(6)} %select_n.245, ...), kind=kLoop, calls=%fused_computation.25 | loop fusion | flops 7340032 | bytes 14680084 | tf_op jit(solution)/shard_map/add | solution.py:665
  291.2 9.5 %fusion.24 = (bf16[1024]{0:T(1024)(128)(2,1)S(1)}, bf16[512,1024]{1,0:T(8,128)(2,1)S(1)}, bf16[1024]{0:T(1024)(128)(2,1)S(1)}, f32[512,1024]{1,0:T(8,128)S(1)}) fusion(bf16[512,1024]{1,0:T(8,128)(2,1)S(1)} %copy-done.29, f32[1024]{0:T(1024)S(1)} %add.458, f32[512,1024]{1,0:T(8,128)S(1)} %copy-done.18, f32[1024]{0:T(1024)S(1)} %bitcast.261, ...), kind=kOutput, calls=%fused_computation.59 | convolution fusion | flops 4325373952 | bytes 27308032 | tf_op jit(solution)/shard_map/dot_general | solution.py:842
  314.0 7.8 %collective-permute-done.31 = bf16[256,1024]{1,0:T(8,128)(2,1)S(1)} collective-permute-done((bf16[256,1024]{1,0:T(8,128)(2,1)}, bf16[256,1024]{1,0:T(8,128)(2,1)S(1)}, u32[]{:S(2)}, u32[]{:S(2)}) %collective-permute-start.31) | collective-permute-done | bytes 524320 | tf_op jit(solution)/shard_map/ppermute | solution.py:732
  324.3 17.6 %attend_back.1 = (bf16[512,1024]{1,0:T(8,128)(2,1)S(1)}, bf16[512,1024]{1,0:T(8,128)(2,1)S(1)}, bf16[512,1024]{1,0:T(8,128)(2,1)S(1)}) custom-call(bf16[512,3072]{1,0:T(8,128)(2,1)} %copy-done.1, bf16[512,3072]{1,0:T(8,128)(2,1)} %copy-done.1, bf16[512,3072]{1,0:T(8,128)(2,1)} %copy-done.1, bf16[512,1024]{1,0:T(8,128)(2,1)S(1)} %convolution_convert_fusion.4.do_ref, ...), custom_call_target="tpu_custom_call" | custom-call | flops 2097152 | bytes 1572864 | tf_op jit(solution)/shard_map/attend_back/pallas_call | solution.py:517
  350.5 11.7 %collective-permute-start.32 = (bf16[64,4096]{1,0:T(8,128)(2,1)S(1)}, bf16[64,4096]{1,0:T(8,128)(2,1)S(1)}, u32[]{:S(2)}, u32[]{:S(2)}) collective-permute-start(bf16[64,4096]{1,0:T(8,128)(2,1)S(1)} %get-tuple-element.128), channel_id=1, source_target_pairs={{0,4},{1,5},{2,6},{3,7},{4,8},{5,9},{6,10},{7,11},{8,12},{9,13},{1... | collective-permute-start | bytes 1572872 | tf_op jit(solution)/shard_map/ppermute | solution.py:684
  383.8 6.1 %collective-permute-done.51 = bf16[256,1024]{1,0:T(8,128)(2,1)} collective-permute-done((bf16[256,1024]{1,0:T(8,128)(2,1)S(1)}, bf16[256,1024]{1,0:T(8,128)(2,1)}, u32[]{:S(2)}, u32[]{:S(2)}) %collective-permute-start.51) | collective-permute-done | bytes 524320 | tf_op jit(solution)/shard_map/ppermute | solution.py:695
  392.2 5.7 %fusion.78 = f32[512,1024]{1,0:T(8,128)S(1)} fusion(bf16[512,3072]{1,0:T(8,128)(2,1)S(1)} %copy-done.14, bf16[1024,3072]{1,0:T(8,128)(2,1)} %bitcast.278), kind=kOutput, calls=%fused_computation.220 | convolution fusion | flops 3221225472 | bytes 11534336 | tf_op jit(solution)/shard_map/dot_general | solution.py:52
  410.3 23.7 %collective-permute-done.37 = bf16[4,32,4096]{2,1,0:T(8,128)(2,1)S(1)} collective-permute-done((bf16[4,32,4096]{2,1,0:T(8,128)(2,1)S(1)}, bf16[4,32,4096]{2,1,0:T(8,128)(2,1)S(1)}, u32[]{:S(2)}, u32[]{:S(2)}) %collective-permute-start.37) | collective-permute-done | bytes 1048608 | tf_op jit(solution)/shard_map/ppermute | solution.py:563
  481.1 7.9 %collective-permute-done.45 = bf16[64,4096]{1,0:T(8,128)(2,1)} collective-permute-done((bf16[64,4096]{1,0:T(8,128)(2,1)}, bf16[64,4096]{1,0:T(8,128)(2,1)}, u32[]{:S(2)}, u32[]{:S(2)}) %collective-permute-start.45) | collective-permute-done | bytes 524320 | tf_op jit(solution)/shard_map/ppermute | solution.py:684
  488.9 8.5 %collective-permute-done.47 = bf16[64,4096]{1,0:T(8,128)(2,1)} collective-permute-done((bf16[64,4096]{1,0:T(8,128)(2,1)}, bf16[64,4096]{1,0:T(8,128)(2,1)}, u32[]{:S(2)}, u32[]{:S(2)}) %collective-permute-start.47) | collective-permute-done | bytes 524320 | tf_op jit(solution)/shard_map/ppermute | solution.py:684
  497.5 22.1 %collective-permute-done.46 = bf16[64,4096]{1,0:T(8,128)(2,1)} collective-permute-done((bf16[64,4096]{1,0:T(8,128)(2,1)}, bf16[64,4096]{1,0:T(8,128)(2,1)}, u32[]{:S(2)}, u32[]{:S(2)}) %collective-permute-start.46) | collective-permute-done | bytes 524320 | tf_op jit(solution)/shard_map/ppermute | solution.py:684
  525.1 9.6 %collective-permute-done.48 = bf16[64,4096]{1,0:T(8,128)(2,1)S(1)} collective-permute-done((bf16[64,4096]{1,0:T(8,128)(2,1)S(1)}, bf16[64,4096]{1,0:T(8,128)(2,1)S(1)}, u32[]{:S(2)}, u32[]{:S(2)}) %collective-permute-start.48) | collective-permute-done | bytes 524320 | tf_op jit(solution)/shard_map/ppermute | solution.py:695
  (346 shorter events, 184.8 us)
Async XLA Ops:
  7.2 47.1 %all-gather.7.cloned.1.call-start = ((), (), s32[]{:S(2)}) async-start(), calls=%async_computation.2 | async-start | bytes 1310720 | tf_op jit(solution)/shard_map/all_gather | solution.py:559
  18.1 36.2 %all-to-all-start = ((f32[16,1,6656]{2,1,0:T(1,128)}), f32[16,1,6656]{2,1,0:T(1,128)S(1)}, u32[]{:S(2)}, u32[]{:S(2)}) async-start(f32[16,1,6656]{2,1,0:T(1,128)} %copy.65), calls=%async_computation | async-start | bytes 851968 | tf_op jit(solution)/shard_map/all_to_all | solution.py:764
  25.4 54.1 %all-gather.9.cloned.1.call-start = ((), (), s32[]{:S(2)}) async-start(), calls=%async_computation.3 | async-start | bytes 1310720 | tf_op jit(solution)/shard_map/all_gather | solution.py:559
  31.4 87.2 %all-gather.11.cloned.1.call-start = ((), (), s32[]{:S(2)}) async-start(), calls=%async_computation.4 | async-start | bytes 1310720 | tf_op jit(solution)/shard_map/all_gather | solution.py:559
  54.3 25.2 %collective-permute-start.3 = (bf16[4,32,4096]{2,1,0:T(8,128)(2,1)}, bf16[4,32,4096]{2,1,0:T(8,128)(2,1)}, u32[]{:S(2)}, u32[]{:S(2)}) collective-permute-start(bf16[4,32,4096]{2,1,0:T(8,128)(2,1)} %bitcast.218), channel_id=1, source_target_pairs={{0,16},{16,0},{1,17},{17,1},{2,18},{18,2},{3,19},{19,3},{4,20},{20... | collective-permute-start | bytes 3145736 | tf_op jit(solution)/shard_map/ppermute | solution.py:567
  56.0 29.9 %collective-permute-start.5 = (bf16[4,32,4096]{2,1,0:T(8,128)(2,1)}, bf16[4,32,4096]{2,1,0:T(8,128)(2,1)}, u32[]{:S(2)}, u32[]{:S(2)}) collective-permute-start(bf16[4,32,4096]{2,1,0:T(8,128)(2,1)} %bitcast.219), channel_id=1, source_target_pairs={{0,2},{1,3},{2,0},{3,1},{4,6},{5,7},{6,4},{7,5},{8,10},{9,11},{10,... | collective-permute-start | bytes 3145736 | tf_op jit(solution)/shard_map/ppermute | solution.py:563
  57.7 28.8 %collective-permute-start.2 = (bf16[4,32,4096]{2,1,0:T(8,128)(2,1)}, bf16[4,32,4096]{2,1,0:T(8,128)(2,1)}, u32[]{:S(2)}, u32[]{:S(2)}) collective-permute-start(bf16[4,32,4096]{2,1,0:T(8,128)(2,1)} %bitcast.220), channel_id=1, source_target_pairs={{0,1},{1,0},{2,3},{3,2},{4,5},{5,4},{6,7},{7,6},{8,9},{9,8},{10,11... | collective-permute-start | bytes 3145736 | tf_op jit(solution)/shard_map/ppermute | solution.py:563
  79.5 26.4 %collective-permute-start.7 = (bf16[4,32,4096]{2,1,0:T(8,128)(2,1)}, bf16[4,32,4096]{2,1,0:T(8,128)(2,1)}, u32[]{:S(2)}, u32[]{:S(2)}) collective-permute-start(bf16[4,32,4096]{2,1,0:T(8,128)(2,1)} %collective-permute-done.3.refs_2_), channel_id=1, source_target_pairs={{0,2},{1,3},{2,0},{3,1},{4,6},{5,7},{6,4},{7,5},{8,10},{9,11},{10,... | collective-permute-start | bytes 3145736 | tf_op jit(solution)/shard_map/ppermute | solution.py:563
  84.4 25.0 %collective-permute-start.4 = (bf16[4,32,4096]{2,1,0:T(8,128)(2,1)}, bf16[4,32,4096]{2,1,0:T(8,128)(2,1)S(1)}, u32[]{:S(2)}, u32[]{:S(2)}) collective-permute-start(bf16[4,32,4096]{2,1,0:T(8,128)(2,1)} %collective-permute-done.3.refs_2_), channel_id=1, source_target_pairs={{0,1},{1,0},{2,3},{3,2},{4,5},{5,4},{6,7},{7,6},{8,9},{9,8},{10,11... | collective-permute-start | bytes 3145736 | tf_op jit(solution)/shard_map/ppermute | solution.py:563
  84.4 34.3 %collective-permute-start.10 = (bf16[4,32,4096]{2,1,0:T(8,128)(2,1)}, bf16[4,32,4096]{2,1,0:T(8,128)(2,1)}, u32[]{:S(2)}, u32[]{:S(2)}) collective-permute-start(bf16[4,32,4096]{2,1,0:T(8,128)(2,1)} %bitcast.222), channel_id=1, source_target_pairs={{0,16},{16,0},{1,17},{17,1},{2,18},{18,2},{3,19},{19,3},{4,20},{20... | collective-permute-start | bytes 3145736 | tf_op jit(solution)/shard_map/ppermute | solution.py:567
  85.9 41.1 %collective-permute-start.9 = (bf16[4,32,4096]{2,1,0:T(8,128)(2,1)}, bf16[4,32,4096]{2,1,0:T(8,128)(2,1)}, u32[]{:S(2)}, u32[]{:S(2)}) collective-permute-start(bf16[4,32,4096]{2,1,0:T(8,128)(2,1)} %bitcast.223), channel_id=1, source_target_pairs={{0,2},{1,3},{2,0},{3,1},{4,6},{5,7},{6,4},{7,5},{8,10},{9,11},{10,... | collective-permute-start | bytes 3145736 | tf_op jit(solution)/shard_map/ppermute | solution.py:563
  108.8 44.7 %collective-permute-start.12 = (bf16[4,32,4096]{2,1,0:T(8,128)(2,1)S(1)}, bf16[4,32,4096]{2,1,0:T(8,128)(2,1)}, u32[]{:S(2)}, u32[]{:S(2)}) collective-permute-start(bf16[4,32,4096]{2,1,0:T(8,128)(2,1)S(1)} %bitcast.224), channel_id=1, source_target_pairs={{0,1},{1,0},{2,3},{3,2},{4,5},{5,4},{6,7},{7,6},{8,9},{9,8},{10,11... | collective-permute-start | bytes 3145736 | tf_op jit(solution)/shard_map/ppermute | solution.py:563
  127.1 26.4 %collective-permute-start.11 = (bf16[4,32,4096]{2,1,0:T(8,128)(2,1)}, bf16[4,32,4096]{2,1,0:T(8,128)(2,1)}, u32[]{:S(2)}, u32[]{:S(2)}) collective-permute-start(bf16[4,32,4096]{2,1,0:T(8,128)(2,1)} %collective-permute-done.9.refs_4_), channel_id=1, source_target_pairs={{0,16},{16,0},{1,17},{17,1},{2,18},{18,2},{3,19},{19,3},{4,20},{20... | collective-permute-start | bytes 3145736 | tf_op jit(solution)/shard_map/ppermute | solution.py:567
  128.6 28.4 %collective-permute-start.14 = (bf16[4,32,4096]{2,1,0:T(8,128)(2,1)}, bf16[4,32,4096]{2,1,0:T(8,128)(2,1)S(1)}, u32[]{:S(2)}, u32[]{:S(2)}) collective-permute-start(bf16[4,32,4096]{2,1,0:T(8,128)(2,1)} %collective-permute-done.9.refs_4_), channel_id=1, source_target_pairs={{0,1},{1,0},{2,3},{3,2},{4,5},{5,4},{6,7},{7,6},{8,9},{9,8},{10,11... | collective-permute-start | bytes 3145736 | tf_op jit(solution)/shard_map/ppermute | solution.py:563
  128.6 45.0 %collective-permute-start.17 = (bf16[4,128,1024]{2,1,0:T(8,128)(2,1)}, bf16[4,128,1024]{2,1,0:T(8,128)(2,1)S(1)}, u32[]{:S(2)}, u32[]{:S(2)}) collective-permute-start(bf16[4,128,1024]{2,1,0:T(8,128)(2,1)} %bitcast.226), channel_id=1, source_target_pairs={{0,16},{16,0},{1,17},{17,1},{2,18},{18,2},{3,19},{19,3},{4,20},{20... | collective-permute-start | bytes 3145736 | tf_op jit(solution)/shard_map/ppermute | solution.py:567
  129.3 44.3 %collective-permute-start.16 = (bf16[4,128,1024]{2,1,0:T(8,128)(2,1)}, bf16[4,128,1024]{2,1,0:T(8,128)(2,1)S(1)}, u32[]{:S(2)}, u32[]{:S(2)}) collective-permute-start(bf16[4,128,1024]{2,1,0:T(8,128)(2,1)} %bitcast.227), channel_id=1, source_target_pairs={{0,2},{1,3},{2,0},{3,1},{4,6},{5,7},{6,4},{7,5},{8,10},{9,11},{10,... | collective-permute-start | bytes 3145736 | tf_op jit(solution)/shard_map/ppermute | solution.py:563
  173.6 26.7 %collective-permute-start.18 = (bf16[4,128,1024]{2,1,0:T(8,128)(2,1)S(1)}, bf16[4,128,1024]{2,1,0:T(8,128)(2,1)S(1)}, u32[]{:S(2)}, u32[]{:S(2)}) collective-permute-start(bf16[4,128,1024]{2,1,0:T(8,128)(2,1)S(1)} %collective-permute-done.17.refs_2_), channel_id=1, source_target_pairs={{0,2},{1,3},{2,0},{3,1},{4,6},{5,7},{6,4},{7,5},{8,10},{9,11},{10,... | collective-permute-start | bytes 3145736 | tf_op jit(solution)/shard_map/ppermute | solution.py:563
  220.8 47.9 %collective-permute-start.24 = (bf16[4,256,1024]{2,1,0:T(8,128)(2,1)S(1)}, bf16[4,256,1024]{2,1,0:T(8,128)(2,1)S(1)}, u32[]{:S(2)}, u32[]{:S(2)}) collective-permute-start(bf16[4,256,1024]{2,1,0:T(8,128)(2,1)S(1)} %get-tuple-element.108), channel_id=1, source_target_pairs={{0,2},{1,3},{2,0},{3,1},{4,6},{5,7},{6,4},{7,5},{8,10},{9,11},{10,... | collective-permute-start | bytes 6291464 | tf_op jit(solution)/shard_map/ppermute | solution.py:563
  290.3 57.0 %collective-permute-start.26 = (bf16[4,64,4096]{2,1,0:T(8,128)(2,1)}, bf16[4,64,4096]{2,1,0:T(8,128)(2,1)}, u32[]{:S(2)}, u32[]{:S(2)}) collective-permute-start(bf16[4,64,4096]{2,1,0:T(8,128)(2,1)} %get-tuple-element.112), channel_id=1, source_target_pairs={{0,2},{1,3},{2,0},{3,1},{4,6},{5,7},{6,4},{7,5},{8,10},{9,11},{10,... | collective-permute-start | bytes 6291464 | tf_op jit(solution)/shard_map/ppermute | solution.py:563
  309.2 33.0 %collective-permute-start.28 = (bf16[256,1024]{1,0:T(8,128)(2,1)}, bf16[256,1024]{1,0:T(8,128)(2,1)S(1)}, u32[]{:S(2)}, u32[]{:S(2)}) collective-permute-start(bf16[256,1024]{1,0:T(8,128)(2,1)} %get-tuple-element.121), channel_id=1, source_target_pairs={{0,4},{1,5},{2,6},{3,7},{4,8},{5,9},{6,10},{7,11},{8,12},{9,13},{1... | collective-permute-start | bytes 1572872 | tf_op jit(solution)/shard_map/ppermute | solution.py:684
  310.5 36.9 %collective-permute-start.29 = (bf16[256,1024]{1,0:T(8,128)(2,1)}, bf16[256,1024]{1,0:T(8,128)(2,1)S(1)}, u32[]{:S(2)}, u32[]{:S(2)}) collective-permute-start(bf16[256,1024]{1,0:T(8,128)(2,1)} %get-tuple-element.122), channel_id=1, source_target_pairs={{0,8},{1,9},{2,10},{3,11},{4,12},{5,13},{6,14},{7,15},{8,0},{9,1},... | collective-permute-start | bytes 1572872 | tf_op jit(solution)/shard_map/ppermute | solution.py:684
  321.8 25.6 %collective-permute-start.30 = (bf16[256,1024]{1,0:T(8,128)(2,1)S(1)}, bf16[256,1024]{1,0:T(8,128)(2,1)S(1)}, u32[]{:S(2)}, u32[]{:S(2)}) collective-permute-start(bf16[256,1024]{1,0:T(8,128)(2,1)S(1)} %copy-done.48), channel_id=1, source_target_pairs={{0,12},{1,13},{2,14},{3,15},{4,0},{5,1},{6,2},{7,3},{8,4},{9,5},{1... | collective-permute-start | bytes 1572872 | tf_op jit(solution)/shard_map/ppermute | solution.py:684
  350.5 23.1 %collective-permute-start.32 = (bf16[64,4096]{1,0:T(8,128)(2,1)S(1)}, bf16[64,4096]{1,0:T(8,128)(2,1)S(1)}, u32[]{:S(2)}, u32[]{:S(2)}) collective-permute-start(bf16[64,4096]{1,0:T(8,128)(2,1)S(1)} %get-tuple-element.128), channel_id=1, source_target_pairs={{0,4},{1,5},{2,6},{3,7},{4,8},{5,9},{6,10},{7,11},{8,12},{9,13},{1... | collective-permute-start | bytes 1572872 | tf_op jit(solution)/shard_map/ppermute | solution.py:684
  373.6 24.4 %collective-permute-start.33 = (bf16[4,2,64,3072]{3,2,0,1:T(8,128)(2,1)}, bf16[4,2,64,3072]{3,2,0,1:T(8,128)(2,1)}, u32[]{:S(2)}, u32[]{:S(2)}) collective-permute-start(bf16[4,2,64,3072]{3,2,0,1:T(8,128)(2,1)} %copy_bitcast_fusion.2), channel_id=1, source_target_pairs={{0,1},{1,0},{2,3},{3,2},{4,5},{5,4},{6,7},{7,6},{8,9},{9,8},{10,11... | collective-permute-start | bytes 9437192 | tf_op jit(solution)/shard_map/ppermute | solution.py:563
  379.0 31.0 %collective-permute-start.34 = (bf16[64,4096]{1,0:T(8,128)(2,1)}, bf16[64,4096]{1,0:T(8,128)(2,1)S(1)}, u32[]{:S(2)}, u32[]{:S(2)}) collective-permute-start(bf16[64,4096]{1,0:T(8,128)(2,1)} %get-tuple-element.136), channel_id=1, source_target_pairs={{0,8},{1,9},{2,10},{3,11},{4,12},{5,13},{6,14},{7,15},{8,0},{9,1},... | collective-permute-start | bytes 1572872 | tf_op jit(solution)/shard_map/ppermute | solution.py:684
  381.1 28.9 %collective-permute-start.35 = (bf16[64,4096]{1,0:T(8,128)(2,1)}, bf16[64,4096]{1,0:T(8,128)(2,1)S(1)}, u32[]{:S(2)}, u32[]{:S(2)}) collective-permute-start(bf16[64,4096]{1,0:T(8,128)(2,1)} %get-tuple-element.137), channel_id=1, source_target_pairs={{0,12},{1,13},{2,14},{3,15},{4,0},{5,1},{6,2},{7,3},{8,4},{9,5},{1... | collective-permute-start | bytes 1572872 | tf_op jit(solution)/shard_map/ppermute | solution.py:684
  406.1 43.3 %collective-permute-start.43 = (f32[256,1024]{1,0:T(8,128)}, f32[256,1024]{1,0:T(8,128)}, u32[]{:S(2)}, u32[]{:S(2)}) collective-permute-start(f32[256,1024]{1,0:T(8,128)} %slice.137), channel_id=1, source_target_pairs={{0,16},{16,0},{1,17},{17,1},{2,18},{18,2},{3,19},{19,3},{4,20},{20... | collective-permute-start | bytes 3145736 | tf_op jit(solution)/shard_map/ppermute | solution.py:732
  408.0 26.1 %collective-permute-start.37 = (bf16[4,32,4096]{2,1,0:T(8,128)(2,1)S(1)}, bf16[4,32,4096]{2,1,0:T(8,128)(2,1)S(1)}, u32[]{:S(2)}, u32[]{:S(2)}) collective-permute-start(bf16[4,32,4096]{2,1,0:T(8,128)(2,1)S(1)} %get-tuple-element.196), channel_id=1, source_target_pairs={{0,2},{1,3},{2,0},{3,1},{4,6},{5,7},{6,4},{7,5},{8,10},{9,11},{10,... | collective-permute-start | bytes 3145736 | tf_op jit(solution)/shard_map/ppermute | solution.py:563
  409.5 52.9 %collective-permute-start.36 = (bf16[4,32,4096]{2,1,0:T(8,128)(2,1)}, bf16[4,32,4096]{2,1,0:T(8,128)(2,1)}, u32[]{:S(2)}, u32[]{:S(2)}) collective-permute-start(bf16[4,32,4096]{2,1,0:T(8,128)(2,1)} %get-tuple-element.197), channel_id=1, source_target_pairs={{0,2},{1,3},{2,0},{3,1},{4,6},{5,7},{6,4},{7,5},{8,10},{9,11},{10,... | collective-permute-start | bytes 3145736 | tf_op jit(solution)/shard_map/ppermute | solution.py:563
  465.6 57.4 %collective-permute-start.50 = (bf16[64,4096]{1,0:T(8,128)(2,1)S(1)}, bf16[64,4096]{1,0:T(8,128)(2,1)}, u32[]{:S(2)}, u32[]{:S(2)}) collective-permute-start(bf16[64,4096]{1,0:T(8,128)(2,1)S(1)} %add_convert_fusion.3), channel_id=1, source_target_pairs={{0,16},{16,0},{1,17},{17,1},{2,18},{18,2},{3,19},{19,3},{4,20},{20... | collective-permute-start | bytes 1572872 | tf_op jit(solution)/shard_map/ppermute | solution.py:695
  473.1 24.4 %collective-permute-start.47 = (bf16[64,4096]{1,0:T(8,128)(2,1)}, bf16[64,4096]{1,0:T(8,128)(2,1)}, u32[]{:S(2)}, u32[]{:S(2)}) collective-permute-start(bf16[64,4096]{1,0:T(8,128)(2,1)} %get-tuple-element.179), channel_id=1, source_target_pairs={{0,12},{1,13},{2,14},{3,15},{4,0},{5,1},{6,2},{7,3},{8,4},{9,5},{1... | collective-permute-start | bytes 1572872 | tf_op jit(solution)/shard_map/ppermute | solution.py:684
  475.8 43.8 %collective-permute-start.46 = (bf16[64,4096]{1,0:T(8,128)(2,1)}, bf16[64,4096]{1,0:T(8,128)(2,1)}, u32[]{:S(2)}, u32[]{:S(2)}) collective-permute-start(bf16[64,4096]{1,0:T(8,128)(2,1)} %get-tuple-element.180), channel_id=1, source_target_pairs={{0,8},{1,9},{2,10},{3,11},{4,12},{5,13},{6,14},{7,15},{8,0},{9,1},... | collective-permute-start | bytes 1572872 | tf_op jit(solution)/shard_map/ppermute | solution.py:684
  (88 other events, 986.2 us)
Sparse Core Ops, SparseCore 0:
  10.2 40.3 all-gather.6
  52.7 26.7 all-gather.8
  82.8 27.6 all-gather.10

commit v7 on v6

--- a/solution.py
+++ b/solution.py
@@ -801,14 +801,13 @@
         w_qkv.shape[1],
         w_out.shape[1],
     )
-    full_qkv, x_b, seq_b, own_c = tied((full_qkv, x_b, seq_b, own_c))
+    qkv_bias = jnp.concatenate([query_bias, jnp.zeros_like(query_bias), value_bias], axis=1)
+    projected = low(jnp.dot(entry_one, full_qkv, preferred_element_type=jnp.float32) + qkv_bias)
+    projected, x_b, seq_b, own_c = tied((projected, x_b, seq_b, own_c))
     both_b = flip_seq(x_b)
     seq_c = flip_seq(own_c)
     x_c = flip(own_c, 2)
-    qkv_bias = jnp.concatenate([query_bias, jnp.zeros_like(query_bias), value_bias], axis=1)
-    projected = low(jnp.dot(entry_one, full_qkv, preferred_element_type=jnp.float32) + qkv_bias)
     mixed, log_totals = attend_local(projected)
-    mixed, both_b = tied((mixed, both_b))
     branch_one = jnp.dot(mixed, full_out, preferred_element_type=jnp.float32) + out_bias
     middle = inputs_full + gate_one * branch_one
     normed_two, inverse_two = normalize_keep(middle)
@@ -840,7 +839,7 @@
         w_fc2.shape[1],
     )
     branch_two = jnp.dot(active, full_fc2, preferred_element_type=jnp.float32) + down_bias
-    result = both_halves(low(middle + gate_two * branch_two))
+    result_tokens = low(middle + gate_two * branch_two)
     grad_gate_two = jnp.sum(grad_output * branch_two, axis=0, keepdims=True)
     grad_active = compared_with(grad_branch_two, full_fc2)
     grad_hidden = low(gelu_pull(grad_active)[0])
@@ -866,9 +865,7 @@
     grad_mixed = low(compared_with(grad_branch_one, full_out))
     grad_mixed, arrived_out = tied((grad_mixed, arrived_out))
     grad_project = jnp.concatenate(attend_local_back(projected, grad_mixed, log_totals), axis=1)
-    crossed_fc1, grad_project, landed_fc2, result = tied(
-        (crossed_fc1, grad_project, landed_fc2, result)
-    )
+    crossed_fc1, grad_project, landed_fc2 = tied((crossed_fc1, grad_project, landed_fc2))
     total_fc1, leaving_fc1 = split_z(here_fc1, crossed_fc1)
     grad_project, leaving_fc1 = tied((grad_project, leaving_fc1))
     landed_fc1 = send_z(leaving_fc1)
@@ -882,9 +879,10 @@
         for parts in zip(split_x(kept_qkv, arrived_qkv), split_x(kept_out, arrived_out))
     ]
     small_inputs = (grad_project, grad_branch_one, grad_hidden, grad_branch_two)
-    grad_entry_one, away_last, small_inputs, total_fc1 = tied(
-        (grad_entry_one, away_last, small_inputs, total_fc1)
-    )
+    grad_entry_one, away_last, small_inputs, total_fc1, total_fc2, result_tokens = tied(
+        (grad_entry_one, away_last, small_inputs, total_fc1, total_fc2, result_tokens)
+    )
+    result = both_halves(result_tokens)
     middle_row = away_last.shape[1] // 2
     crossed_early = flip(away_last[:, :middle_row], 2)
     crossed_late = flip(away_last[:, middle_row:], 2)
@@ -927,8 +925,8 @@
         lax.all_to_all(small_sums, "fsdp", 0, 0, tiled=True), axis=0, keepdims=True
     )
     mine_fc1 = sum_z(total_fc1, [landed_first, *landed_fc1[1:]])
-    mine_fc1, crossed_late, small_here, grad_mod_z, grad_latents = tied(
-        (mine_fc1, crossed_late, small_here, grad_mod_z, grad_latents)
+    mine_fc1, crossed_late, small_here, grad_mod_z, grad_latents, result = tied(
+        (mine_fc1, crossed_late, small_here, grad_mod_z, grad_latents, result)
     )
     crossed_last = jnp.concatenate([crossed_early, crossed_late], axis=1)
     sum_fc1 = sum_seq(mine_fc1)

time: 554 us -> 565 us (1.020)
  starting transfers between devices: 71.2 us -> 80.5 us
    ppermute x27, waiting for transfers between devices: 79 us -> 59.4 us  [flip(): lax.ppermute(tensor, 'fsdp', swapped_pairs(lax.axis_size('fsdp'), bit))]
    ppermute x9, waiting for transfers between devices: 47.2 us -> 62.6 us  [send_z(): arrived.append(lax.ppermute(part, 'fsdp', pairs))]
    ppermute x5, waiting for transfers between devices: 10.6 us -> 22.1 us  [flip_seq(): return lax.ppermute(tensor, 'seq', swapped_pairs(2, 1))]
    all_to_all x1, starting transfers between devices: 4.37 us -> 14.8 us  [local_whole_latent(): lax.all_to_all(small_sums, 'fsdp', 0, 0, tiled=True)]
    ppermute x2, waiting for transfers between devices: 7.77 us -> 0.68 us  [both_halves(): given = lax.ppermute(tokens[rows_here:], 'seq', seq_swap)]
    convert_element_type x7 -> x6, other arithmetic: 12.6 us -> 6.3 us  [low(): return tensor.astype(jnp.bfloat16)]
    unnamed x135 -> x143, local copies, waits for them, and re-layouts: 17.6 us -> 20.9 us
  transfers between devices with their start and end apart: 57 -> 57, of which waited for: 22 -> 23; matrix products, arithmetic and copies ran while one was open for 31% -> 30% of each run, Pallas kernels for 10% -> 10%
where the time goes in v7:
time: 565 us; the launch traced here: 555 us
  waiting for transfers between devices  207 us (37%)
  matrix products  85.1 us (15%)
  starting transfers between devices  80.5 us (14%)
  other arithmetic  66 us (12%)
  Pallas kernels  53.2 us (9%)
  local copies, waits for them, and re-layouts  47.3 us (8%)
  between operations  15.2 us (3%)
    ppermute x9, waiting for transfers between devices, send_z(): arrived.append(lax.ppermute(part, 'fsdp', pairs))  62.6 us
    ppermute x27, waiting for transfers between devices, flip(): lax.ppermute(tensor, 'fsdp', swapped_pairs(lax.axis_size('fsdp'), bit))  59.4 us
    dot_general x5, matrix products, compared_with(): lax.dot_general(earlier_value, latter, (((1,), (1,)), ((), ())), preferre...  29.1 us
    ppermute x9, starting transfers between devices, send_z(): arrived.append(lax.ppermute(part, 'fsdp', pairs))  24.4 us
    pallas_call x3, Pallas kernels, assemble(): pl.pallas_call(assemble_kernel, grid_spec=pltpu.PrefetchScalarGridSpec(nu...  23.1 us
    ppermute x5, waiting for transfers between devices, flip_seq(): return lax.ppermute(tensor, 'seq', swapped_pairs(2, 1))  22.1 us
    dot_general x5, matrix products, outer_sum(): lax.dot_general(earlier_value, latter, (((0,), (0,)), ((), ())), preferre...  22 us
    all_gather x3, waiting for transfers between devices, gather_half(): lax.all_gather(half, 'fsdp', axis=0, tiled=False, axis_index_groups=z_gro...  22 us
  transfers between devices with their start and end apart: 57, of which 23 were waited for; matrix products, arithmetic and copies ran while one was open for 30% of the time, Pallas kernels for 10%

profile of v7, /device:TPU:0, one launch (start us, length us, event | category | flops | bytes accessed | tf_op | source)
XLA Modules:
  0.0 554.7 jit_solution(4599870696041104862)
XLA Ops:
  18.1 7.4 %all-to-all-start = ((f32[16,1,6656]{2,1,0:T(1,128)}), f32[16,1,6656]{2,1,0:T(1,128)S(1)}, u32[]{:S(2)}, u32[]{:S(2)}) async-start(f32[16,1,6656]{2,1,0:T(1,128)} %copy.65), calls=%async_computation | async-start | bytes 851968 | tf_op jit(solution)/shard_map/all_to_all | solution.py:764
  31.5 9.8 %collective-permute-done = bf16[256,1024]{1,0:T(8,128)(2,1)S(1)} collective-permute-done((bf16[256,1024]{1,0:T(8,128)(2,1)}, bf16[256,1024]{1,0:T(8,128)(2,1)S(1)}, u32[]{:S(2)}, u32[]{:S(2)}) %collective-permute-start) | collective-permute-done | bytes 524320 | tf_op jit(solution)/shard_map/ppermute | solution.py:729
  42.3 9.8 %collective-permute-done.1 = bf16[256,1024]{1,0:T(8,128)(2,1)} collective-permute-done((bf16[256,1024]{1,0:T(8,128)(2,1)S(1)}, bf16[256,1024]{1,0:T(8,128)(2,1)}, u32[]{:S(2)}, u32[]{:S(2)}) %collective-permute-start.1) | collective-permute-done | bytes 524320 | tf_op jit(solution)/shard_map/ppermute | solution.py:729
  57.5 22.0 %all-gather.9.cloned.1.call-done = bf16[128,4096]{1,0:T(8,128)(2,1)} async-done(((bf16[32,4096]{1,0:T(8,128)(2,1)}), bf16[128,4096]{1,0:T(8,128)(2,1)}) %all-gather.9.cloned.1.call-update) | async-done | bytes 1048592 | tf_op jit(solution)/shard_map/all_gather | solution.py:559
  83.7 20.8 %collective-permute-done.7.refs_6_ = bf16[4,32,4096]{2,1,0:T(8,128)(2,1)} collective-permute-done((bf16[4,32,4096]{2,1,0:T(8,128)(2,1)}, bf16[4,32,4096]{2,1,0:T(8,128)(2,1)}, u32[]{:S(2)}, u32[]{:S(2)}) %collective-permute-start.7) | collective-permute-done | bytes 1048608 | tf_op jit(solution)/shard_map/ppermute | solution.py:563
  112.7 7.9 %assemble.3 = (bf16[4,4,2,32,3072]{4,3,2,1,0:T(8,128)(2,1)}, bf16[4,4,2,32,1024]{4,3,2,1,0:T(8,128)(2,1)}) custom-call(s32[16]{0:T(128)S(1)} %pad_add_fusion.place_ref, bf16[4,32,4096]{2,1,0:T(8,128)(2,1)S(1)} %bitcast.219, bf16[4,32,4096]{2,1,0:T(8,128)(2,1)} %collective-permute-done.2.refs_1_, bf16[4,32,4096]{2,1,0:T(8,128)(2,1)} %collective-permute-done.3.refs_2_, ...), custom_call_target="tpu_custom_call" | custom-call | bytes 524288 | tf_op jit(solution)/shard_map/assemble/pallas_call | solution.py:589
  120.6 8.0 %add_convert_fusion.q_ref.k_ref.v_ref = bf16[512,3072]{1,0:T(8,128)(2,1)} fusion(bf16[1024,3072]{1,0:T(8,128)(2,1)} %bitcast.269, f32[3072]{0:T(1024)S(1)} %bitcast.261, bf16[512,1024]{1,0:T(8,128)(2,1)S(1)} %copy-done.10, f32[1024]{0:T(1024)S(1)} %bitcast.264, f32[1024]{0:T(1024)S(1)} %bitcast.246, f32[512]{0:T(512)S(1)} %add_rsqrt_fusion.1, ...), kind=kOutput, calls=%fused_computation.19 | convolution fusion | flops 3227516928 | bytes 10510336 | tf_op jit(solution)/shard_map/dot_general | solution.py:805
  140.6 12.9 %attend.1 = (bf16[512,1024]{1,0:T(8,128)(2,1)S(1)}, f32[8,2,512]{2,1,0:T(2,128)S(1)}) custom-call(bf16[512,3072]{1,0:T(8,128)(2,1)S(1)} %copy-done.1, bf16[512,3072]{1,0:T(8,128)(2,1)S(1)} %copy-done.1, bf16[512,3072]{1,0:T(8,128)(2,1)S(1)} %copy-done.1), custom_call_target="tpu_custom_call" | custom-call | flops 2097152 | bytes 1572864 | tf_op jit(solution)/shard_map/attend/pallas_call | solution.py:489
  153.7 7.4 %collective-permute-done.14.refs_6_ = bf16[4,32,4096]{2,1,0:T(8,128)(2,1)} collective-permute-done((bf16[4,32,4096]{2,1,0:T(8,128)(2,1)}, bf16[4,32,4096]{2,1,0:T(8,128)(2,1)}, u32[]{:S(2)}, u32[]{:S(2)}) %collective-permute-start.14) | collective-permute-done | bytes 1048608 | tf_op jit(solution)/shard_map/ppermute | solution.py:567
  166.4 8.0 %assemble.4 = bf16[4,4,2,32,4096]{4,3,2,1,0:T(8,128)(2,1)} custom-call(s32[16]{0:T(128)S(1)} %pad_add_fusion.place_ref, bf16[4,32,4096]{2,1,0:T(8,128)(2,1)S(1)} %bitcast.223, bf16[4,32,4096]{2,1,0:T(8,128)(2,1)} %collective-permute-done.11.refs_1_, bf16[4,32,4096]{2,1,0:T(8,128)(2,1)} %collective-permute-done.10.refs_2_, ...), custom_call_target="tpu_custom_call" | custom-call | bytes 524288 | tf_op jit(solution)/shard_map/assemble/pallas_call | solution.py:589
  174.4 7.4 %collective-permute-done.17.refs_2_ = bf16[4,128,1024]{2,1,0:T(8,128)(2,1)S(1)} collective-permute-done((bf16[4,128,1024]{2,1,0:T(8,128)(2,1)}, bf16[4,128,1024]{2,1,0:T(8,128)(2,1)S(1)}, u32[]{:S(2)}, u32[]{:S(2)}) %collective-permute-start.17) | collective-permute-done | bytes 1048608 | tf_op jit(solution)/shard_map/ppermute | solution.py:567
  183.3 10.5 %fusion.69 = f32[512,4096]{1,0:T(8,128)} fusion(bf16[1024,4096]{1,0:T(8,128)(2,1)} %bitcast.224, f32[512,1024]{1,0:T(8,128)S(1)} %get-tuple-element.171, f32[1024]{0:T(1024)S(1)} %bitcast.266, f32[1024]{0:T(1024)S(1)} %bitcast.257, f32[512]{0:T(512)S(1)} %add_rsqrt_fusion, f32[512]{0:T(512)S(1)} %broadcast_multiply_fusion.4), kind=kOutput, calls=%fused_computation.212 | convolution fusion | flops 4297588736 | bytes 18886656 | tf_op jit(solution)/shard_map/dot_general | solution.py:824
  193.8 9.8 %convolution_convert_fusion.1 = bf16[4096,1024]{1,0:T(8,128)(2,1)S(1)} fusion(bf16[512,1024]{1,0:T(8,128)(2,1)S(1)} %fusion.23, f32[512,4096]{1,0:T(8,128)} %fusion.69, f32[4096]{0:T(1024)S(1)} %bitcast.254), kind=kOutput, calls=%fused_computation.17 | convolution fusion | flops 4320133120 | bytes 17842176 | tf_op jit(solution)/shard_map/dot_general | solution.py:46
  210.3 11.0 %collective-permute-done.19 = bf16[4,2,256,1024]{3,2,0,1:T(8,128)(2,1)} collective-permute-done((bf16[4,2,256,1024]{3,2,0,1:T(8,128)(2,1)}, bf16[4,2,256,1024]{3,2,0,1:T(8,128)(2,1)}, u32[]{:S(2)}, u32[]{:S(2)}) %collective-permute-start.19) | collective-permute-done | bytes 4194336 | tf_op jit(solution)/shard_map/ppermute | solution.py:563
  221.2 7.4 %convert_add_fusion.2 = (f32[4,256,1024]{2,1,0:T(8,128)}, bf16[4,256,1024]{2,1,0:T(8,128)(2,1)S(1)}) fusion(bf16[4,2,256,1024]{3,2,0,1:T(8,128)(2,1)} %collective-permute-done.19, s32[]{:T(128)S(6)} %select_n.250, bf16[4,2,2,256,1024]{4,3,2,1,0:T(8,128)(2,1)} %bitcast.233, s32[]{:T(128)S(6)} %select_n.251, s32[]{:T(128)S(6)} %select_n.248, ...), kind=kLoop, calls=%fused_computation.28 | loop fusion | flops 7340032 | bytes 14680084 | tf_op jit(solution)/shard_map/add | solution.py:665
  231.3 7.1 %assemble.5 = bf16[4,4,2,128,1024]{4,3,2,1,0:T(8,128)(2,1)} custom-call(s32[16]{0:T(128)S(1)} %pad_add_fusion.place_ref, bf16[4,128,1024]{2,1,0:T(8,128)(2,1)S(1)} %bitcast.215, bf16[4,128,1024]{2,1,0:T(8,128)(2,1)S(1)} %collective-permute-done.20.refs_1_, bf16[4,128,1024]{2,1,0:T(8,128)(2,1)S(1)} %collective-permute-done.17.refs_2_, ...), custom_call_target="tpu_custom_call" | custom-call | bytes 524288 | tf_op jit(solution)/shard_map/assemble/pallas_call | solution.py:589
  238.5 14.7 %fusion.3 = bf16[512,4096]{1,0:T(8,128)(2,1)S(1)} fusion(f32[512,4096]{1,0:T(8,128)} %fusion.69, f32[4096]{0:T(1024)S(1)} %bitcast.255, bf16[512,1024]{1,0:T(8,128)(2,1)S(1)} %copy-done.28, bf16[4096,1024]{1,0:T(8,128)(2,1)} %bitcast.226), kind=kOutput, calls=%fused_computation.7 | convolution fusion | flops 4347396096 | bytes 22036480 | tf_op jit(solution)/shard_map/dot_general | solution.py:52
  263.0 13.7 %collective-permute-done.24 = bf16[4,256,1024]{2,1,0:T(8,128)(2,1)S(1)} collective-permute-done((bf16[4,256,1024]{2,1,0:T(8,128)(2,1)S(1)}, bf16[4,256,1024]{2,1,0:T(8,128)(2,1)S(1)}, u32[]{:S(2)}, u32[]{:S(2)}) %collective-permute-start.24) | collective-permute-done | bytes 2097184 | tf_op jit(solution)/shard_map/ppermute | solution.py:563
  283.0 7.3 %fusion.74 = f32[512,1024]{1,0:T(8,128)S(1)} fusion(bf16[512,4096]{1,0:T(8,128)(2,1)S(1)} %copy-done.26, bf16[1024,4096]{1,0:T(8,128)(2,1)} %bitcast.225), kind=kOutput, calls=%fused_computation.217 | convolution fusion | flops 4294967296 | bytes 14680064 | tf_op jit(solution)/shard_map/dot_general | solution.py:52
  290.3 6.3 %convert_add_fusion = (f32[4,64,4096]{2,1,0:T(8,128)S(1)}, bf16[4,64,4096]{2,1,0:T(8,128)(2,1)}) fusion(bf16[4,2,64,4096]{3,2,0,1:T(8,128)(2,1)} %collective-permute-done.25, s32[]{:T(128)S(6)} %select_n.250, bf16[4,2,2,64,4096]{4,3,2,1,0:T(8,128)(2,1)} %bitcast.231, s32[]{:T(128)S(6)} %select_n.251, s32[]{:T(128)S(6)} %select_n.248, s32[]{:T(128)S(6)} %select_n.245, ...), kind=kLoop, calls=%fused_computation.25 | loop fusion | flops 7340032 | bytes 14680084 | tf_op jit(solution)/shard_map/add | solution.py:665
  298.3 9.8 %fusion.24 = (bf16[1024]{0:T(1024)(128)(2,1)S(1)}, bf16[512,1024]{1,0:T(8,128)(2,1)}, bf16[1024]{0:T(1024)(128)(2,1)S(1)}, f32[512,1024]{1,0:T(8,128)S(1)}) fusion(bf16[512,1024]{1,0:T(8,128)(2,1)S(1)} %copy-done.31, f32[1024]{0:T(1024)S(1)} %add.469, f32[512,1024]{1,0:T(8,128)S(1)} %copy-done.18, f32[1024]{0:T(1024)S(1)} %bitcast.253, ...), kind=kOutput, calls=%fused_computation.59 | convolution fusion | flops 4325373952 | bytes 27308032 | tf_op jit(solution)/shard_map/dot_general | solution.py:841
  319.3 17.2 %attend_back.1 = (bf16[512,1024]{1,0:T(8,128)(2,1)S(1)}, bf16[512,1024]{1,0:T(8,128)(2,1)S(1)}, bf16[512,1024]{1,0:T(8,128)(2,1)S(1)}) custom-call(bf16[512,3072]{1,0:T(8,128)(2,1)} %add_convert_fusion.q_ref.k_ref.v_ref, bf16[512,3072]{1,0:T(8,128)(2,1)} %add_convert_fusion.q_ref.k_ref.v_ref, bf16[512,3072]{1,0:T(8,128)(2,1)} %add_convert_fusion.q_ref.k_ref.v_ref, ...), custom_call_target="tpu_custom_call" | custom-call | flops 2097152 | bytes 1572864 | tf_op jit(solution)/shard_map/attend_back/pallas_call | solution.py:517
  336.9 13.6 %collective-permute-done.29 = bf16[256,1024]{1,0:T(8,128)(2,1)S(1)} collective-permute-done((bf16[256,1024]{1,0:T(8,128)(2,1)S(1)}, bf16[256,1024]{1,0:T(8,128)(2,1)S(1)}, u32[]{:S(2)}, u32[]{:S(2)}) %collective-permute-start.29) | collective-permute-done | bytes 524320 | tf_op jit(solution)/shard_map/ppermute | solution.py:684
  354.8 11.5 %collective-permute-start.31 = (bf16[64,4096]{1,0:T(8,128)(2,1)S(1)}, bf16[64,4096]{1,0:T(8,128)(2,1)S(1)}, u32[]{:S(2)}, u32[]{:S(2)}) collective-permute-start(bf16[64,4096]{1,0:T(8,128)(2,1)S(1)} %get-tuple-element.125), channel_id=1, source_target_pairs={{0,4},{1,5},{2,6},{3,7},{4,8},{5,9},{6,10},{7,11},{8,12},{9,13},{1... | collective-permute-start | bytes 1572872 | tf_op jit(solution)/shard_map/ppermute | solution.py:684
  403.2 5.6 %collective-permute-done.33 = bf16[64,4096]{1,0:T(8,128)(2,1)S(1)} collective-permute-done((bf16[64,4096]{1,0:T(8,128)(2,1)}, bf16[64,4096]{1,0:T(8,128)(2,1)S(1)}, u32[]{:S(2)}, u32[]{:S(2)}) %collective-permute-start.33) | collective-permute-done | bytes 524320 | tf_op jit(solution)/shard_map/ppermute | solution.py:684
  413.0 10.1 %collective-permute-done.51 = bf16[256,1024]{1,0:T(8,128)(2,1)S(1)} collective-permute-done((bf16[256,1024]{1,0:T(8,128)(2,1)S(1)}, bf16[256,1024]{1,0:T(8,128)(2,1)S(1)}, u32[]{:S(2)}, u32[]{:S(2)}) %collective-permute-start.51) | collective-permute-done | bytes 524320 | tf_op jit(solution)/shard_map/ppermute | solution.py:695
  424.3 10.7 %collective-permute-done.36 = bf16[4,32,4096]{2,1,0:T(8,128)(2,1)S(1)} collective-permute-done((bf16[4,32,4096]{2,1,0:T(8,128)(2,1)S(1)}, bf16[4,32,4096]{2,1,0:T(8,128)(2,1)S(1)}, u32[]{:S(2)}, u32[]{:S(2)}) %collective-permute-start.36) | collective-permute-done | bytes 1048608 | tf_op jit(solution)/shard_map/ppermute | solution.py:563
  441.8 14.8 %all-to-all-start.1 = ((f32[16,1,512]{2,1,0:T(1,128)}), f32[16,1,512]{2,1,0:T(1,128)S(1)}, u32[]{:S(2)}, u32[]{:S(2)}) async-start(f32[16,1,512]{2,1,0:T(1,128)} %all_to_all.17), calls=%async_computation.1 | async-start | bytes 65536 | tf_op jit(solution)/shard_map/all_to_all | solution.py:925
  492.4 7.9 %collective-permute-done.45 = bf16[64,4096]{1,0:T(8,128)(2,1)} collective-permute-done((bf16[64,4096]{1,0:T(8,128)(2,1)}, bf16[64,4096]{1,0:T(8,128)(2,1)}, u32[]{:S(2)}, u32[]{:S(2)}) %collective-permute-start.45) | collective-permute-done | bytes 524320 | tf_op jit(solution)/shard_map/ppermute | solution.py:684
  500.3 8.5 %collective-permute-done.47 = bf16[64,4096]{1,0:T(8,128)(2,1)} collective-permute-done((bf16[64,4096]{1,0:T(8,128)(2,1)}, bf16[64,4096]{1,0:T(8,128)(2,1)}, u32[]{:S(2)}, u32[]{:S(2)}) %collective-permute-start.47) | collective-permute-done | bytes 524320 | tf_op jit(solution)/shard_map/ppermute | solution.py:684
  508.8 22.1 %collective-permute-done.46 = bf16[64,4096]{1,0:T(8,128)(2,1)} collective-permute-done((bf16[64,4096]{1,0:T(8,128)(2,1)}, bf16[64,4096]{1,0:T(8,128)(2,1)}, u32[]{:S(2)}, u32[]{:S(2)}) %collective-permute-start.46) | collective-permute-done | bytes 524320 | tf_op jit(solution)/shard_map/ppermute | solution.py:684
  535.3 10.6 %collective-permute-done.48 = bf16[64,4096]{1,0:T(8,128)(2,1)S(1)} collective-permute-done((bf16[64,4096]{1,0:T(8,128)(2,1)S(1)}, bf16[64,4096]{1,0:T(8,128)(2,1)S(1)}, u32[]{:S(2)}, u32[]{:S(2)}) %collective-permute-start.48) | collective-permute-done | bytes 524320 | tf_op jit(solution)/shard_map/ppermute | solution.py:695
  (353 shorter events, 187.6 us)
Async XLA Ops:
  7.2 47.1 %all-gather.7.cloned.1.call-start = ((), (), s32[]{:S(2)}) async-start(), calls=%async_computation.2 | async-start | bytes 1310720 | tf_op jit(solution)/shard_map/all_gather | solution.py:559
  18.1 36.2 %all-to-all-start = ((f32[16,1,6656]{2,1,0:T(1,128)}), f32[16,1,6656]{2,1,0:T(1,128)S(1)}, u32[]{:S(2)}, u32[]{:S(2)}) async-start(f32[16,1,6656]{2,1,0:T(1,128)} %copy.65), calls=%async_computation | async-start | bytes 851968 | tf_op jit(solution)/shard_map/all_to_all | solution.py:764
  25.4 54.1 %all-gather.9.cloned.1.call-start = ((), (), s32[]{:S(2)}) async-start(), calls=%async_computation.3 | async-start | bytes 1310720 | tf_op jit(solution)/shard_map/all_gather | solution.py:559
  31.4 97.2 %all-gather.11.cloned.1.call-start = ((), (), s32[]{:S(2)}) async-start(), calls=%async_computation.4 | async-start | bytes 1310720 | tf_op jit(solution)/shard_map/all_gather | solution.py:559
  54.3 25.2 %collective-permute-start.3 = (bf16[4,32,4096]{2,1,0:T(8,128)(2,1)}, bf16[4,32,4096]{2,1,0:T(8,128)(2,1)}, u32[]{:S(2)}, u32[]{:S(2)}) collective-permute-start(bf16[4,32,4096]{2,1,0:T(8,128)(2,1)} %bitcast.216), channel_id=1, source_target_pairs={{0,16},{16,0},{1,17},{17,1},{2,18},{18,2},{3,19},{19,3},{4,20},{20... | collective-permute-start | bytes 3145736 | tf_op jit(solution)/shard_map/ppermute | solution.py:567
  55.9 27.8 %collective-permute-start.5 = (bf16[4,32,4096]{2,1,0:T(8,128)(2,1)}, bf16[4,32,4096]{2,1,0:T(8,128)(2,1)}, u32[]{:S(2)}, u32[]{:S(2)}) collective-permute-start(bf16[4,32,4096]{2,1,0:T(8,128)(2,1)} %bitcast.217), channel_id=1, source_target_pairs={{0,2},{1,3},{2,0},{3,1},{4,6},{5,7},{6,4},{7,5},{8,10},{9,11},{10,... | collective-permute-start | bytes 3145736 | tf_op jit(solution)/shard_map/ppermute | solution.py:563
  79.5 25.1 %collective-permute-start.7 = (bf16[4,32,4096]{2,1,0:T(8,128)(2,1)}, bf16[4,32,4096]{2,1,0:T(8,128)(2,1)}, u32[]{:S(2)}, u32[]{:S(2)}) collective-permute-start(bf16[4,32,4096]{2,1,0:T(8,128)(2,1)} %collective-permute-done.3.refs_2_), channel_id=1, source_target_pairs={{0,2},{1,3},{2,0},{3,1},{4,6},{5,7},{6,4},{7,5},{8,10},{9,11},{10,... | collective-permute-start | bytes 3145736 | tf_op jit(solution)/shard_map/ppermute | solution.py:563
  81.1 28.2 %collective-permute-start.2 = (bf16[4,32,4096]{2,1,0:T(8,128)(2,1)}, bf16[4,32,4096]{2,1,0:T(8,128)(2,1)}, u32[]{:S(2)}, u32[]{:S(2)}) collective-permute-start(bf16[4,32,4096]{2,1,0:T(8,128)(2,1)} %bitcast.218), channel_id=1, source_target_pairs={{0,1},{1,0},{2,3},{3,2},{4,5},{5,4},{6,7},{7,6},{8,9},{9,8},{10,11... | collective-permute-start | bytes 3145736 | tf_op jit(solution)/shard_map/ppermute | solution.py:563
  83.1 27.8 %collective-permute-start.4 = (bf16[4,32,4096]{2,1,0:T(8,128)(2,1)}, bf16[4,32,4096]{2,1,0:T(8,128)(2,1)S(1)}, u32[]{:S(2)}, u32[]{:S(2)}) collective-permute-start(bf16[4,32,4096]{2,1,0:T(8,128)(2,1)} %collective-permute-done.3.refs_2_), channel_id=1, source_target_pairs={{0,1},{1,0},{2,3},{3,2},{4,5},{5,4},{6,7},{7,6},{8,9},{9,8},{10,11... | collective-permute-start | bytes 3145736 | tf_op jit(solution)/shard_map/ppermute | solution.py:563
  83.7 27.1 %collective-permute-start.6 = (bf16[4,32,4096]{2,1,0:T(8,128)(2,1)}, bf16[4,32,4096]{2,1,0:T(8,128)(2,1)S(1)}, u32[]{:S(2)}, u32[]{:S(2)}) collective-permute-start(bf16[4,32,4096]{2,1,0:T(8,128)(2,1)} %collective-permute-done.5.refs_4_), channel_id=1, source_target_pairs={{0,1},{1,0},{2,3},{3,2},{4,5},{5,4},{6,7},{7,6},{8,9},{9,8},{10,11... | collective-permute-start | bytes 3145736 | tf_op jit(solution)/shard_map/ppermute | solution.py:563
  107.7 25.7 %collective-permute-start.10 = (bf16[4,32,4096]{2,1,0:T(8,128)(2,1)S(1)}, bf16[4,32,4096]{2,1,0:T(8,128)(2,1)}, u32[]{:S(2)}, u32[]{:S(2)}) collective-permute-start(bf16[4,32,4096]{2,1,0:T(8,128)(2,1)S(1)} %bitcast.220), channel_id=1, source_target_pairs={{0,16},{16,0},{1,17},{17,1},{2,18},{18,2},{3,19},{19,3},{4,20},{20... | collective-permute-start | bytes 3145736 | tf_op jit(solution)/shard_map/ppermute | solution.py:567
  109.3 25.4 %collective-permute-start.9 = (bf16[4,32,4096]{2,1,0:T(8,128)(2,1)S(1)}, bf16[4,32,4096]{2,1,0:T(8,128)(2,1)}, u32[]{:S(2)}, u32[]{:S(2)}) collective-permute-start(bf16[4,32,4096]{2,1,0:T(8,128)(2,1)S(1)} %bitcast.221), channel_id=1, source_target_pairs={{0,2},{1,3},{2,0},{3,1},{4,6},{5,7},{6,4},{7,5},{8,10},{9,11},{10,... | collective-permute-start | bytes 3145736 | tf_op jit(solution)/shard_map/ppermute | solution.py:563
  110.8 42.8 %collective-permute-start.11 = (bf16[4,32,4096]{2,1,0:T(8,128)(2,1)S(1)}, bf16[4,32,4096]{2,1,0:T(8,128)(2,1)}, u32[]{:S(2)}, u32[]{:S(2)}) collective-permute-start(bf16[4,32,4096]{2,1,0:T(8,128)(2,1)S(1)} %bitcast.222), channel_id=1, source_target_pairs={{0,1},{1,0},{2,3},{3,2},{4,5},{5,4},{6,7},{7,6},{8,9},{9,8},{10,11... | collective-permute-start | bytes 3145736 | tf_op jit(solution)/shard_map/ppermute | solution.py:563
  134.7 26.4 %collective-permute-start.14 = (bf16[4,32,4096]{2,1,0:T(8,128)(2,1)}, bf16[4,32,4096]{2,1,0:T(8,128)(2,1)}, u32[]{:S(2)}, u32[]{:S(2)}) collective-permute-start(bf16[4,32,4096]{2,1,0:T(8,128)(2,1)} %collective-permute-done.9.refs_4_), channel_id=1, source_target_pairs={{0,16},{16,0},{1,17},{17,1},{2,18},{18,2},{3,19},{19,3},{4,20},{20... | collective-permute-start | bytes 3145736 | tf_op jit(solution)/shard_map/ppermute | solution.py:567
  135.6 28.5 %collective-permute-start.13 = (bf16[4,32,4096]{2,1,0:T(8,128)(2,1)}, bf16[4,32,4096]{2,1,0:T(8,128)(2,1)S(1)}, u32[]{:S(2)}, u32[]{:S(2)}) collective-permute-start(bf16[4,32,4096]{2,1,0:T(8,128)(2,1)} %collective-permute-done.9.refs_4_), channel_id=1, source_target_pairs={{0,1},{1,0},{2,3},{3,2},{4,5},{5,4},{6,7},{7,6},{8,9},{9,8},{10,11... | collective-permute-start | bytes 3145736 | tf_op jit(solution)/shard_map/ppermute | solution.py:563
  135.7 46.1 %collective-permute-start.17 = (bf16[4,128,1024]{2,1,0:T(8,128)(2,1)}, bf16[4,128,1024]{2,1,0:T(8,128)(2,1)S(1)}, u32[]{:S(2)}, u32[]{:S(2)}) collective-permute-start(bf16[4,128,1024]{2,1,0:T(8,128)(2,1)} %bitcast.212), channel_id=1, source_target_pairs={{0,16},{16,0},{1,17},{17,1},{2,18},{18,2},{3,19},{19,3},{4,20},{20... | collective-permute-start | bytes 3145736 | tf_op jit(solution)/shard_map/ppermute | solution.py:567
  137.2 44.6 %collective-permute-start.16 = (bf16[4,128,1024]{2,1,0:T(8,128)(2,1)}, bf16[4,128,1024]{2,1,0:T(8,128)(2,1)S(1)}, u32[]{:S(2)}, u32[]{:S(2)}) collective-permute-start(bf16[4,128,1024]{2,1,0:T(8,128)(2,1)} %bitcast.213), channel_id=1, source_target_pairs={{0,2},{1,3},{2,0},{3,1},{4,6},{5,7},{6,4},{7,5},{8,10},{9,11},{10,... | collective-permute-start | bytes 3145736 | tf_op jit(solution)/shard_map/ppermute | solution.py:563
  181.8 26.4 %collective-permute-start.18 = (bf16[4,128,1024]{2,1,0:T(8,128)(2,1)S(1)}, bf16[4,128,1024]{2,1,0:T(8,128)(2,1)S(1)}, u32[]{:S(2)}, u32[]{:S(2)}) collective-permute-start(bf16[4,128,1024]{2,1,0:T(8,128)(2,1)S(1)} %collective-permute-done.17.refs_2_), channel_id=1, source_target_pairs={{0,2},{1,3},{2,0},{3,1},{4,6},{5,7},{6,4},{7,5},{8,10},{9,11},{10,... | collective-permute-start | bytes 3145736 | tf_op jit(solution)/shard_map/ppermute | solution.py:563
  228.8 47.9 %collective-permute-start.24 = (bf16[4,256,1024]{2,1,0:T(8,128)(2,1)S(1)}, bf16[4,256,1024]{2,1,0:T(8,128)(2,1)S(1)}, u32[]{:S(2)}, u32[]{:S(2)}) collective-permute-start(bf16[4,256,1024]{2,1,0:T(8,128)(2,1)S(1)} %get-tuple-element.106), channel_id=1, source_target_pairs={{0,2},{1,3},{2,0},{3,1},{4,6},{5,7},{6,4},{7,5},{8,10},{9,11},{10,... | collective-permute-start | bytes 6291464 | tf_op jit(solution)/shard_map/ppermute | solution.py:563
  297.7 52.8 %collective-permute-start.26 = (bf16[4,64,4096]{2,1,0:T(8,128)(2,1)}, bf16[4,64,4096]{2,1,0:T(8,128)(2,1)}, u32[]{:S(2)}, u32[]{:S(2)}) collective-permute-start(bf16[4,64,4096]{2,1,0:T(8,128)(2,1)} %get-tuple-element.110), channel_id=1, source_target_pairs={{0,2},{1,3},{2,0},{3,1},{4,6},{5,7},{6,4},{7,5},{8,10},{9,11},{10,... | collective-permute-start | bytes 6291464 | tf_op jit(solution)/shard_map/ppermute | solution.py:563
  311.8 25.1 %collective-permute-start.28 = (bf16[256,1024]{1,0:T(8,128)(2,1)}, bf16[256,1024]{1,0:T(8,128)(2,1)S(1)}, u32[]{:S(2)}, u32[]{:S(2)}) collective-permute-start(bf16[256,1024]{1,0:T(8,128)(2,1)} %get-tuple-element.119), channel_id=1, source_target_pairs={{0,4},{1,5},{2,6},{3,7},{4,8},{5,9},{6,10},{7,11},{8,12},{9,13},{1... | collective-permute-start | bytes 1572872 | tf_op jit(solution)/shard_map/ppermute | solution.py:684
  313.2 37.3 %collective-permute-start.29 = (bf16[256,1024]{1,0:T(8,128)(2,1)S(1)}, bf16[256,1024]{1,0:T(8,128)(2,1)S(1)}, u32[]{:S(2)}, u32[]{:S(2)}) collective-permute-start(bf16[256,1024]{1,0:T(8,128)(2,1)S(1)} %get-tuple-element.120), channel_id=1, source_target_pairs={{0,8},{1,9},{2,10},{3,11},{4,12},{5,13},{6,14},{7,15},{8,0},{9,1},... | collective-permute-start | bytes 1572872 | tf_op jit(solution)/shard_map/ppermute | solution.py:684
  314.6 35.9 %collective-permute-start.30 = (bf16[256,1024]{1,0:T(8,128)(2,1)S(1)}, bf16[256,1024]{1,0:T(8,128)(2,1)S(1)}, u32[]{:S(2)}, u32[]{:S(2)}) collective-permute-start(bf16[256,1024]{1,0:T(8,128)(2,1)S(1)} %get-tuple-element.121), channel_id=1, source_target_pairs={{0,12},{1,13},{2,14},{3,15},{4,0},{5,1},{6,2},{7,3},{8,4},{9,5},{1... | collective-permute-start | bytes 1572872 | tf_op jit(solution)/shard_map/ppermute | solution.py:684
  381.7 27.1 %collective-permute-start.33 = (bf16[64,4096]{1,0:T(8,128)(2,1)}, bf16[64,4096]{1,0:T(8,128)(2,1)S(1)}, u32[]{:S(2)}, u32[]{:S(2)}) collective-permute-start(bf16[64,4096]{1,0:T(8,128)(2,1)} %get-tuple-element.133), channel_id=1, source_target_pairs={{0,8},{1,9},{2,10},{3,11},{4,12},{5,13},{6,14},{7,15},{8,0},{9,1},... | collective-permute-start | bytes 1572872 | tf_op jit(solution)/shard_map/ppermute | solution.py:684
  382.8 27.5 %collective-permute-start.34 = (bf16[64,4096]{1,0:T(8,128)(2,1)S(1)}, bf16[64,4096]{1,0:T(8,128)(2,1)S(1)}, u32[]{:S(2)}, u32[]{:S(2)}) collective-permute-start(bf16[64,4096]{1,0:T(8,128)(2,1)S(1)} %get-tuple-element.134), channel_id=1, source_target_pairs={{0,12},{1,13},{2,14},{3,15},{4,0},{5,1},{6,2},{7,3},{8,4},{9,5},{1... | collective-permute-start | bytes 1572872 | tf_op jit(solution)/shard_map/ppermute | solution.py:684
  398.1 25.1 %collective-permute-start.51 = (bf16[256,1024]{1,0:T(8,128)(2,1)S(1)}, bf16[256,1024]{1,0:T(8,128)(2,1)S(1)}, u32[]{:S(2)}, u32[]{:S(2)}) collective-permute-start(bf16[256,1024]{1,0:T(8,128)(2,1)S(1)} %add_convert_fusion.3), channel_id=1, source_target_pairs={{0,16},{16,0},{1,17},{17,1},{2,18},{18,2},{3,19},{19,3},{4,20},{20... | collective-permute-start | bytes 1572872 | tf_op jit(solution)/shard_map/ppermute | solution.py:695
  401.4 59.3 %collective-permute-start.42 = (f32[256,1024]{1,0:T(8,128)}, f32[256,1024]{1,0:T(8,128)}, u32[]{:S(2)}, u32[]{:S(2)}) collective-permute-start(f32[256,1024]{1,0:T(8,128)} %slice.135), channel_id=1, source_target_pairs={{0,16},{16,0},{1,17},{17,1},{2,18},{18,2},{3,19},{19,3},{4,20},{20... | collective-permute-start | bytes 3145736 | tf_op jit(solution)/shard_map/ppermute | solution.py:732
  408.9 26.1 %collective-permute-start.36 = (bf16[4,32,4096]{2,1,0:T(8,128)(2,1)S(1)}, bf16[4,32,4096]{2,1,0:T(8,128)(2,1)S(1)}, u32[]{:S(2)}, u32[]{:S(2)}) collective-permute-start(bf16[4,32,4096]{2,1,0:T(8,128)(2,1)S(1)} %get-tuple-element.197), channel_id=1, source_target_pairs={{0,2},{1,3},{2,0},{3,1},{4,6},{5,7},{6,4},{7,5},{8,10},{9,11},{10,... | collective-permute-start | bytes 3145736 | tf_op jit(solution)/shard_map/ppermute | solution.py:563
  410.3 63.4 %collective-permute-start.35 = (bf16[4,32,4096]{2,1,0:T(8,128)(2,1)}, bf16[4,32,4096]{2,1,0:T(8,128)(2,1)}, u32[]{:S(2)}, u32[]{:S(2)}) collective-permute-start(bf16[4,32,4096]{2,1,0:T(8,128)(2,1)} %get-tuple-element.198), channel_id=1, source_target_pairs={{0,2},{1,3},{2,0},{3,1},{4,6},{5,7},{6,4},{7,5},{8,10},{9,11},{10,... | collective-permute-start | bytes 3145736 | tf_op jit(solution)/shard_map/ppermute | solution.py:563
  441.8 30.6 %all-to-all-start.1 = ((f32[16,1,512]{2,1,0:T(1,128)}), f32[16,1,512]{2,1,0:T(1,128)S(1)}, u32[]{:S(2)}, u32[]{:S(2)}) async-start(f32[16,1,512]{2,1,0:T(1,128)} %all_to_all.17), calls=%async_computation.1 | async-start | bytes 65536 | tf_op jit(solution)/shard_map/all_to_all | solution.py:925
  475.8 57.4 %collective-permute-start.50 = (bf16[64,4096]{1,0:T(8,128)(2,1)S(1)}, bf16[64,4096]{1,0:T(8,128)(2,1)}, u32[]{:S(2)}, u32[]{:S(2)}) collective-permute-start(bf16[64,4096]{1,0:T(8,128)(2,1)S(1)} %add_convert_fusion.4), channel_id=1, source_target_pairs={{0,16},{16,0},{1,17},{17,1},{2,18},{18,2},{3,19},{19,3},{4,20},{20... | collective-permute-start | bytes 1572872 | tf_op jit(solution)/shard_map/ppermute | solution.py:695
  487.1 43.8 %collective-permute-start.46 = (bf16[64,4096]{1,0:T(8,128)(2,1)}, bf16[64,4096]{1,0:T(8,128)(2,1)}, u32[]{:S(2)}, u32[]{:S(2)}) collective-permute-start(bf16[64,4096]{1,0:T(8,128)(2,1)} %get-tuple-element.180), channel_id=1, source_target_pairs={{0,8},{1,9},{2,10},{3,11},{4,12},{5,13},{6,14},{7,15},{8,0},{9,1},... | collective-permute-start | bytes 1572872 | tf_op jit(solution)/shard_map/ppermute | solution.py:684
  (92 other events, 1080.4 us)
Sparse Core Ops, SparseCore 0:
  10.2 40.3 all-gather.6
  52.7 26.7 all-gather.8
  83.2 27.7 all-gather.10
